TPU v7x, 256 devices: a whole 4x4x8 slice. The times are simulated.
256 devices in a mesh: dp: 8 (over y_hi, x), loop: 32 (over z, y_lo, core).
Axes of the slice: x: 4, y: 4 (y_hi: 2, y_lo: 2; y = y_hi * 2 + y_lo), z: 8, core: 2. Of those that a mesh axis runs over, the one named last changes fastest.
Arguments:
- tokens: bfloat16 [8, 16384, 1536], P('dp', 'loop'), may hold values from -6 to 6
- weights: bfloat16 [1536, 2304], replicated, may hold values from -2 to 2
- cotangent: bfloat16 [8, 16384, 768], P('dp', 'loop'), may hold values from -6 to 6
- token_types: int32 [8, 16384], P('dp'), may hold values from 0 to 1
- incidence: int32 [8, 256, 3], P('dp', 'loop'), may hold values 0 or 1
- window_reach: int32 [8, 256], P('dp', 'loop'), may hold values from 32 to 64, as said below
Outputs:
- attended: bfloat16 [8, 16384, 768], P('dp', 'loop')
- token_grad: bfloat16 [8, 16384, 1536], P('dp', 'loop')
- weight_grad: float32 [1536, 2304], P(('dp', 'loop'))
Inputs may be any that keep to these rules, and one draw needn't show every extreme that they name: `token_types`: 0 marks a vertex token, 1 a face token. `incidence`: entry r of a query block is 1 where that block's tokens touch the key block r - 1 blocks away along the curve. `window_reach`: equal to 64 in at least one block of every mesh.
All inputs are finite; a program needn't handle non-finite values.
Results may differ from a plain program's by a relative error of at most 0.02.
Values may be sent and summed in bfloat16 or wider, within the bound.
No kernel may reach another device: no remote copies, remote signals or barrier semaphores. Data moves between devices by JAX's collectives and lax.ppermute only.
A program may use at most 128 MiB of HBM per device.

v0:
```python
import functools

import jax
import jax.numpy as jnp
from jax import lax
from jax.experimental import pallas as pl
from jax.experimental.pallas import tpu as pltpu
from jax.sharding import PartitionSpec as P

HEADS = 12
HD = 64
TILE = 64
CAP = 20
HW = 768
HALO = 64
GROUPS = 3
GW = HW // GROUPS
GH = HEADS // GROUPS
ROWS = 512
EXT = ROWS + 2 * HALO
TILES = ROWS // TILE
WIN = 3 * TILE
D = 1536
HALF = D // 2
AXES = ("dp", "loop")
MIB = 1024 * 1024
F32 = jnp.float32
BF16 = jnp.bfloat16

NT = (((1,), (1,)), ((), ()))
TN = (((0,), (0,)), ((), ()))
NN = (((1,), (0,)), ((), ()))


def dot(a, b, dims):
    return lax.dot_general(a, b, dims, preferred_element_type=F32)


def device_at(x, y, z, core):
    return (((y // 2 * 4 + x) * 8 + z) * 2 + y % 2) * 2 + core


def route(move):
    pairs = []
    for x in range(4):
        for y in range(4):
            for z in range(8):
                for core in range(2):
                    pairs.append((device_at(x, y, z, core), device_at(*move(x, y, z, core))))
    return pairs


TO_CORE = route(lambda x, y, z, c: (x, y, z, 1 - c))
ACROSS_X = [route(lambda x, y, z, c, m=m: (x ^ m, y, z, c)) for m in (1, 2, 3)]
ACROSS_Y = [route(lambda x, y, z, c, m=m: (x, y ^ m, z, c)) for m in (1, 2, 3)]
ACROSS_Z = [route(lambda x, y, z, c, m=m: (x, y, z ^ m, c)) for m in (1, 2, 4)]


def along_loop(distance):
    return [((i - distance) % 32, i) for i in range(32)]


def call(kernel, out_shape, *args, vmem=16, **kwargs):
    return pl.pallas_call(
        kernel,
        out_shape=out_shape,
        compiler_params=pltpu.CompilerParams(vmem_limit_bytes=vmem * MIB),
        **kwargs,
    )(*args)


def whole():
    return pl.BlockSpec(memory_space=pltpu.VMEM)


def scalars():
    return pl.BlockSpec(memory_space=pltpu.SMEM)


def anywhere():
    return pl.BlockSpec(memory_space=pl.ANY)


def shape(rows, cols, dtype):
    return jax.ShapeDtypeStruct((rows, cols), dtype)


def cost(flops, size, transcendentals=0):
    return pl.CostEstimate(flops=flops, bytes_accessed=size, transcendentals=transcendentals)


def mask_kernel(incidence_ref, reach_ref, types_ref, out_ref):
    row = types_ref[...].astype(F32)
    column = jnp.broadcast_to(row, (2 * TILE, EXT)).T
    key = lax.broadcasted_iota(jnp.int32, (WIN, 2 * TILE), 0)
    query = lax.broadcasted_iota(jnp.int32, (WIN, 2 * TILE), 1) % TILE
    distance = jnp.abs(key - HALO - query)
    for t in range(TILES):
        own = row[:, HALO + t * TILE : HALO + (t + 1) * TILE]
        other_kind = column[t * TILE : t * TILE + WIN] != jnp.concatenate([own, own], axis=1)
        linked = [jnp.full((TILE, 2 * TILE), incidence_ref[t, r], jnp.int32) for r in range(3)]
        linked = jnp.concatenate(linked, axis=0) == 1
        allowed = (distance == 0) | ((distance <= reach_ref[t]) & other_kind & linked)
        out_ref[t * WIN : (t + 1) * WIN, :] = jnp.where(allowed, 1.0, 0.0)


def make_mask(types, row_start, incidence, reach):
    seq_len = types.shape[1]
    padded = jnp.concatenate([types[:, seq_len - HALO :], types, types[:, :HALO]], axis=1)
    near = lax.dynamic_slice_in_dim(padded, row_start, EXT, 1)
    return call(
        mask_kernel,
        shape(TILES * WIN, 2 * TILE, F32),
        incidence,
        reach,
        near,
        in_specs=[scalars(), scalars(), whole()],
        out_specs=whole(),
    )


def projection_kernel(own_ref, left_ref, right_ref, w_ref, out_ref, rows):
    @pl.when(pl.program_id(0) == 0)
    def _():
        rows[:ROWS] = own_ref[...]
        rows[ROWS : ROWS + HALO] = left_ref[...]
        rows[ROWS + HALO :] = right_ref[...]

    out_ref[...] = dot(rows[...], w_ref[...], NN).astype(BF16)


def projection(own, left, right, weights):
    cols = weights.shape[1]
    return call(
        projection_kernel,
        shape(EXT, cols, BF16),
        own,
        left,
        right,
        weights,
        vmem=24,
        grid=(cols // GW,),
        in_specs=[
            pl.BlockSpec((ROWS, D), lambda i: (0, 0)),
            pl.BlockSpec((HALO, D), lambda i: (0, 0)),
            pl.BlockSpec((HALO, D), lambda i: (0, 0)),
            pl.BlockSpec((D, GW), lambda i: (0, i)),
        ],
        out_specs=pl.BlockSpec((EXT, GW), lambda i: (0, i)),
        scratch_shapes=[pltpu.VMEM((EXT, D), BF16)],
        cost_estimate=cost(2 * EXT * D * cols, 12_000_000),
    )


def reorder_kernel(place_ref, own_ref, left_ref, right_ref, same_ref, other_ref, rows):
    x, y, z, core = place_ref[0], place_ref[1], place_ref[2], place_ref[3]
    rows[:ROWS] = own_ref[...]
    rows[ROWS : ROWS + HALO] = left_ref[...]
    rows[ROWS + HALO :] = right_ref[...]
    block = D // 4
    half = block // 2
    place = lax.broadcasted_iota(jnp.int32, (block, block), 0)
    feature = lax.broadcasted_iota(jnp.int32, (block, block), 1)
    other = (place >= half).astype(jnp.int32)
    place = place - other * half
    low_y = (place >= half // 2).astype(jnp.int32)
    place = place - low_y * (half // 2)
    low_x = (place >= half // 4).astype(jnp.int32)
    place = place - low_x * (half // 4)
    spot = lax.shift_right_logical(place * 10923, 16)
    place = place - spot * 6
    to_z = z ^ (lax.shift_right_logical(spot, 2) + (spot & 2) + (spot & 1) * 4)
    source = (low_x ^ (x & 1)) * half + to_z * 24 + (low_y ^ (y & 1)) * 12 + (other ^ core) * 6 + place
    pick = jnp.where(feature == source, 1.0, 0.0).astype(BF16)
    piece = half // 4
    for a in range(2):
        for b in range(2):
            at = (lax.shift_right_logical(y, 1) ^ a) * 2 + (lax.shift_right_logical(x, 1) ^ b)
            cols = rows[:, pl.ds(pl.multiple_of(at * block, 128), block)]
            got = dot(pick, cols, NT).astype(BF16)
            for c, ref in enumerate((same_ref, other_ref)):
                for low in range(4):
                    jy, jx = 2 * a + low // 2, 2 * b + low % 2
                    ref[jy * half + jx * piece : jy * half + (jx + 1) * piece] = got[
                        c * half + low * piece : c * half + (low + 1) * piece
                    ]


def reorder(place, own, left, right, after):
    def kernel(place_ref, own_ref, left_ref, right_ref, _, *refs):
        reorder_kernel(place_ref, own_ref, left_ref, right_ref, *refs)

    return call(
        kernel,
        (shape(HALF, EXT, BF16),) * 2,
        place,
        own,
        left,
        right,
        after,
        in_specs=[scalars(), whole(), whole(), whole(), anywhere()],
        out_specs=(whole(),) * 2,
        scratch_shapes=[pltpu.VMEM((EXT, D), BF16)],
        cost_estimate=cost(8 * EXT * (D // 4) ** 2, 4_000_000),
    )


def attention_kernel(n_carried, q_ref, k_ref, v_ref, go_ref, mask_ref, *refs):
    att_ref, left_ref, right_ref, grad_ref, ke, ve, dk, dv = refs[n_carried:]
    for src, dst in ((k_ref, ke), (v_ref, ve)):
        dst[:HALO] = src[ROWS : ROWS + HALO]
        dst[HALO : HALO + ROWS] = src[:ROWS]
        dst[HALO + ROWS :] = src[ROWS + HALO :]
    dk[...] = jnp.zeros_like(dk)
    dv[...] = jnp.zeros_like(dv)
    head_of_lane = lax.broadcasted_iota(jnp.int32, (TILE, GW), 1) // HD

    def spread(rows):
        zero = jnp.zeros_like(rows)
        return jnp.concatenate([jnp.where(head_of_lane == h, rows, zero) for h in range(GH)], axis=0)

    def gather(square):
        out = square[:TILE]
        for h in range(1, GH):
            out = jnp.where(head_of_lane == h, square[h * TILE : (h + 1) * TILE], out)
        return out

    def step(t, _):
        at = pl.multiple_of(t * TILE, TILE)
        rows = pl.ds(at, TILE)
        window = pl.ds(at, WIN)
        q_bd = spread(q_ref[rows, :])
        g_bd = spread(go_ref[rows, :])
        k_win = ke[window, :]
        v_win = ve[window, :]
        mask = mask_ref[pl.ds(pl.multiple_of(t * WIN, WIN), WIN), :]
        mask = jnp.concatenate([mask] * (GH // 2), axis=1)
        bent = jnp.tanh(dot(k_win, q_bd, NT) * (HD**-0.5 / CAP))
        numer = jnp.exp(bent * CAP) * mask
        probs = numer * (1.0 / jnp.sum(numer, axis=0, keepdims=True))
        low = probs.astype(BF16)
        weighted = probs * dot(v_win, g_bd, NT)
        delta = jnp.sum(weighted, axis=0, keepdims=True)
        scores = ((weighted - probs * delta) * (1.0 - bent * bent)).astype(BF16)
        dk[window, :] += dot(scores, q_bd, NN)
        dv[window, :] += dot(low, g_bd, NN)
        att_ref[rows, :] = gather(dot(low, v_win, TN)).astype(BF16)
        grad_ref[rows, :GW] = (gather(dot(scores, k_win, TN)) * HD**-0.5).astype(BF16)
        return 0

    lax.fori_loop(0, TILES, step, 0, unroll=4)
    grad_ref[ROWS:, :GW] = jnp.zeros((2 * HALO, GW), BF16)
    for part, acc, factor in ((1, dk, HD**-0.5), (2, dv, 1.0)):
        cols = slice(part * GW, (part + 1) * GW)
        rim_cols = slice((part - 1) * GW, part * GW)
        left = (acc[:HALO] * factor).astype(BF16)
        right = (acc[HALO + ROWS :] * factor).astype(BF16)
        grad_ref[:ROWS, cols] = (acc[HALO : HALO + ROWS] * factor).astype(BF16)
        grad_ref[ROWS : ROWS + HALO, cols] = left
        grad_ref[ROWS + HALO :, cols] = right
        left_ref[:, rim_cols] = left
        right_ref[:, rim_cols] = right


def attention(group, proj, grad_out, mask, carried, after):
    def cols(rows, block, width=GW):
        return pl.BlockSpec((rows, width), lambda i: (0, block))

    extra = list(carried) + list(after)
    return call(
        functools.partial(attention_kernel, len(extra)),
        (shape(ROWS, HW, BF16), shape(HALO, 2 * HW, BF16), shape(HALO, 2 * HW, BF16), shape(EXT, 3 * GW, BF16)),
        proj,
        proj,
        proj,
        grad_out,
        mask,
        *extra,
        vmem=20,
        grid=(1,),
        in_specs=[
            cols(ROWS, group),
            cols(EXT, GROUPS + group),
            cols(EXT, 2 * GROUPS + group),
            cols(ROWS, group),
            pl.BlockSpec((TILES * WIN, 2 * TILE), lambda i: (0, 0)),
        ]
        + [anywhere()] * len(extra),
        out_specs=(
            cols(ROWS, group),
            cols(HALO, group, 2 * GW),
            cols(HALO, group, 2 * GW),
            pl.BlockSpec((EXT, 3 * GW), lambda i: (0, 0)),
        ),
        scratch_shapes=[
            pltpu.VMEM((EXT, GW), BF16),
            pltpu.VMEM((EXT, GW), BF16),
            pltpu.VMEM((EXT, GW), F32),
            pltpu.VMEM((EXT, GW), F32),
        ],
        input_output_aliases={5 + i: i for i in range(len(carried))},
        cost_estimate=cost(36 * TILES * WIN * GW * GW, 4_000_000, 2 * TILES * WIN * GW),
    )


def weight_kernel(first, x_ref, xp_ref, g_ref, gp_ref, _, keep_ref, *send_refs):
    total = dot(x_ref[...], g_ref[...], NN) + dot(xp_ref[...], gp_ref[...], NN)
    part = HALF // 4
    piece = part // 4
    for j in range(4):
        for i in range(4):
            jy, jx = (j, i) if first == "y" else (i, j)
            rows = total[jy * part + jx * piece : jy * part + (jx + 1) * piece]
            at = slice(i * piece, (i + 1) * piece)
            if j == 0:
                keep_ref[at] = rows
            else:
                send_refs[j - 1][at] = rows.astype(BF16)


def weight_parts(first, x_own, x_other, g_own, g_other, after):
    part = HALF // 4
    resident = pl.BlockSpec((HALF, EXT), lambda i: (0, 0))
    moving = pl.BlockSpec((EXT, GW), lambda i: (0, i))
    return call(
        functools.partial(weight_kernel, first),
        (shape(part, 3 * GW, F32),) + (shape(part, 3 * GW, BF16),) * 3,
        x_own,
        x_other,
        g_own,
        g_other,
        after,
        grid=(3,),
        in_specs=[resident, resident, moving, moving, anywhere()],
        out_specs=(pl.BlockSpec((part, GW), lambda i: (0, i)),) * 4,
        cost_estimate=cost(4 * HALF * EXT * 3 * GW, 6_000_000),
    )


def split_kernel(keep_ref, a_ref, b_ref, c_ref, out_ref, *send_refs):
    part = out_ref.shape[0]
    for j in range(4):
        rows = slice(j * part, (j + 1) * part)
        total = keep_ref[rows] + a_ref[rows].astype(F32) + b_ref[rows].astype(F32) + c_ref[rows].astype(F32)
        if j == 0:
            out_ref[...] = total
        else:
            send_refs[j - 1][...] = total.astype(BF16)


def split_sum(keep, received):
    rows, cols = keep.shape[0] // 4, keep.shape[1]
    return call(
        split_kernel,
        (shape(rows, cols, F32),) + (shape(rows, cols, BF16),) * 3,
        keep,
        *received,
        in_specs=[whole()] * 4,
        out_specs=(whole(),) * 4,
    )


def join_kernel(*refs):
    keep_ref, send_ref = refs[-2:]
    half = keep_ref.shape[0]
    for g in range(GROUPS):
        total = refs[4 * g][...]
        for r in refs[4 * g + 1 : 4 * g + 4]:
            total = total + r[...].astype(F32)
        cols = slice(g * 3 * GW, (g + 1) * 3 * GW)
        keep_ref[:, cols] = total[:half]
        send_ref[:, cols] = total[half:].astype(BF16)


def halve_kernel(keep_ref, got_ref, out_ref, send_ref):
    half = out_ref.shape[0]
    total = keep_ref[...] + got_ref[...].astype(F32)
    out_ref[...] = total[:half]
    send_ref[...] = total[half:].astype(BF16)


def last_kernel(factor, keep_ref, got_ref, out_ref):
    total = (keep_ref[...] + got_ref[...].astype(F32)) * factor
    for g in range(GROUPS):
        for k in range(3):
            at = (g * 3 + k) * GW
            out_ref[:, k * HW + g * GW : k * HW + (g + 1) * GW] = total[:, at : at + GW]


def halves(kernel, rows, *args):
    cols = 3 * HW
    return call(
        kernel,
        (shape(rows, cols, F32), shape(rows, cols, BF16)),
        *args,
        in_specs=[whole()] * len(args),
        out_specs=(whole(),) * 2,
    )


def exchange(parts, routes):
    return [lax.ppermute(part, AXES, way) for part, way in zip(parts, routes)]


def token_kernel(a_ref, b_ref, c_ref, left_ref, right_ref, w_ref, out_ref, grad):
    @pl.when(pl.program_id(0) == 0)
    def _():
        for g, ref in enumerate((a_ref, b_ref, c_ref)):
            for k in range(3):
                cols = slice(k * HW + g * GW, k * HW + (g + 1) * GW)
                own = slice(k * GW, (k + 1) * GW)
                if k == 0:
                    grad[:, cols] = ref[:ROWS, own]
                    continue
                rim = slice((2 * g + k - 1) * GW, (2 * g + k) * GW)
                for edge, got in ((slice(0, HALO), left_ref), (slice(ROWS - HALO, ROWS), right_ref)):
                    grad[edge, cols] = (ref[edge, own].astype(F32) + got[:, rim].astype(F32)).astype(BF16)
                grad[HALO : ROWS - HALO, cols] = ref[HALO : ROWS - HALO, own]

    out_ref[...] = dot(grad[...], w_ref[...], NT).astype(BF16)


def token_gradient(grads, from_left, from_right, weights):
    block = 256
    cols = weights.shape[1]
    grad_spec = pl.BlockSpec((EXT, 3 * GW), lambda i: (0, 0))
    rim_spec = pl.BlockSpec((HALO, 2 * HW), lambda i: (0, 0))
    return call(
        token_kernel,
        shape(ROWS, D, BF16),
        *grads,
        from_left,
        from_right,
        weights,
        vmem=24,
        grid=(D // block,),
        in_specs=[grad_spec] * 3 + [rim_spec] * 2 + [pl.BlockSpec((block, cols), lambda i: (i, 0))],
        out_specs=pl.BlockSpec((ROWS, block), lambda i: (0, i)),
        scratch_shapes=[pltpu.VMEM((ROWS, cols), BF16)],
        cost_estimate=cost(2 * ROWS * D * cols, 12_000_000),
    )


def body(tokens, weights, cotangent, token_types, incidence, window_reach):
    own = tokens[0]
    dp, loop = lax.axis_index("dp"), lax.axis_index("loop")
    place = jnp.stack([dp % 4, dp // 4 * 2 + loop // 2 % 2, loop // 4, loop % 2]).astype(jnp.int32)
    left = lax.ppermute(own[ROWS - HALO :], "loop", along_loop(1))
    right = lax.ppermute(own[:HALO], "loop", along_loop(-1))
    mask = make_mask(token_types, loop * ROWS, incidence[0], window_reach[0])
    proj = projection(own, left, right, weights)

    first = ("y", "x", "y")
    carried, grads, others, waiting = (), [], [], []

    def attend(group, after):
        nonlocal carried
        *carried, grad = attention(group, proj, cotangent[0], mask, carried, after)
        grads.append(grad)
        others.append(lax.ppermute(grad, AXES, TO_CORE))

    def weigh(group, after):
        keep, *sent = weight_parts(first[group], x_own, x_other, grads[group], others[group], after)
        waiting.append((keep, exchange(sent, ACROSS_Y if first[group] == "y" else ACROSS_X)))
        return keep

    attend(0, ())
    x_own, x_send = reorder(place, own, left, right, grads[0])
    x_other = lax.ppermute(x_send, AXES, TO_CORE)
    attend(1, (x_own,))
    keep = weigh(0, grads[1])
    attend(2, (keep,))
    keep = weigh(1, grads[2])
    weigh(2, keep)
    attended, rim_left, rim_right = carried
    from_right = lax.ppermute(rim_left, "loop", along_loop(-1))
    from_left = lax.ppermute(rim_right, "loop", along_loop(1))

    parts = []
    for group in range(GROUPS):
        keep, *sent = split_sum(*waiting[group])
        parts += [keep, *exchange(sent, ACROSS_X if first[group] == "y" else ACROSS_Y)]
    keep, send = halves(join_kernel, 24, *parts)
    keep, send = halves(halve_kernel, 12, keep, lax.ppermute(send, AXES, ACROSS_Z[0]))
    keep, send = halves(halve_kernel, 6, keep, lax.ppermute(send, AXES, ACROSS_Z[1]))
    weight_grad = call(
        functools.partial(last_kernel, (256 * ROWS) ** -0.5),
        shape(6, 3 * HW, F32),
        keep,
        lax.ppermute(send, AXES, ACROSS_Z[2]),
        in_specs=[whole()] * 2,
        out_specs=whole(),
    )
    token_grad = token_gradient(grads, from_left, from_right, weights)
    return attended[None], token_grad[None], weight_grad


def solution(mesh):
    in_specs = (
        P("dp", "loop", None),
        P(),
        P("dp", "loop", None),
        P("dp", None),
        P("dp", "loop", None),
        P("dp", "loop"),
    )
    out_specs = (P("dp", "loop", None), P("dp", "loop", None), P(("dp", "loop"), None))
    return jax.shard_map(body, mesh=mesh, in_specs=in_specs, out_specs=out_specs, check_vma=False)
```

profile of v0, /device:TPU:8, one launch (start us, length us, event | category | flops | bytes accessed | tf_op | source)
XLA Modules:
  0.0 116.9 jit_solution(3493348326816081828)
XLA Ops:
  8.0 3.0 %copy-done.2 = bf16[1536,2304]{1,0:T(8,128)(2,1)S(1)} copy-done((bf16[1536,2304]{1,0:T(8,128)(2,1)S(1)}, bf16[1536,2304]{1,0:T(8,128)(2,1)}, u32[]{:S(2)}) %copy-start.2) | copy-done | bytes 7077912
  11.0 6.9 %shard_map.85.q_ref.k_ref.v_ref = bf16[640,2304]{1,0:T(8,128)(2,1)S(1)} custom-call(bf16[512,1536]{1,0:T(8,128)(2,1)S(1)} %bitcast.14, bf16[64,1536]{1,0:T(8,128)(2,1)S(1)} %collective-permute-done.left_ref, bf16[64,1536]{1,0:T(8,128)(2,1)S(1)} %collective-permute-done.1.right_ref, bf16[1536,2304]{1,0:T(8,128)(2,1)S(1)} %copy-done.2), custom_call_target="tpu_custom_call" | custom-call | flops 4529848320 | bytes 12000000 | tf_op jit(solution)/shard_map/pallas_call | solution.py:64
  17.9 4.3 %shard_map.87 = (bf16[512,768]{1,0:T(8,128)(2,1)}, bf16[64,1536]{1,0:T(8,128)(2,1)S(1)}, bf16[64,1536]{1,0:T(8,128)(2,1)S(1)}, bf16[640,768]{1,0:T(8,128)(2,1)S(1)}) custom-call(bf16[640,2304]{1,0:T(8,128)(2,1)S(1)} %shard_map.85.q_ref.k_ref.v_ref, bf16[640,2304]{1,0:T(8,128)(2,1)S(1)} %shard_map.85.q_ref.k_ref.v_ref, ...), custom_call_target="tpu_custom_call" | custom-call | flops 3623878656 | bytes 4000000 | tf_op jit(solution)/shard_map/pallas_call | solution.py:64
  26.3 4.3 %shard_map.89 = (bf16[512,768]{1,0:T(8,128)(2,1)}, bf16[64,1536]{1,0:T(8,128)(2,1)S(1)}, bf16[64,1536]{1,0:T(8,128)(2,1)S(1)}, bf16[640,768]{1,0:T(8,128)(2,1)S(1)}) custom-call(bf16[640,2304]{1,0:T(8,128)(2,1)S(1)} %shard_map.85.q_ref.k_ref.v_ref, ...), custom_call_target="tpu_custom_call", output_to_operand_aliasing={{0}: (5, {}), {1}: (6, {}), {2}: (7, {})} | custom-call | flops 3623878656 | bytes 4000000 | tf_op jit(solution)/shard_map/pallas_call | solution.py:64
  31.0 2.6 %shard_map.90 = (f32[192,768]{1,0:T(8,128)S(1)}, bf16[192,768]{1,0:T(8,128)(2,1)S(1)}, bf16[192,768]{1,0:T(8,128)(2,1)S(1)}, bf16[192,768]{1,0:T(8,128)(2,1)S(1)}) custom-call(bf16[768,640]{1,0:T(8,128)(2,1)S(1)} %get-tuple-element.51.refs_3_.x_ref, bf16[768,640]{1,0:T(8,128)(2,1)S(1)} %collective-permute-done.2.xp_ref, ...), custom_call_target="tpu_custom_call" | custom-call | flops 1509949440 | bytes 6000000 | tf_op jit(solution)/shard_map/pallas_call | solution.py:64
  33.6 4.3 %shard_map.91 = (bf16[512,768]{1,0:T(8,128)(2,1)}, bf16[64,1536]{1,0:T(8,128)(2,1)S(1)}, bf16[64,1536]{1,0:T(8,128)(2,1)S(1)}, bf16[640,768]{1,0:T(8,128)(2,1)S(1)}) custom-call(bf16[640,2304]{1,0:T(8,128)(2,1)S(1)} %shard_map.85.q_ref.k_ref.v_ref, ...), custom_call_target="tpu_custom_call", output_to_operand_aliasing={{0}: (5, {}), {1}: (6, {}), {2}: (7, {})} | custom-call | flops 3623878656 | bytes 4000000 | tf_op jit(solution)/shard_map/pallas_call | solution.py:64
  38.0 2.6 %shard_map.94 = (f32[192,768]{1,0:T(8,128)S(1)}, bf16[192,768]{1,0:T(8,128)(2,1)S(1)}, bf16[192,768]{1,0:T(8,128)(2,1)S(1)}, bf16[192,768]{1,0:T(8,128)(2,1)S(1)}) custom-call(bf16[768,640]{1,0:T(8,128)(2,1)S(1)} %get-tuple-element.51.refs_3_.x_ref, bf16[768,640]{1,0:T(8,128)(2,1)S(1)} %collective-permute-done.2.xp_ref, ...), custom_call_target="tpu_custom_call" | custom-call | flops 1509949440 | bytes 6000000 | tf_op jit(solution)/shard_map/pallas_call | solution.py:64
  42.1 2.7 %collective-permute-start.14 = (bf16[192,768]{1,0:T(8,128)(2,1)S(1)}, bf16[192,768]{1,0:T(8,128)(2,1)S(1)}, u32[]{:S(2)}, u32[]{:S(2)}) collective-permute-start(bf16[192,768]{1,0:T(8,128)(2,1)S(1)} %get-tuple-element.71), channel_id=1, source_target_pairs={{0,64},{1,65},{4,68},{5,69},{8,72},{9,73},{12,76},{13,77},{16,80},... | collective-permute-start | bytes 884744 | tf_op jit(solution)/shard_map/ppermute | solution.py:402
  45.4 3.7 %collective-permute-start.6 = (bf16[192,768]{1,0:T(8,128)(2,1)S(1)}, bf16[192,768]{1,0:T(8,128)(2,1)S(1)}, u32[]{:S(2)}, u32[]{:S(2)}) collective-permute-start(bf16[192,768]{1,0:T(8,128)(2,1)S(1)} %get-tuple-element.62), channel_id=1, source_target_pairs={{0,2},{1,3},{4,6},{5,7},{8,10},{9,11},{12,14},{13,15},{16,18},{17,... | collective-permute-start | bytes 884744 | tf_op jit(solution)/shard_map/ppermute | solution.py:402
  50.5 2.6 %collective-permute-start.7 = (bf16[192,768]{1,0:T(8,128)(2,1)S(1)}, bf16[192,768]{1,0:T(8,128)(2,1)S(1)}, u32[]{:S(2)}, u32[]{:S(2)}) collective-permute-start(bf16[192,768]{1,0:T(8,128)(2,1)S(1)} %get-tuple-element.63), channel_id=1, source_target_pairs={{0,128},{1,129},{4,132},{5,133},{8,136},{9,137},{12,140},{13,141},... | collective-permute-start | bytes 884744 | tf_op jit(solution)/shard_map/ppermute | solution.py:402
  53.0 2.6 %collective-permute-start.8 = (bf16[192,768]{1,0:T(8,128)(2,1)S(1)}, bf16[192,768]{1,0:T(8,128)(2,1)S(1)}, u32[]{:S(2)}, u32[]{:S(2)}) collective-permute-start(bf16[192,768]{1,0:T(8,128)(2,1)S(1)} %get-tuple-element.64), channel_id=1, source_target_pairs={{0,130},{1,131},{4,134},{5,135},{8,138},{9,139},{12,142},{13,143},... | collective-permute-start | bytes 884744 | tf_op jit(solution)/shard_map/ppermute | solution.py:402
  55.7 2.6 %shard_map.96 = (f32[192,768]{1,0:T(8,128)S(1)}, bf16[192,768]{1,0:T(8,128)(2,1)S(1)}, bf16[192,768]{1,0:T(8,128)(2,1)S(1)}, bf16[192,768]{1,0:T(8,128)(2,1)S(1)}) custom-call(bf16[768,640]{1,0:T(8,128)(2,1)S(1)} %get-tuple-element.51.refs_3_.x_ref, bf16[768,640]{1,0:T(8,128)(2,1)S(1)} %collective-permute-done.2.xp_ref, ...), custom_call_target="tpu_custom_call" | custom-call | flops 1509949440 | bytes 6000000 | tf_op jit(solution)/shard_map/pallas_call | solution.py:64
  58.6 3.4 %collective-permute-start.20 = (bf16[192,768]{1,0:T(8,128)(2,1)S(1)}, bf16[192,768]{1,0:T(8,128)(2,1)S(1)}, u32[]{:S(2)}, u32[]{:S(2)}) collective-permute-start(bf16[192,768]{1,0:T(8,128)(2,1)S(1)} %get-tuple-element.78), channel_id=1, source_target_pairs={{0,2},{1,3},{4,6},{5,7},{8,10},{9,11},{12,14},{13,15},{16,18},{17,... | collective-permute-start | bytes 884744 | tf_op jit(solution)/shard_map/ppermute | solution.py:402
  62.0 2.3 %collective-permute-start.21 = (bf16[192,768]{1,0:T(8,128)(2,1)S(1)}, bf16[192,768]{1,0:T(8,128)(2,1)S(1)}, u32[]{:S(2)}, u32[]{:S(2)}) collective-permute-start(bf16[192,768]{1,0:T(8,128)(2,1)S(1)} %get-tuple-element.79), channel_id=1, source_target_pairs={{0,128},{1,129},{4,132},{5,133},{8,136},{9,137},{12,140},{13,141},... | collective-permute-start | bytes 884744 | tf_op jit(solution)/shard_map/ppermute | solution.py:402
  69.5 3.7 %collective-permute-start.17 = (bf16[48,768]{1,0:T(8,128)(2,1)S(1)}, bf16[48,768]{1,0:T(8,128)(2,1)S(1)}, u32[]{:S(2)}, u32[]{:S(2)}) collective-permute-start(bf16[48,768]{1,0:T(8,128)(2,1)S(1)} %get-tuple-element.75), channel_id=1, source_target_pairs={{0,128},{1,129},{4,132},{5,133},{8,136},{9,137},{12,140},{13,141},... | collective-permute-start | bytes 221192 | tf_op jit(solution)/shard_map/ppermute | solution.py:402
  73.4 4.1 %collective-permute-done.16.refs_5_ = bf16[48,768]{1,0:T(8,128)(2,1)S(1)} collective-permute-done((bf16[48,768]{1,0:T(8,128)(2,1)S(1)}, bf16[48,768]{1,0:T(8,128)(2,1)S(1)}, u32[]{:S(2)}, u32[]{:S(2)}) %collective-permute-start.16) | collective-permute-done | bytes 73760 | tf_op jit(solution)/shard_map/ppermute | solution.py:402
  77.5 2.1 %collective-permute-start.18 = (bf16[48,768]{1,0:T(8,128)(2,1)S(1)}, bf16[48,768]{1,0:T(8,128)(2,1)S(1)}, u32[]{:S(2)}, u32[]{:S(2)}) collective-permute-start(bf16[48,768]{1,0:T(8,128)(2,1)S(1)} %get-tuple-element.76), channel_id=1, source_target_pairs={{0,130},{1,131},{4,134},{5,135},{8,138},{9,139},{12,142},{13,143},... | collective-permute-start | bytes 221192 | tf_op jit(solution)/shard_map/ppermute | solution.py:402
  84.8 2.7 %collective-permute-start.24 = (bf16[48,768]{1,0:T(8,128)(2,1)S(1)}, bf16[48,768]{1,0:T(8,128)(2,1)S(1)}, u32[]{:S(2)}, u32[]{:S(2)}) collective-permute-start(bf16[48,768]{1,0:T(8,128)(2,1)S(1)} %get-tuple-element.83), channel_id=1, source_target_pairs={{0,64},{1,65},{4,68},{5,69},{8,72},{9,73},{12,76},{13,77},{16,80},... | collective-permute-start | bytes 221192 | tf_op jit(solution)/shard_map/ppermute | solution.py:402
  90.7 2.4 %collective-permute-done.25.refs_11_ = bf16[48,768]{1,0:T(8,128)(2,1)S(1)} collective-permute-done((bf16[48,768]{1,0:T(8,128)(2,1)S(1)}, bf16[48,768]{1,0:T(8,128)(2,1)S(1)}, u32[]{:S(2)}, u32[]{:S(2)}) %collective-permute-start.25) | collective-permute-done | bytes 73760 | tf_op jit(solution)/shard_map/ppermute | solution.py:402
  94.0 4.0 %collective-permute-done.26.got_ref = bf16[24,2304]{1,0:T(8,128)(2,1)S(1)} collective-permute-done((bf16[24,2304]{1,0:T(8,128)(2,1)S(1)}, bf16[24,2304]{1,0:T(8,128)(2,1)S(1)}, u32[]{:S(2)}, u32[]{:S(2)}) %collective-permute-start.26) | collective-permute-done | bytes 110624 | tf_op jit(solution)/shard_map/ppermute | solution.py:484
  98.0 4.4 %collective-permute-start.27 = (bf16[12,2304]{1,0:T(8,128)(2,1)S(1)}, bf16[12,2304]{1,0:T(8,128)(2,1)S(1)}, u32[]{:S(2)}, u32[]{:S(2)}) collective-permute-start(bf16[12,2304]{1,0:T(8,128)(2,1)S(1)} %get-tuple-element.88), channel_id=1, source_target_pairs={{0,8},{1,9},{4,12},{5,13},{8,0},{9,1},{12,4},{13,5},{16,24},{17,25... | collective-permute-start | bytes 165896 | tf_op jit(solution)/shard_map/ppermute | solution.py:485
  102.5 2.3 %collective-permute-done.27.got_ref = bf16[12,2304]{1,0:T(8,128)(2,1)S(1)} collective-permute-done((bf16[12,2304]{1,0:T(8,128)(2,1)S(1)}, bf16[12,2304]{1,0:T(8,128)(2,1)S(1)}, u32[]{:S(2)}, u32[]{:S(2)}) %collective-permute-start.27) | collective-permute-done | bytes 55328 | tf_op jit(solution)/shard_map/ppermute | solution.py:485
  104.8 5.6 %collective-permute-start.28 = (bf16[6,2304]{1,0:T(8,128)(2,1)S(1)}, bf16[6,2304]{1,0:T(8,128)(2,1)S(1)}, u32[]{:S(2)}, u32[]{:S(2)}) collective-permute-start(bf16[6,2304]{1,0:T(8,128)(2,1)S(1)} %get-tuple-element.90), channel_id=1, source_target_pairs={{0,16},{1,17},{4,20},{5,21},{8,24},{9,25},{12,28},{13,29},{16,0},{... | collective-permute-start | bytes 82952 | tf_op jit(solution)/shard_map/ppermute | solution.py:490
  110.5 5.8 %shard_map.92 = bf16[512,1536]{1,0:T(8,128)(2,1)} custom-call(bf16[640,768]{1,0:T(8,128)(2,1)S(1)} %get-tuple-element.50._.g_ref.a_ref, bf16[640,768]{1,0:T(8,128)(2,1)S(1)} %get-tuple-element.56._.b_ref.g_ref, bf16[640,768]{1,0:T(8,128)(2,1)S(1)} %get-tuple-element.59.c_ref._.g_ref, bf16[64,1536]{1,0:T(8,128)(2,1)S(1)} %collective-permute-done.4.left_ref, ...), custom_call_target="tpu_custom_call" | custom-call | flops 3623878656 | bytes 12000000 | tf_op jit(solution)/shard_map/pallas_call | solution.py:64
  (70 shorter events, 31.2 us)
Async XLA Ops:
  1.8 6.2 %collective-permute-start = (bf16[64,1536]{1,0:T(8,128)(2,1)S(1)}, bf16[64,1536]{1,0:T(8,128)(2,1)S(1)}, u32[]{:S(2)}, u32[]{:S(2)}) collective-permute-start(bf16[64,1536]{1,0:T(8,128)(2,1)S(1)} %get-tuple-element.92), channel_id=1, source_target_pairs={{31,0},{0,1},{1,2},{2,3},{3,4},{4,5},{5,6},{6,7},{7,8},{8,9},{9,10... | collective-permute-start | bytes 589832 | tf_op jit(solution)/shard_map/ppermute | solution.py:448
  24.3 6.7 %collective-permute-start.2 = (bf16[768,640]{1,0:T(8,128)(2,1)S(1)}, bf16[768,640]{1,0:T(8,128)(2,1)S(1)}, u32[]{:S(2)}, u32[]{:S(2)}) collective-permute-start(bf16[768,640]{1,0:T(8,128)(2,1)S(1)} %get-tuple-element.55), channel_id=1, source_target_pairs={{0,1},{1,0},{4,5},{5,4},{8,9},{9,8},{12,13},{13,12},{16,17},{17,16... | collective-permute-start | bytes 2949128 | tf_op jit(solution)/shard_map/ppermute | solution.py:469
  30.6 7.4 %collective-permute-start.12 = (bf16[640,768]{1,0:T(8,128)(2,1)S(1)}, bf16[640,768]{1,0:T(8,128)(2,1)S(1)}, u32[]{:S(2)}, u32[]{:S(2)}) collective-permute-start(bf16[640,768]{1,0:T(8,128)(2,1)S(1)} %get-tuple-element.56._.b_ref.g_ref), channel_id=1, source_target_pairs={{0,1},{1,0},{4,5},{5,4},{8,9},{9,8},{12,13},{13,12},{16,17},{17,16... | collective-permute-start | bytes 2949128 | tf_op jit(solution)/shard_map/ppermute | solution.py:460
  37.9 15.2 %collective-permute-start.19 = (bf16[640,768]{1,0:T(8,128)(2,1)S(1)}, bf16[640,768]{1,0:T(8,128)(2,1)S(1)}, u32[]{:S(2)}, u32[]{:S(2)}) collective-permute-start(bf16[640,768]{1,0:T(8,128)(2,1)S(1)} %get-tuple-element.59.c_ref._.g_ref), channel_id=1, source_target_pairs={{0,1},{1,0},{4,5},{5,4},{8,9},{9,8},{12,13},{13,12},{16,17},{17,16... | collective-permute-start | bytes 2949128 | tf_op jit(solution)/shard_map/ppermute | solution.py:460
  40.6 9.9 %collective-permute-start.13 = (bf16[192,768]{1,0:T(8,128)(2,1)S(1)}, bf16[192,768]{1,0:T(8,128)(2,1)S(1)}, u32[]{:S(2)}, u32[]{:S(2)}) collective-permute-start(bf16[192,768]{1,0:T(8,128)(2,1)S(1)} %get-tuple-element.70), channel_id=1, source_target_pairs={{0,32},{1,33},{4,36},{5,37},{8,40},{9,41},{12,44},{13,45},{16,48},... | collective-permute-start | bytes 884744 | tf_op jit(solution)/shard_map/ppermute | solution.py:402
  42.1 16.5 %collective-permute-start.14 = (bf16[192,768]{1,0:T(8,128)(2,1)S(1)}, bf16[192,768]{1,0:T(8,128)(2,1)S(1)}, u32[]{:S(2)}, u32[]{:S(2)}) collective-permute-start(bf16[192,768]{1,0:T(8,128)(2,1)S(1)} %get-tuple-element.71), channel_id=1, source_target_pairs={{0,64},{1,65},{4,68},{5,69},{8,72},{9,73},{12,76},{13,77},{16,80},... | collective-permute-start | bytes 884744 | tf_op jit(solution)/shard_map/ppermute | solution.py:402
  44.9 17.1 %collective-permute-start.15 = (bf16[192,768]{1,0:T(8,128)(2,1)S(1)}, bf16[192,768]{1,0:T(8,128)(2,1)S(1)}, u32[]{:S(2)}, u32[]{:S(2)}) collective-permute-start(bf16[192,768]{1,0:T(8,128)(2,1)S(1)} %get-tuple-element.72), channel_id=1, source_target_pairs={{0,96},{1,97},{4,100},{5,101},{8,104},{9,105},{12,108},{13,109},{1... | collective-permute-start | bytes 884744 | tf_op jit(solution)/shard_map/ppermute | solution.py:402
  45.4 18.9 %collective-permute-start.6 = (bf16[192,768]{1,0:T(8,128)(2,1)S(1)}, bf16[192,768]{1,0:T(8,128)(2,1)S(1)}, u32[]{:S(2)}, u32[]{:S(2)}) collective-permute-start(bf16[192,768]{1,0:T(8,128)(2,1)S(1)} %get-tuple-element.62), channel_id=1, source_target_pairs={{0,2},{1,3},{4,6},{5,7},{8,10},{9,11},{12,14},{13,15},{16,18},{17,... | collective-permute-start | bytes 884744 | tf_op jit(solution)/shard_map/ppermute | solution.py:402
  50.5 15.7 %collective-permute-start.7 = (bf16[192,768]{1,0:T(8,128)(2,1)S(1)}, bf16[192,768]{1,0:T(8,128)(2,1)S(1)}, u32[]{:S(2)}, u32[]{:S(2)}) collective-permute-start(bf16[192,768]{1,0:T(8,128)(2,1)S(1)} %get-tuple-element.63), channel_id=1, source_target_pairs={{0,128},{1,129},{4,132},{5,133},{8,136},{9,137},{12,140},{13,141},... | collective-permute-start | bytes 884744 | tf_op jit(solution)/shard_map/ppermute | solution.py:402
  53.0 16.5 %collective-permute-start.8 = (bf16[192,768]{1,0:T(8,128)(2,1)S(1)}, bf16[192,768]{1,0:T(8,128)(2,1)S(1)}, u32[]{:S(2)}, u32[]{:S(2)}) collective-permute-start(bf16[192,768]{1,0:T(8,128)(2,1)S(1)} %get-tuple-element.64), channel_id=1, source_target_pairs={{0,130},{1,131},{4,134},{5,135},{8,138},{9,139},{12,142},{13,143},... | collective-permute-start | bytes 884744 | tf_op jit(solution)/shard_map/ppermute | solution.py:402
  58.6 21.0 %collective-permute-start.20 = (bf16[192,768]{1,0:T(8,128)(2,1)S(1)}, bf16[192,768]{1,0:T(8,128)(2,1)S(1)}, u32[]{:S(2)}, u32[]{:S(2)}) collective-permute-start(bf16[192,768]{1,0:T(8,128)(2,1)S(1)} %get-tuple-element.78), channel_id=1, source_target_pairs={{0,2},{1,3},{4,6},{5,7},{8,10},{9,11},{12,14},{13,15},{16,18},{17,... | collective-permute-start | bytes 884744 | tf_op jit(solution)/shard_map/ppermute | solution.py:402
  62.0 19.3 %collective-permute-start.21 = (bf16[192,768]{1,0:T(8,128)(2,1)S(1)}, bf16[192,768]{1,0:T(8,128)(2,1)S(1)}, u32[]{:S(2)}, u32[]{:S(2)}) collective-permute-start(bf16[192,768]{1,0:T(8,128)(2,1)S(1)} %get-tuple-element.79), channel_id=1, source_target_pairs={{0,128},{1,129},{4,132},{5,133},{8,136},{9,137},{12,140},{13,141},... | collective-permute-start | bytes 884744 | tf_op jit(solution)/shard_map/ppermute | solution.py:402
  64.3 18.3 %collective-permute-start.22 = (bf16[192,768]{1,0:T(8,128)(2,1)S(1)}, bf16[192,768]{1,0:T(8,128)(2,1)S(1)}, u32[]{:S(2)}, u32[]{:S(2)}) collective-permute-start(bf16[192,768]{1,0:T(8,128)(2,1)S(1)} %get-tuple-element.80), channel_id=1, source_target_pairs={{0,130},{1,131},{4,134},{5,135},{8,138},{9,139},{12,142},{13,143},... | collective-permute-start | bytes 884744 | tf_op jit(solution)/shard_map/ppermute | solution.py:402
  66.1 11.4 %collective-permute-start.16 = (bf16[48,768]{1,0:T(8,128)(2,1)S(1)}, bf16[48,768]{1,0:T(8,128)(2,1)S(1)}, u32[]{:S(2)}, u32[]{:S(2)}) collective-permute-start(bf16[48,768]{1,0:T(8,128)(2,1)S(1)} %get-tuple-element.74), channel_id=1, source_target_pairs={{0,2},{1,3},{4,6},{5,7},{8,10},{9,11},{12,14},{13,15},{16,18},{17,... | collective-permute-start | bytes 221192 | tf_op jit(solution)/shard_map/ppermute | solution.py:402
  69.5 14.3 %collective-permute-start.17 = (bf16[48,768]{1,0:T(8,128)(2,1)S(1)}, bf16[48,768]{1,0:T(8,128)(2,1)S(1)}, u32[]{:S(2)}, u32[]{:S(2)}) collective-permute-start(bf16[48,768]{1,0:T(8,128)(2,1)S(1)} %get-tuple-element.75), channel_id=1, source_target_pairs={{0,128},{1,129},{4,132},{5,133},{8,136},{9,137},{12,140},{13,141},... | collective-permute-start | bytes 221192 | tf_op jit(solution)/shard_map/ppermute | solution.py:402
  77.5 7.3 %collective-permute-start.18 = (bf16[48,768]{1,0:T(8,128)(2,1)S(1)}, bf16[48,768]{1,0:T(8,128)(2,1)S(1)}, u32[]{:S(2)}, u32[]{:S(2)}) collective-permute-start(bf16[48,768]{1,0:T(8,128)(2,1)S(1)} %get-tuple-element.76), channel_id=1, source_target_pairs={{0,130},{1,131},{4,134},{5,135},{8,138},{9,139},{12,142},{13,143},... | collective-permute-start | bytes 221192 | tf_op jit(solution)/shard_map/ppermute | solution.py:402
  79.6 7.9 %collective-permute-start.10 = (bf16[48,768]{1,0:T(8,128)(2,1)S(1)}, bf16[48,768]{1,0:T(8,128)(2,1)S(1)}, u32[]{:S(2)}, u32[]{:S(2)}) collective-permute-start(bf16[48,768]{1,0:T(8,128)(2,1)S(1)} %get-tuple-element.67), channel_id=1, source_target_pairs={{0,64},{1,65},{4,68},{5,69},{8,72},{9,73},{12,76},{13,77},{16,80},... | collective-permute-start | bytes 221192 | tf_op jit(solution)/shard_map/ppermute | solution.py:402
  81.3 7.5 %collective-permute-start.11 = (bf16[48,768]{1,0:T(8,128)(2,1)S(1)}, bf16[48,768]{1,0:T(8,128)(2,1)S(1)}, u32[]{:S(2)}, u32[]{:S(2)}) collective-permute-start(bf16[48,768]{1,0:T(8,128)(2,1)S(1)} %get-tuple-element.68), channel_id=1, source_target_pairs={{0,96},{1,97},{4,100},{5,101},{8,104},{9,105},{12,108},{13,109},{1... | collective-permute-start | bytes 221192 | tf_op jit(solution)/shard_map/ppermute | solution.py:402
  82.6 6.3 %collective-permute-start.9 = (bf16[48,768]{1,0:T(8,128)(2,1)S(1)}, bf16[48,768]{1,0:T(8,128)(2,1)S(1)}, u32[]{:S(2)}, u32[]{:S(2)}) collective-permute-start(bf16[48,768]{1,0:T(8,128)(2,1)S(1)} %get-tuple-element.66), channel_id=1, source_target_pairs={{0,32},{1,33},{4,36},{5,37},{8,40},{9,41},{12,44},{13,45},{16,48},... | collective-permute-start | bytes 221192 | tf_op jit(solution)/shard_map/ppermute | solution.py:402
  83.8 6.7 %collective-permute-start.23 = (bf16[48,768]{1,0:T(8,128)(2,1)S(1)}, bf16[48,768]{1,0:T(8,128)(2,1)S(1)}, u32[]{:S(2)}, u32[]{:S(2)}) collective-permute-start(bf16[48,768]{1,0:T(8,128)(2,1)S(1)} %get-tuple-element.82), channel_id=1, source_target_pairs={{0,32},{1,33},{4,36},{5,37},{8,40},{9,41},{12,44},{13,45},{16,48},... | collective-permute-start | bytes 221192 | tf_op jit(solution)/shard_map/ppermute | solution.py:402
  88.8 21.6 %collective-permute-start.4 = (bf16[64,1536]{1,0:T(8,128)(2,1)S(1)}, bf16[64,1536]{1,0:T(8,128)(2,1)S(1)}, u32[]{:S(2)}, u32[]{:S(2)}) collective-permute-start(bf16[64,1536]{1,0:T(8,128)(2,1)S(1)} %get-tuple-element.60), channel_id=1, source_target_pairs={{31,0},{0,1},{1,2},{2,3},{3,4},{4,5},{5,6},{6,7},{7,8},{8,9},{9,10... | collective-permute-start | bytes 589832 | tf_op jit(solution)/shard_map/ppermute | solution.py:477
  88.8 21.6 %collective-permute-start.5 = (bf16[64,1536]{1,0:T(8,128)(2,1)S(1)}, bf16[64,1536]{1,0:T(8,128)(2,1)S(1)}, u32[]{:S(2)}, u32[]{:S(2)}) collective-permute-start(bf16[64,1536]{1,0:T(8,128)(2,1)S(1)} %get-tuple-element.61), channel_id=1, source_target_pairs={{1,0},{2,1},{3,2},{4,3},{5,4},{6,5},{7,6},{8,7},{9,8},{10,9},{11,1... | collective-permute-start | bytes 589832 | tf_op jit(solution)/shard_map/ppermute | solution.py:476
  98.0 6.8 %collective-permute-start.27 = (bf16[12,2304]{1,0:T(8,128)(2,1)S(1)}, bf16[12,2304]{1,0:T(8,128)(2,1)S(1)}, u32[]{:S(2)}, u32[]{:S(2)}) collective-permute-start(bf16[12,2304]{1,0:T(8,128)(2,1)S(1)} %get-tuple-element.88), channel_id=1, source_target_pairs={{0,8},{1,9},{4,12},{5,13},{8,0},{9,1},{12,4},{13,5},{16,24},{17,25... | collective-permute-start | bytes 165896 | tf_op jit(solution)/shard_map/ppermute | solution.py:485
  104.8 11.5 %collective-permute-start.28 = (bf16[6,2304]{1,0:T(8,128)(2,1)S(1)}, bf16[6,2304]{1,0:T(8,128)(2,1)S(1)}, u32[]{:S(2)}, u32[]{:S(2)}) collective-permute-start(bf16[6,2304]{1,0:T(8,128)(2,1)S(1)} %get-tuple-element.90), channel_id=1, source_target_pairs={{0,16},{1,17},{4,20},{5,21},{8,24},{9,25},{12,28},{13,29},{16,0},{... | collective-permute-start | bytes 82952 | tf_op jit(solution)/shard_map/ppermute | solution.py:490
  (11 other events, 172.3 us)
where the time goes:
time: 117 us
  starting transfers between devices  54.5 us (47%)
  Pallas kernels  37.5 us (32%)
  waiting for transfers between devices  16.6 us (14%)
  local copies, waits for them, and re-layouts  7.47 us (6%)
    pallas_call x17, Pallas kernels, call(): pl.pallas_call(kernel, out_shape=out_shape, compiler_params=pltpu.Compile...  37.5 us
    ppermute x18, starting transfers between devices, exchange(): return [lax.ppermute(part, AXES, way) for part, way in zip(parts, routes)]  37.5 us
    ppermute x18, waiting for transfers between devices, exchange(): return [lax.ppermute(part, AXES, way) for part, way in zip(parts, routes)]  10.3 us
    ppermute x1, starting transfers between devices, body(): lax.ppermute(send, AXES, ACROSS_Z[2])  5.6 us
    ppermute x1, starting transfers between devices, body(): lax.ppermute(send, AXES, ACROSS_Z[1])  4.44 us
    ppermute x1, waiting for transfers between devices, body(): lax.ppermute(send, AXES, ACROSS_Z[0])  3.96 us
    unnamed x12, local copies, waits for them, and re-layouts  3.67 us
  transfers between devices with their start and end apart: 29, of which 8 were waited for; matrix products, arithmetic and copies ran while one was open for 2% of the time, Pallas kernels for 20%

commit v1 on v0

--- a/solution.py
+++ b/solution.py
@@ -53,17 +53,18 @@
 TO_CORE = route(lambda x, y, z, c: (x, y, z, 1 - c))
 ACROSS_X = [route(lambda x, y, z, c, m=m: (x ^ m, y, z, c)) for m in (1, 2, 3)]
 ACROSS_Y = [route(lambda x, y, z, c, m=m: (x, y ^ m, z, c)) for m in (1, 2, 3)]
-ACROSS_Z = [route(lambda x, y, z, c, m=m: (x, y, z ^ m, c)) for m in (1, 2, 4)]
+ACROSS_Z = {m: route(lambda x, y, z, c, m=m: (x, y, z ^ m, c)) for m in (1, 2, 3, 4)}
 
 
 def along_loop(distance):
     return [((i - distance) % 32, i) for i in range(32)]
 
 
-def call(kernel, out_shape, *args, vmem=16, **kwargs):
+def call(kernel, out_shape, *args, vmem=16, estimate=None, **kwargs):
     return pl.pallas_call(
         kernel,
         out_shape=out_shape,
+        cost_estimate=estimate or TINY,
         compiler_params=pltpu.CompilerParams(vmem_limit_bytes=vmem * MIB),
         **kwargs,
     )(*args)
@@ -85,12 +86,22 @@
     return jax.ShapeDtypeStruct((rows, cols), dtype)
 
 
-def cost(flops, size, transcendentals=0):
-    return pl.CostEstimate(flops=flops, bytes_accessed=size, transcendentals=transcendentals)
-
-
-def mask_kernel(incidence_ref, reach_ref, types_ref, out_ref):
-    row = types_ref[...].astype(F32)
+TINY = pl.CostEstimate(flops=1000, bytes_accessed=1000, transcendentals=0)
+
+
+def cost(microseconds):
+    return pl.CostEstimate(flops=microseconds * 1_000_000_000, bytes_accessed=1000, transcendentals=0)
+
+
+def mask_kernel(incidence_ref, reach_ref, place_ref, types_ref, _, out_ref):
+    seq_len = types_ref.shape[1]
+    start = place_ref[4] * ROWS
+    ahead = pl.multiple_of(lax.rem(start + seq_len - 2 * HALO, seq_len), 2 * HALO)
+    behind = pl.multiple_of(lax.rem(start + ROWS, seq_len), 2 * HALO)
+    before = types_ref[:, pl.ds(ahead, 2 * HALO)]
+    here = types_ref[:, pl.ds(pl.multiple_of(start, ROWS), ROWS)]
+    after = types_ref[:, pl.ds(behind, 2 * HALO)]
+    row = jnp.concatenate([before[:, HALO:], here, after[:, :HALO]], axis=1).astype(F32)
     column = jnp.broadcast_to(row, (2 * TILE, EXT)).T
     key = lax.broadcasted_iota(jnp.int32, (WIN, 2 * TILE), 0)
     query = lax.broadcasted_iota(jnp.int32, (WIN, 2 * TILE), 1) % TILE
@@ -98,28 +109,28 @@
     for t in range(TILES):
         own = row[:, HALO + t * TILE : HALO + (t + 1) * TILE]
         other_kind = column[t * TILE : t * TILE + WIN] != jnp.concatenate([own, own], axis=1)
-        linked = [jnp.full((TILE, 2 * TILE), incidence_ref[t, r], jnp.int32) for r in range(3)]
+        linked = [jnp.full((TILE, 2 * TILE), incidence_ref[r, t], jnp.int32) for r in range(3)]
         linked = jnp.concatenate(linked, axis=0) == 1
         allowed = (distance == 0) | ((distance <= reach_ref[t]) & other_kind & linked)
         out_ref[t * WIN : (t + 1) * WIN, :] = jnp.where(allowed, 1.0, 0.0)
 
 
-def make_mask(types, row_start, incidence, reach):
-    seq_len = types.shape[1]
-    padded = jnp.concatenate([types[:, seq_len - HALO :], types, types[:, :HALO]], axis=1)
-    near = lax.dynamic_slice_in_dim(padded, row_start, EXT, 1)
+def make_mask(types, place, incidence, reach, after):
     return call(
         mask_kernel,
         shape(TILES * WIN, 2 * TILE, F32),
-        incidence,
+        incidence.T,
         reach,
-        near,
-        in_specs=[scalars(), scalars(), whole()],
+        place,
+        types,
+        after,
+        estimate=cost(2),
+        in_specs=[scalars(), scalars(), scalars(), whole(), anywhere()],
         out_specs=whole(),
     )
 
 
-def projection_kernel(own_ref, left_ref, right_ref, w_ref, out_ref, rows):
+def projection_kernel(own_ref, left_ref, right_ref, w_ref, _, out_ref, rows):
     @pl.when(pl.program_id(0) == 0)
     def _():
         rows[:ROWS] = own_ref[...]
@@ -129,7 +140,7 @@
     out_ref[...] = dot(rows[...], w_ref[...], NN).astype(BF16)
 
 
-def projection(own, left, right, weights):
+def projection(own, left, right, weights, after):
     cols = weights.shape[1]
     return call(
         projection_kernel,
@@ -138,25 +149,25 @@
         left,
         right,
         weights,
-        vmem=24,
-        grid=(cols // GW,),
+        after,
+        vmem=32,
+        grid=(3,),
         in_specs=[
             pl.BlockSpec((ROWS, D), lambda i: (0, 0)),
             pl.BlockSpec((HALO, D), lambda i: (0, 0)),
             pl.BlockSpec((HALO, D), lambda i: (0, 0)),
-            pl.BlockSpec((D, GW), lambda i: (0, i)),
+            pl.BlockSpec((D, HW), lambda i: (0, i)),
+            anywhere(),
         ],
-        out_specs=pl.BlockSpec((EXT, GW), lambda i: (0, i)),
+        out_specs=pl.BlockSpec((EXT, HW), lambda i: (0, i)),
         scratch_shapes=[pltpu.VMEM((EXT, D), BF16)],
-        cost_estimate=cost(2 * EXT * D * cols, 12_000_000),
-    )
-
-
-def reorder_kernel(place_ref, own_ref, left_ref, right_ref, same_ref, other_ref, rows):
+    )
+
+
+def reorder_kernel(n_carried, place_ref, rows, *refs):
+    same_ref, other_ref, mark_ref = refs[n_carried:]
+    mark_ref[...] = jnp.zeros_like(mark_ref)
     x, y, z, core = place_ref[0], place_ref[1], place_ref[2], place_ref[3]
-    rows[:ROWS] = own_ref[...]
-    rows[ROWS : ROWS + HALO] = left_ref[...]
-    rows[ROWS + HALO :] = right_ref[...]
     block = D // 4
     half = block // 2
     place = lax.broadcasted_iota(jnp.int32, (block, block), 0)
@@ -186,22 +197,21 @@
                     ]
 
 
-def reorder(place, own, left, right, after):
-    def kernel(place_ref, own_ref, left_ref, right_ref, _, *refs):
-        reorder_kernel(place_ref, own_ref, left_ref, right_ref, *refs)
-
-    return call(
-        kernel,
-        (shape(HALF, EXT, BF16),) * 2,
+def reorder(place, rows, at, carried, after):
+    n_rows = rows.shape[0]
+    out_spec = pl.BlockSpec((HALF, n_rows), lambda i: (0, at // n_rows))
+    extra = list(carried) + list(after)
+    return call(
+        functools.partial(reorder_kernel, len(extra)),
+        (shape(HALF, EXT, BF16),) * 2 + (shape(8, 128, F32),),
         place,
-        own,
-        left,
-        right,
-        after,
-        in_specs=[scalars(), whole(), whole(), whole(), anywhere()],
-        out_specs=(whole(),) * 2,
-        scratch_shapes=[pltpu.VMEM((EXT, D), BF16)],
-        cost_estimate=cost(8 * EXT * (D // 4) ** 2, 4_000_000),
+        rows,
+        *extra,
+        estimate=cost(4),
+        grid=(1,),
+        in_specs=[scalars(), pl.BlockSpec((n_rows, D), lambda i: (0, 0))] + [anywhere()] * len(extra),
+        out_specs=(out_spec,) * 2 + (whole(),),
+        input_output_aliases={2 + i: i for i in range(len(carried))},
     )
 
 
@@ -248,7 +258,7 @@
         grad_ref[rows, :GW] = (gather(dot(scores, k_win, TN)) * HD**-0.5).astype(BF16)
         return 0
 
-    lax.fori_loop(0, TILES, step, 0, unroll=4)
+    lax.fori_loop(0, TILES, step, 0, unroll=True)
     grad_ref[ROWS:, :GW] = jnp.zeros((2 * HALO, GW), BF16)
     for part, acc, factor in ((1, dk, HD**-0.5), (2, dv, 1.0)):
         cols = slice(part * GW, (part + 1) * GW)
@@ -299,82 +309,116 @@
             pltpu.VMEM((EXT, GW), F32),
         ],
         input_output_aliases={5 + i: i for i in range(len(carried))},
-        cost_estimate=cost(36 * TILES * WIN * GW * GW, 4_000_000, 2 * TILES * WIN * GW),
-    )
-
-
-def weight_kernel(first, x_ref, xp_ref, g_ref, gp_ref, _, keep_ref, *send_refs):
-    total = dot(x_ref[...], g_ref[...], NN) + dot(xp_ref[...], gp_ref[...], NN)
+    )
+
+
+SENT = (((0, 3), (1, 2)), ((0, 1), (3, 2)))
+
+
+def weight_kernel(first, chosen, n_grads, x_ref, xp_ref, *refs):
     part = HALF // 4
     piece = part // 4
-    for j in range(4):
-        for i in range(4):
-            jy, jx = (j, i) if first == "y" else (i, j)
-            rows = total[jy * part + jx * piece : jy * part + (jx + 1) * piece]
-            at = slice(i * piece, (i + 1) * piece)
-            if j == 0:
-                keep_ref[at] = rows
-            else:
-                send_refs[j - 1][at] = rows.astype(BF16)
-
-
-def weight_parts(first, x_own, x_other, g_own, g_other, after):
-    part = HALF // 4
-    resident = pl.BlockSpec((HALF, EXT), lambda i: (0, 0))
-    moving = pl.BlockSpec((EXT, GW), lambda i: (0, i))
-    return call(
-        functools.partial(weight_kernel, first),
-        (shape(part, 3 * GW, F32),) + (shape(part, 3 * GW, BF16),) * 3,
+    outs = refs[-4:]
+    for n, (g, block) in enumerate(chosen):
+        cols = slice(block * GW, (block + 1) * GW)
+        total = dot(x_ref[...], refs[g][:, cols], NN) + dot(xp_ref[...], refs[n_grads + g][:, cols], NN)
+        cols = slice(n * GW, (n + 1) * GW)
+        for half, picked in enumerate(SENT):
+            for ref, parts in zip(outs[2 * half : 2 * half + 2], picked):
+                for m, j in enumerate(parts):
+                    for i in range(2):
+                        jy, jx = (j, 2 * half + i) if first == "y" else (2 * half + i, j)
+                        rows = total[jy * part + jx * piece : jy * part + (jx + 1) * piece]
+                        ref[(2 * m + i) * piece : (2 * m + i + 1) * piece, cols] = rows.astype(ref.dtype)
+
+
+def weight_parts(first, chosen, x_own, x_other, grads, others, after):
+    rows, cols = HALF // 4, GW * len(chosen)
+    n_in = 2 + 2 * len(grads)
+    return call(
+        functools.partial(weight_kernel, first, chosen, len(grads)),
+        (shape(rows, cols, F32), shape(rows, cols, BF16)) * 2,
         x_own,
         x_other,
-        g_own,
-        g_other,
-        after,
-        grid=(3,),
-        in_specs=[resident, resident, moving, moving, anywhere()],
-        out_specs=(pl.BlockSpec((part, GW), lambda i: (0, i)),) * 4,
-        cost_estimate=cost(4 * HALF * EXT * 3 * GW, 6_000_000),
-    )
-
-
-def split_kernel(keep_ref, a_ref, b_ref, c_ref, out_ref, *send_refs):
+        *grads,
+        *others,
+        *after,
+        vmem=24,
+        in_specs=[whole()] * n_in + [anywhere()] * len(after),
+        out_specs=(whole(),) * 4,
+    )
+
+
+def middle_kernel(a_ref, got_a_ref, b_ref, got_b_ref, *refs):
+    for n, (ref, got) in enumerate(((a_ref, got_a_ref), (b_ref, got_b_ref))):
+        keep_ref, send_ref = refs[2 * n - 4], refs[2 * n - 3]
+        half = keep_ref.shape[0]
+        total = ref[...] + got[...].astype(F32)
+        keep_ref[...] = total[:half]
+        send_ref[...] = total[half:].astype(BF16)
+
+
+def middle(keep_a, got_a, keep_b, got_b, after):
+    rows, cols = keep_a.shape[0] // 2, keep_a.shape[1]
+    return call(
+        middle_kernel,
+        (shape(rows, cols, F32), shape(rows, cols, BF16)) * 2,
+        keep_a,
+        got_a,
+        keep_b,
+        got_b,
+        *after,
+        in_specs=[whole()] * 4 + [anywhere()] * len(after),
+        out_specs=(whole(),) * 4,
+    )
+
+
+def split_kernel(a_ref, got_a_ref, b_ref, got_b_ref, *refs):
+    out_ref, *send_refs = refs[-4:]
     part = out_ref.shape[0]
     for j in range(4):
-        rows = slice(j * part, (j + 1) * part)
-        total = keep_ref[rows] + a_ref[rows].astype(F32) + b_ref[rows].astype(F32) + c_ref[rows].astype(F32)
+        ref, got = ((a_ref, got_a_ref), (b_ref, got_b_ref))[j // 2]
+        rows = slice(j % 2 * part, (j % 2 + 1) * part)
+        total = ref[rows] + got[rows].astype(F32)
         if j == 0:
             out_ref[...] = total
         else:
             send_refs[j - 1][...] = total.astype(BF16)
 
 
-def split_sum(keep, received):
-    rows, cols = keep.shape[0] // 4, keep.shape[1]
+def split_sum(keep_a, got_a, keep_b, got_b, after):
+    rows, cols = keep_a.shape[0] // 2, keep_a.shape[1]
     return call(
         split_kernel,
         (shape(rows, cols, F32),) + (shape(rows, cols, BF16),) * 3,
-        keep,
-        *received,
-        in_specs=[whole()] * 4,
+        keep_a,
+        got_a,
+        keep_b,
+        got_b,
+        *after,
+        in_specs=[whole()] * 4 + [anywhere()] * len(after),
         out_specs=(whole(),) * 4,
     )
 
 
 def join_kernel(*refs):
-    keep_ref, send_ref = refs[-2:]
-    half = keep_ref.shape[0]
-    for g in range(GROUPS):
-        total = refs[4 * g][...]
-        for r in refs[4 * g + 1 : 4 * g + 4]:
+    keep_ref, *send_refs = refs[-4:]
+    at = 0
+    for n in range(0, len(refs) - 4, 4):
+        total = refs[n][...]
+        for r in refs[n + 1 : n + 4]:
             total = total + r[...].astype(F32)
-        cols = slice(g * 3 * GW, (g + 1) * 3 * GW)
-        keep_ref[:, cols] = total[:half]
-        send_ref[:, cols] = total[half:].astype(BF16)
-
-
-def halve_kernel(keep_ref, got_ref, out_ref, send_ref):
+        cols = slice(at, at + total.shape[1])
+        at += total.shape[1]
+        part = keep_ref.shape[0]
+        keep_ref[:, cols] = total[:part]
+        for j in range(3):
+            send_refs[j][:, cols] = total[(j + 1) * part : (j + 2) * part].astype(BF16)
+
+
+def halve_kernel(keep_ref, a_ref, b_ref, c_ref, out_ref, send_ref):
     half = out_ref.shape[0]
-    total = keep_ref[...] + got_ref[...].astype(F32)
+    total = keep_ref[...] + a_ref[...].astype(F32) + b_ref[...].astype(F32) + c_ref[...].astype(F32)
     out_ref[...] = total[:half]
     send_ref[...] = total[half:].astype(BF16)
 
@@ -387,22 +431,18 @@
             out_ref[:, k * HW + g * GW : k * HW + (g + 1) * GW] = total[:, at : at + GW]
 
 
-def halves(kernel, rows, *args):
+def cut_rows(kernel, rows, n_sent, *args):
     cols = 3 * HW
     return call(
         kernel,
-        (shape(rows, cols, F32), shape(rows, cols, BF16)),
+        (shape(rows, cols, F32),) + (shape(rows, cols, BF16),) * n_sent,
         *args,
         in_specs=[whole()] * len(args),
-        out_specs=(whole(),) * 2,
-    )
-
-
-def exchange(parts, routes):
-    return [lax.ppermute(part, AXES, way) for part, way in zip(parts, routes)]
-
-
-def token_kernel(a_ref, b_ref, c_ref, left_ref, right_ref, w_ref, out_ref, grad):
+        out_specs=(whole(),) * (1 + n_sent),
+    )
+
+
+def token_kernel(a_ref, b_ref, c_ref, left_ref, right_ref, w_ref, _, out_ref, mark_ref, grad):
     @pl.when(pl.program_id(0) == 0)
     def _():
         for g, ref in enumerate((a_ref, b_ref, c_ref)):
@@ -418,40 +458,44 @@
                 grad[HALO : ROWS - HALO, cols] = ref[HALO : ROWS - HALO, own]
 
     out_ref[...] = dot(grad[...], w_ref[...], NT).astype(BF16)
-
-
-def token_gradient(grads, from_left, from_right, weights):
-    block = 256
+    mark_ref[...] = jnp.zeros_like(mark_ref)
+
+
+def token_gradient(grads, from_left, from_right, weights, after):
+    block = 512
     cols = weights.shape[1]
     grad_spec = pl.BlockSpec((EXT, 3 * GW), lambda i: (0, 0))
     rim_spec = pl.BlockSpec((HALO, 2 * HW), lambda i: (0, 0))
     return call(
         token_kernel,
-        shape(ROWS, D, BF16),
+        (shape(ROWS, D, BF16), shape(8, 128, F32)),
         *grads,
         from_left,
         from_right,
         weights,
+        after,
         vmem=24,
         grid=(D // block,),
-        in_specs=[grad_spec] * 3 + [rim_spec] * 2 + [pl.BlockSpec((block, cols), lambda i: (i, 0))],
-        out_specs=pl.BlockSpec((ROWS, block), lambda i: (0, i)),
+        in_specs=[grad_spec] * 3 + [rim_spec] * 2 + [pl.BlockSpec((block, cols), lambda i: (i, 0)), anywhere()],
+        out_specs=(pl.BlockSpec((ROWS, block), lambda i: (0, i)), pl.BlockSpec((8, 128), lambda i: (0, 0))),
         scratch_shapes=[pltpu.VMEM((ROWS, cols), BF16)],
-        cost_estimate=cost(2 * ROWS * D * cols, 12_000_000),
     )
 
 
 def body(tokens, weights, cotangent, token_types, incidence, window_reach):
     own = tokens[0]
     dp, loop = lax.axis_index("dp"), lax.axis_index("loop")
-    place = jnp.stack([dp % 4, dp // 4 * 2 + loop // 2 % 2, loop // 4, loop % 2]).astype(jnp.int32)
+    place = jnp.stack([dp % 4, dp // 4 * 2 + loop // 2 % 2, loop // 4, loop % 2, loop]).astype(jnp.int32)
     left = lax.ppermute(own[ROWS - HALO :], "loop", along_loop(1))
     right = lax.ppermute(own[:HALO], "loop", along_loop(-1))
-    mask = make_mask(token_types, loop * ROWS, incidence[0], window_reach[0])
-    proj = projection(own, left, right, weights)
-
-    first = ("y", "x", "y")
-    carried, grads, others, waiting = (), [], [], []
+    *arranged, mark = reorder(place, own, 0, (), ())
+    mask = make_mask(token_types, place, incidence[0], window_reach[0], mark)
+    x_own, x_send, mark = reorder(place, jnp.concatenate([left, right], axis=0), ROWS, arranged, (mask,))
+    x_other = lax.ppermute(x_send, AXES, TO_CORE)
+    proj = projection(own, left, right, weights, mark)
+
+    blocks = [(g, k) for g in range(GROUPS) for k in range(3)]
+    carried, grads, others = (), [], []
 
     def attend(group, after):
         nonlocal carried
@@ -459,39 +503,48 @@
         grads.append(grad)
         others.append(lax.ppermute(grad, AXES, TO_CORE))
 
-    def weigh(group, after):
-        keep, *sent = weight_parts(first[group], x_own, x_other, grads[group], others[group], after)
-        waiting.append((keep, exchange(sent, ACROSS_Y if first[group] == "y" else ACROSS_X)))
-        return keep
+    def swap(n, way, part):
+        return lax.ppermute(part, AXES, (ACROSS_Y if way == "y" else ACROSS_X)[n - 1])
+
+    def round_one(way, chosen, after):
+        used = sorted({g for g, _ in chosen})
+        chosen = tuple((used.index(g), k) for g, k in chosen)
+        mine, theirs = [grads[g] for g in used], [others[g] for g in used]
+        keep_a, send_a, keep_b, send_b = weight_parts(way, chosen, x_own, x_other, mine, theirs, after)
+        return keep_a, swap(1, way, send_a), keep_b, swap(3, way, send_b)
+
+    def round_two(way, state, after):
+        keep_a, send_a, keep_b, send_b = middle(*state, after)
+        return keep_a, swap(3, way, send_a), keep_b, swap(1, way, send_b)
+
+    def round_three(way, state, after):
+        keep, *sent = split_sum(*state, after)
+        return [keep, *(swap(n + 1, way, part) for n, part in enumerate(sent))]
 
     attend(0, ())
-    x_own, x_send = reorder(place, own, left, right, grads[0])
-    x_other = lax.ppermute(x_send, AXES, TO_CORE)
-    attend(1, (x_own,))
-    keep = weigh(0, grads[1])
-    attend(2, (keep,))
-    keep = weigh(1, grads[2])
-    weigh(2, keep)
+    attend(1, ())
+    attend(2, ())
     attended, rim_left, rim_right = carried
     from_right = lax.ppermute(rim_left, "loop", along_loop(-1))
     from_left = lax.ppermute(rim_right, "loop", along_loop(1))
-
-    parts = []
-    for group in range(GROUPS):
-        keep, *sent = split_sum(*waiting[group])
-        parts += [keep, *exchange(sent, ACROSS_X if first[group] == "y" else ACROSS_Y)]
-    keep, send = halves(join_kernel, 24, *parts)
-    keep, send = halves(halve_kernel, 12, keep, lax.ppermute(send, AXES, ACROSS_Z[0]))
-    keep, send = halves(halve_kernel, 6, keep, lax.ppermute(send, AXES, ACROSS_Z[1]))
+    by_y = round_one("y", blocks[:5], (rim_left,))
+    by_x = round_one("x", blocks[5:], (by_y[0], from_left, from_right))
+    token_grad, mark = token_gradient(grads, from_left, from_right, weights, by_x[0])
+    by_y = round_two("y", by_y, (mark,))
+    by_x = round_two("x", by_x, (by_y[0],))
+    by_y = round_three("x", by_y, (by_x[0],))
+    by_x = round_three("y", by_x, (by_y[0],))
+    keep, *sent = cut_rows(join_kernel, 12, 3, *by_y, *by_x)
+    got = [lax.ppermute(part, AXES, ACROSS_Z[m]) for part, m in zip(sent, (2, 1, 3))]
+    keep, send = cut_rows(halve_kernel, 6, 1, keep, *got)
     weight_grad = call(
         functools.partial(last_kernel, (256 * ROWS) ** -0.5),
         shape(6, 3 * HW, F32),
         keep,
-        lax.ppermute(send, AXES, ACROSS_Z[2]),
+        lax.ppermute(send, AXES, ACROSS_Z[4]),
         in_specs=[whole()] * 2,
         out_specs=whole(),
     )
-    token_grad = token_gradient(grads, from_left, from_right, weights)
     return attended[None], token_grad[None], weight_grad
 
 

time: 117 us -> 100 us (0.85)
  starting transfers between devices: 54.5 us -> 38.6 us
  waiting for transfers between devices: 16.6 us -> 21.3 us
  Pallas kernels: 37.5 us -> 33.9 us
  local copies, waits for them, and re-layouts: 7.47 us -> 4.74 us
    ppermute x21 -> x18, starting transfers between devices: 48.4 us -> 31.1 us  [the longest x14 22.9 us: swap(): lax.ppermute(part, AXES, (ACROSS_Y if way == 'y' else ACROSS_X)[n - 1])]
    ppermute x1, starting transfers between devices: 1.74 us -> 5.82 us  [body(): from_right = lax.ppermute(rim_left, 'loop', along_loop(-1))]
    pallas_call x17, Pallas kernels: 37.5 us -> 33.9 us  [call(): pl.pallas_call(kernel, out_shape=out_shape, cost_estimate=estimate or TIN...]
    ppermute x1, waiting for transfers between devices: 0.01 us -> 3.15 us  [body(): left = lax.ppermute(own[ROWS - HALO:], 'loop', along_loop(1))]
    ppermute x1, starting transfers between devices: 1.93 us -> 0.09 us  [body(): x_other = lax.ppermute(x_send, AXES, TO_CORE)]
    ppermute x1, starting transfers between devices: 1.73 us -> 0.08 us  [body(): right = lax.ppermute(own[:HALO], 'loop', along_loop(-1))]
    ppermute x21 -> x18, waiting for transfers between devices: 16.6 us -> 18.1 us  [the longest x14 10.5 us: swap(): lax.ppermute(part, AXES, (ACROSS_Y if way == 'y' else ACROSS_X)[n - 1])]
    unnamed x12 -> x17, local copies, waits for them, and re-layouts: 3.67 us -> 3.6 us
  transfers between devices with their start and end apart: 29 -> 26, of which waited for: 8 -> 10; matrix products, arithmetic and copies ran while one was open for 2% -> 0% of each run, Pallas kernels for 20% -> 32%
where the time goes in v1:
time: 100 us; the launch traced here: 99.4 us
  starting transfers between devices  38.6 us (39%)
  Pallas kernels  33.9 us (34%)
  waiting for transfers between devices  21.3 us (21%)
  local copies, waits for them, and re-layouts  4.74 us (5%)
    pallas_call x17, Pallas kernels, call(): pl.pallas_call(kernel, out_shape=out_shape, cost_estimate=estimate or TIN...  33.9 us
    ppermute x14, starting transfers between devices, swap(): lax.ppermute(part, AXES, (ACROSS_Y if way == 'y' else ACROSS_X)[n - 1])  22.9 us
    ppermute x14, waiting for transfers between devices, swap(): lax.ppermute(part, AXES, (ACROSS_Y if way == 'y' else ACROSS_X)[n - 1])  10.5 us
    ppermute x1, starting transfers between devices, body(): from_right = lax.ppermute(rim_left, 'loop', along_loop(-1))  5.82 us
    ppermute x3, starting transfers between devices, body(): lax.ppermute(part, AXES, ACROSS_Z[m])  4.46 us
    ppermute x1, waiting for transfers between devices, body(): lax.ppermute(send, AXES, ACROSS_Z[4])  4.23 us
    ppermute x1, starting transfers between devices, body(): lax.ppermute(send, AXES, ACROSS_Z[4])  3.73 us
    unnamed x17, local copies, waits for them, and re-layouts  3.6 us
  transfers between devices with their start and end apart: 26, of which 10 were waited for; matrix products, arithmetic and copies ran while one was open for 0% of the time, Pallas kernels for 32%

profile of v1, /device:TPU:8, one launch (start us, length us, event | category | flops | bytes accessed | tf_op | source)
XLA Modules:
  0.0 99.4 jit_solution(5532592762573600696)
XLA Ops:
  3.8 1.6 %shard_map.85 = (bf16[768,640]{1,0:T(8,128)(2,1)S(1)}, bf16[768,640]{1,0:T(8,128)(2,1)S(1)}, f32[8,128]{1,0:T(8,128)S(1)}) custom-call(s32[5]{0:T(128)S(1)} %stack.23.place_ref, bf16[512,1536]{1,0:T(8,128)(2,1)S(1)} %bitcast.24), custom_call_target="tpu_custom_call" | custom-call | flops 4000000000 | bytes 1000 | tf_op jit(solution)/shard_map/pallas_call | solution.py:64
  6.4 3.1 %collective-permute-done.left_ref = bf16[64,1536]{1,0:T(8,128)(2,1)S(1)} collective-permute-done((bf16[64,1536]{1,0:T(8,128)(2,1)S(1)}, bf16[64,1536]{1,0:T(8,128)(2,1)S(1)}, u32[]{:S(2)}, u32[]{:S(2)}) %collective-permute-start) | collective-permute-done | bytes 196640 | tf_op jit(solution)/shard_map/ppermute | solution.py:489
  13.1 5.9 %shard_map.88.q_ref.k_ref.v_ref = bf16[640,2304]{1,0:T(8,128)(2,1)S(1)} custom-call(bf16[512,1536]{1,0:T(8,128)(2,1)S(1)} %bitcast.25, bf16[64,1536]{1,0:T(8,128)(2,1)S(1)} %collective-permute-done.left_ref, bf16[64,1536]{1,0:T(8,128)(2,1)S(1)} %collective-permute-done.1.right_ref, bf16[1536,2304]{1,0:T(8,128)(2,1)S(1)} %bitcast.20, ...), custom_call_target="tpu_custom_call" | custom-call | flops 1000 | bytes 1000 | tf_op jit(solution)/shard_map/pallas_call | solution.py:64
  18.9 4.0 %shard_map.89 = (bf16[512,768]{1,0:T(8,128)(2,1)}, bf16[64,1536]{1,0:T(8,128)(2,1)S(1)}, bf16[64,1536]{1,0:T(8,128)(2,1)S(1)}, bf16[640,768]{1,0:T(8,128)(2,1)S(1)}) custom-call(bf16[640,2304]{1,0:T(8,128)(2,1)S(1)} %shard_map.88.q_ref.k_ref.v_ref, bf16[640,2304]{1,0:T(8,128)(2,1)S(1)} %shard_map.88.q_ref.k_ref.v_ref, ...), custom_call_target="tpu_custom_call" | custom-call | flops 1000 | bytes 1000 | tf_op jit(solution)/shard_map/pallas_call | solution.py:64
  22.9 4.0 %shard_map.90 = (bf16[512,768]{1,0:T(8,128)(2,1)}, bf16[64,1536]{1,0:T(8,128)(2,1)S(1)}, bf16[64,1536]{1,0:T(8,128)(2,1)S(1)}, bf16[640,768]{1,0:T(8,128)(2,1)S(1)}) custom-call(bf16[640,2304]{1,0:T(8,128)(2,1)S(1)} %shard_map.88.q_ref.k_ref.v_ref, ...), custom_call_target="tpu_custom_call", output_to_operand_aliasing={{0}: (5, {}), {1}: (6, {}), {2}: (7, {})} | custom-call | flops 1000 | bytes 1000 | tf_op jit(solution)/shard_map/pallas_call | solution.py:64
  27.4 4.0 %shard_map.91 = (bf16[512,768]{1,0:T(8,128)(2,1)}, bf16[64,1536]{1,0:T(8,128)(2,1)S(1)}, bf16[64,1536]{1,0:T(8,128)(2,1)S(1)}, bf16[640,768]{1,0:T(8,128)(2,1)S(1)}) custom-call(bf16[640,2304]{1,0:T(8,128)(2,1)S(1)} %shard_map.88.q_ref.k_ref.v_ref, ...), custom_call_target="tpu_custom_call", output_to_operand_aliasing={{0}: (5, {}), {1}: (6, {}), {2}: (7, {})} | custom-call | flops 1000 | bytes 1000 | tf_op jit(solution)/shard_map/pallas_call | solution.py:64
  31.9 5.8 %collective-permute-start.3 = (bf16[64,1536]{1,0:T(8,128)(2,1)S(1)}, bf16[64,1536]{1,0:T(8,128)(2,1)S(1)}, u32[]{:S(2)}, u32[]{:S(2)}) collective-permute-start(bf16[64,1536]{1,0:T(8,128)(2,1)S(1)} %get-tuple-element.68.refs_4_), channel_id=1, source_target_pairs={{1,0},{2,1},{3,2},{4,3},{5,4},{6,5},{7,6},{8,7},{9,8},{10,9},{11,1... | collective-permute-start | bytes 589832 | tf_op jit(solution)/shard_map/ppermute | solution.py:528
  37.7 3.2 %shard_map.92 = (f32[192,1280]{1,0:T(8,128)S(1)}, bf16[192,1280]{1,0:T(8,128)(2,1)S(1)}, f32[192,1280]{1,0:T(8,128)S(1)}, bf16[192,1280]{1,0:T(8,128)(2,1)S(1)}) custom-call(bf16[768,640]{1,0:T(8,128)(2,1)S(1)} %get-tuple-element.69.x_ref, bf16[768,640]{1,0:T(8,128)(2,1)S(1)} %collective-permute-done.4.xp_ref, ...), custom_call_target="tpu_custom_call" | custom-call | flops 1000 | bytes 1000 | tf_op jit(solution)/shard_map/pallas_call | solution.py:64
  40.9 3.8 %collective-permute-start.8 = (bf16[192,1280]{1,0:T(8,128)(2,1)S(1)}, bf16[192,1280]{1,0:T(8,128)(2,1)S(1)}, u32[]{:S(2)}, u32[]{:S(2)}) collective-permute-start(bf16[192,1280]{1,0:T(8,128)(2,1)S(1)} %get-tuple-element.74), channel_id=1, source_target_pairs={{0,2},{1,3},{4,6},{5,7},{8,10},{9,11},{12,14},{13,15},{16,18},{17,... | collective-permute-start | bytes 1474568 | tf_op jit(solution)/shard_map/ppermute | solution.py:507
  45.7 2.6 %shard_map.93 = (f32[192,1024]{1,0:T(8,128)S(1)}, bf16[192,1024]{1,0:T(8,128)(2,1)S(1)}, f32[192,1024]{1,0:T(8,128)S(1)}, bf16[192,1024]{1,0:T(8,128)(2,1)S(1)}) custom-call(bf16[768,640]{1,0:T(8,128)(2,1)S(1)} %get-tuple-element.69.x_ref, bf16[768,640]{1,0:T(8,128)(2,1)S(1)} %collective-permute-done.4.xp_ref, ...), custom_call_target="tpu_custom_call" | custom-call | flops 1000 | bytes 1000 | tf_op jit(solution)/shard_map/pallas_call | solution.py:64
  48.3 1.6 %collective-permute-start.12 = (bf16[192,1024]{1,0:T(8,128)(2,1)S(1)}, bf16[192,1024]{1,0:T(8,128)(2,1)S(1)}, u32[]{:S(2)}, u32[]{:S(2)}) collective-permute-start(bf16[192,1024]{1,0:T(8,128)(2,1)S(1)} %get-tuple-element.82), channel_id=1, source_target_pairs={{0,32},{1,33},{4,36},{5,37},{8,40},{9,41},{12,44},{13,45},{16,48},... | collective-permute-start | bytes 1179656 | tf_op jit(solution)/shard_map/ppermute | solution.py:507
  49.9 2.1 %collective-permute-start.13 = (bf16[192,1024]{1,0:T(8,128)(2,1)S(1)}, bf16[192,1024]{1,0:T(8,128)(2,1)S(1)}, u32[]{:S(2)}, u32[]{:S(2)}) collective-permute-start(bf16[192,1024]{1,0:T(8,128)(2,1)S(1)} %get-tuple-element.84), channel_id=1, source_target_pairs={{0,96},{1,97},{4,100},{5,101},{8,104},{9,105},{12,108},{13,109},{1... | collective-permute-start | bytes 1179656 | tf_op jit(solution)/shard_map/ppermute | solution.py:507
  52.0 5.2 %shard_map.94 = (bf16[512,1536]{1,0:T(8,128)(2,1)}, f32[8,128]{1,0:T(8,128)S(1)}) custom-call(bf16[640,768]{1,0:T(8,128)(2,1)S(1)} %get-tuple-element.64.refs_0_.a_ref, bf16[640,768]{1,0:T(8,128)(2,1)S(1)} %get-tuple-element.65.refs_1_.refs_0_.b_ref, bf16[640,768]{1,0:T(8,128)(2,1)S(1)} %get-tuple-element.66.refs_1_.c_ref, ...), custom_call_target="tpu_custom_call" | custom-call | flops 1000 | bytes 1000 | tf_op jit(solution)/shard_map/pallas_call | solution.py:64
  58.6 1.8 %collective-permute-start.11 = (bf16[96,1280]{1,0:T(8,128)(2,1)S(1)}, bf16[96,1280]{1,0:T(8,128)(2,1)S(1)}, u32[]{:S(2)}, u32[]{:S(2)}) collective-permute-start(bf16[96,1280]{1,0:T(8,128)(2,1)S(1)} %get-tuple-element.81), channel_id=1, source_target_pairs={{0,2},{1,3},{4,6},{5,7},{8,10},{9,11},{12,14},{13,15},{16,18},{17,... | collective-permute-start | bytes 737288 | tf_op jit(solution)/shard_map/ppermute | solution.py:507
  60.5 2.2 %collective-permute-start.17 = (bf16[96,1024]{1,0:T(8,128)(2,1)S(1)}, bf16[96,1024]{1,0:T(8,128)(2,1)S(1)}, u32[]{:S(2)}, u32[]{:S(2)}) collective-permute-start(bf16[96,1024]{1,0:T(8,128)(2,1)S(1)} %get-tuple-element.90), channel_id=1, source_target_pairs={{0,96},{1,97},{4,100},{5,101},{8,104},{9,105},{12,108},{13,109},{1... | collective-permute-start | bytes 589832 | tf_op jit(solution)/shard_map/ppermute | solution.py:507
  65.6 1.9 %collective-permute-done.17.got_a_ref = bf16[96,1024]{1,0:T(8,128)(2,1)S(1)} collective-permute-done((bf16[96,1024]{1,0:T(8,128)(2,1)S(1)}, bf16[96,1024]{1,0:T(8,128)(2,1)S(1)}, u32[]{:S(2)}, u32[]{:S(2)}) %collective-permute-start.17) | collective-permute-done | bytes 196640 | tf_op jit(solution)/shard_map/ppermute | solution.py:507
  68.7 2.9 %collective-permute-start.19 = (bf16[48,1024]{1,0:T(8,128)(2,1)S(1)}, bf16[48,1024]{1,0:T(8,128)(2,1)S(1)}, u32[]{:S(2)}, u32[]{:S(2)}) collective-permute-start(bf16[48,1024]{1,0:T(8,128)(2,1)S(1)} %get-tuple-element.94), channel_id=1, source_target_pairs={{0,2},{1,3},{4,6},{5,7},{8,10},{9,11},{12,14},{13,15},{16,18},{17,... | collective-permute-start | bytes 294920 | tf_op jit(solution)/shard_map/ppermute | solution.py:507
  71.6 1.9 %collective-permute-start.15 = (bf16[48,1280]{1,0:T(8,128)(2,1)S(1)}, bf16[48,1280]{1,0:T(8,128)(2,1)S(1)}, u32[]{:S(2)}, u32[]{:S(2)}) collective-permute-start(bf16[48,1280]{1,0:T(8,128)(2,1)S(1)} %get-tuple-element.88), channel_id=1, source_target_pairs={{0,64},{1,65},{4,68},{5,69},{8,72},{9,73},{12,76},{13,77},{16,80},... | collective-permute-start | bytes 368648 | tf_op jit(solution)/shard_map/ppermute | solution.py:507
  73.5 2.8 %collective-permute-start.16 = (bf16[48,1280]{1,0:T(8,128)(2,1)S(1)}, bf16[48,1280]{1,0:T(8,128)(2,1)S(1)}, u32[]{:S(2)}, u32[]{:S(2)}) collective-permute-start(bf16[48,1280]{1,0:T(8,128)(2,1)S(1)} %get-tuple-element.89), channel_id=1, source_target_pairs={{0,96},{1,97},{4,100},{5,101},{8,104},{9,105},{12,108},{13,109},{1... | collective-permute-start | bytes 368648 | tf_op jit(solution)/shard_map/ppermute | solution.py:507
  77.8 4.7 %collective-permute-done.20.refs_6_ = bf16[48,1024]{1,0:T(8,128)(2,1)S(1)} collective-permute-done((bf16[48,1024]{1,0:T(8,128)(2,1)S(1)}, bf16[48,1024]{1,0:T(8,128)(2,1)S(1)}, u32[]{:S(2)}, u32[]{:S(2)}) %collective-permute-start.20) | collective-permute-done | bytes 98336 | tf_op jit(solution)/shard_map/ppermute | solution.py:507
  83.1 4.3 %collective-permute-start.24 = (bf16[12,2304]{1,0:T(8,128)(2,1)S(1)}, bf16[12,2304]{1,0:T(8,128)(2,1)S(1)}, u32[]{:S(2)}, u32[]{:S(2)}) collective-permute-start(bf16[12,2304]{1,0:T(8,128)(2,1)S(1)} %get-tuple-element.100), channel_id=1, source_target_pairs={{0,12},{1,13},{4,8},{5,9},{8,4},{9,5},{12,0},{13,1},{16,28},{17,29... | collective-permute-start | bytes 165896 | tf_op jit(solution)/shard_map/ppermute | solution.py:538
  88.2 2.5 %collective-permute-done.24.c_ref = bf16[12,2304]{1,0:T(8,128)(2,1)S(1)} collective-permute-done((bf16[12,2304]{1,0:T(8,128)(2,1)S(1)}, bf16[12,2304]{1,0:T(8,128)(2,1)S(1)}, u32[]{:S(2)}, u32[]{:S(2)}) %collective-permute-start.24) | collective-permute-done | bytes 55328 | tf_op jit(solution)/shard_map/ppermute | solution.py:538
  90.8 3.7 %collective-permute-start.25 = (bf16[6,2304]{1,0:T(8,128)(2,1)S(1)}, bf16[6,2304]{1,0:T(8,128)(2,1)S(1)}, u32[]{:S(2)}, u32[]{:S(2)}) collective-permute-start(bf16[6,2304]{1,0:T(8,128)(2,1)S(1)} %get-tuple-element.102), channel_id=1, source_target_pairs={{0,16},{1,17},{4,20},{5,21},{8,24},{9,25},{12,28},{13,29},{16,0},{... | collective-permute-start | bytes 82952 | tf_op jit(solution)/shard_map/ppermute | solution.py:544
  94.6 4.2 %collective-permute-done.25.got_ref = bf16[6,2304]{1,0:T(8,128)(2,1)S(1)} collective-permute-done((bf16[6,2304]{1,0:T(8,128)(2,1)S(1)}, bf16[6,2304]{1,0:T(8,128)(2,1)S(1)}, u32[]{:S(2)}, u32[]{:S(2)}) %collective-permute-start.25) | collective-permute-done | bytes 27680 | tf_op jit(solution)/shard_map/ppermute | solution.py:544
  (66 shorter events, 18.8 us)
Async XLA Ops:
  1.8 7.7 %collective-permute-start = (bf16[64,1536]{1,0:T(8,128)(2,1)S(1)}, bf16[64,1536]{1,0:T(8,128)(2,1)S(1)}, u32[]{:S(2)}, u32[]{:S(2)}) collective-permute-start(bf16[64,1536]{1,0:T(8,128)(2,1)S(1)} %get-tuple-element.104), channel_id=1, source_target_pairs={{31,0},{0,1},{1,2},{2,3},{3,4},{4,5},{5,6},{6,7},{7,8},{8,9},{9,10... | collective-permute-start | bytes 589832 | tf_op jit(solution)/shard_map/ppermute | solution.py:489
  10.8 21.1 %collective-permute-start.4 = (bf16[768,640]{1,0:T(8,128)(2,1)S(1)}, bf16[768,640]{1,0:T(8,128)(2,1)S(1)}, u32[]{:S(2)}, u32[]{:S(2)}) collective-permute-start(bf16[768,640]{1,0:T(8,128)(2,1)S(1)} %get-tuple-element.70), channel_id=1, source_target_pairs={{0,1},{1,0},{4,5},{5,4},{8,9},{9,8},{12,13},{13,12},{16,17},{17,16... | collective-permute-start | bytes 2949128 | tf_op jit(solution)/shard_map/ppermute | solution.py:494
  26.9 10.8 %collective-permute-start.5 = (bf16[640,768]{1,0:T(8,128)(2,1)S(1)}, bf16[640,768]{1,0:T(8,128)(2,1)S(1)}, u32[]{:S(2)}, u32[]{:S(2)}) collective-permute-start(bf16[640,768]{1,0:T(8,128)(2,1)S(1)} %get-tuple-element.65.refs_1_.refs_0_.b_ref), channel_id=1, source_target_pairs={{0,1},{1,0},{4,5},{5,4},{8,9},{9,8},{12,13},{13,12},{16,17},{17,16... | collective-permute-start | bytes 2949128 | tf_op jit(solution)/shard_map/ppermute | solution.py:504
  26.9 10.8 %collective-permute-start.7 = (bf16[640,768]{1,0:T(8,128)(2,1)S(1)}, bf16[640,768]{1,0:T(8,128)(2,1)S(1)}, u32[]{:S(2)}, u32[]{:S(2)}) collective-permute-start(bf16[640,768]{1,0:T(8,128)(2,1)S(1)} %get-tuple-element.64.refs_0_.a_ref), channel_id=1, source_target_pairs={{0,1},{1,0},{4,5},{5,4},{8,9},{9,8},{12,13},{13,12},{16,17},{17,16... | collective-permute-start | bytes 2949128 | tf_op jit(solution)/shard_map/ppermute | solution.py:504
  31.4 14.3 %collective-permute-start.6 = (bf16[640,768]{1,0:T(8,128)(2,1)S(1)}, bf16[640,768]{1,0:T(8,128)(2,1)S(1)}, u32[]{:S(2)}, u32[]{:S(2)}) collective-permute-start(bf16[640,768]{1,0:T(8,128)(2,1)S(1)} %get-tuple-element.66.refs_1_.c_ref), channel_id=1, source_target_pairs={{0,1},{1,0},{4,5},{5,4},{8,9},{9,8},{12,13},{13,12},{16,17},{17,16... | collective-permute-start | bytes 2949128 | tf_op jit(solution)/shard_map/ppermute | solution.py:504
  31.4 14.3 %collective-permute-start.2 = (bf16[64,1536]{1,0:T(8,128)(2,1)S(1)}, bf16[64,1536]{1,0:T(8,128)(2,1)S(1)}, u32[]{:S(2)}, u32[]{:S(2)}) collective-permute-start(bf16[64,1536]{1,0:T(8,128)(2,1)S(1)} %get-tuple-element.67), channel_id=1, source_target_pairs={{31,0},{0,1},{1,2},{2,3},{3,4},{4,5},{5,6},{6,7},{7,8},{8,9},{9,10... | collective-permute-start | bytes 589832 | tf_op jit(solution)/shard_map/ppermute | solution.py:529
  31.9 13.8 %collective-permute-start.3 = (bf16[64,1536]{1,0:T(8,128)(2,1)S(1)}, bf16[64,1536]{1,0:T(8,128)(2,1)S(1)}, u32[]{:S(2)}, u32[]{:S(2)}) collective-permute-start(bf16[64,1536]{1,0:T(8,128)(2,1)S(1)} %get-tuple-element.68.refs_4_), channel_id=1, source_target_pairs={{1,0},{2,1},{3,2},{4,3},{5,4},{6,5},{7,6},{8,7},{9,8},{10,9},{11,1... | collective-permute-start | bytes 589832 | tf_op jit(solution)/shard_map/ppermute | solution.py:528
  40.9 16.3 %collective-permute-start.8 = (bf16[192,1280]{1,0:T(8,128)(2,1)S(1)}, bf16[192,1280]{1,0:T(8,128)(2,1)S(1)}, u32[]{:S(2)}, u32[]{:S(2)}) collective-permute-start(bf16[192,1280]{1,0:T(8,128)(2,1)S(1)} %get-tuple-element.74), channel_id=1, source_target_pairs={{0,2},{1,3},{4,6},{5,7},{8,10},{9,11},{12,14},{13,15},{16,18},{17,... | collective-permute-start | bytes 1474568 | tf_op jit(solution)/shard_map/ppermute | solution.py:507
  44.7 12.5 %collective-permute-start.9 = (bf16[192,1280]{1,0:T(8,128)(2,1)S(1)}, bf16[192,1280]{1,0:T(8,128)(2,1)S(1)}, u32[]{:S(2)}, u32[]{:S(2)}) collective-permute-start(bf16[192,1280]{1,0:T(8,128)(2,1)S(1)} %get-tuple-element.76), channel_id=1, source_target_pairs={{0,130},{1,131},{4,134},{5,135},{8,138},{9,139},{12,142},{13,143},... | collective-permute-start | bytes 1474568 | tf_op jit(solution)/shard_map/ppermute | solution.py:507
  48.3 12.1 %collective-permute-start.12 = (bf16[192,1024]{1,0:T(8,128)(2,1)S(1)}, bf16[192,1024]{1,0:T(8,128)(2,1)S(1)}, u32[]{:S(2)}, u32[]{:S(2)}) collective-permute-start(bf16[192,1024]{1,0:T(8,128)(2,1)S(1)} %get-tuple-element.82), channel_id=1, source_target_pairs={{0,32},{1,33},{4,36},{5,37},{8,40},{9,41},{12,44},{13,45},{16,48},... | collective-permute-start | bytes 1179656 | tf_op jit(solution)/shard_map/ppermute | solution.py:507
  49.9 10.5 %collective-permute-start.13 = (bf16[192,1024]{1,0:T(8,128)(2,1)S(1)}, bf16[192,1024]{1,0:T(8,128)(2,1)S(1)}, u32[]{:S(2)}, u32[]{:S(2)}) collective-permute-start(bf16[192,1024]{1,0:T(8,128)(2,1)S(1)} %get-tuple-element.84), channel_id=1, source_target_pairs={{0,96},{1,97},{4,100},{5,101},{8,104},{9,105},{12,108},{13,109},{1... | collective-permute-start | bytes 1179656 | tf_op jit(solution)/shard_map/ppermute | solution.py:507
  57.4 6.6 %collective-permute-start.10 = (bf16[96,1280]{1,0:T(8,128)(2,1)S(1)}, bf16[96,1280]{1,0:T(8,128)(2,1)S(1)}, u32[]{:S(2)}, u32[]{:S(2)}) collective-permute-start(bf16[96,1280]{1,0:T(8,128)(2,1)S(1)} %get-tuple-element.79), channel_id=1, source_target_pairs={{0,130},{1,131},{4,134},{5,135},{8,138},{9,139},{12,142},{13,143},... | collective-permute-start | bytes 737288 | tf_op jit(solution)/shard_map/ppermute | solution.py:507
  58.6 6.9 %collective-permute-start.11 = (bf16[96,1280]{1,0:T(8,128)(2,1)S(1)}, bf16[96,1280]{1,0:T(8,128)(2,1)S(1)}, u32[]{:S(2)}, u32[]{:S(2)}) collective-permute-start(bf16[96,1280]{1,0:T(8,128)(2,1)S(1)} %get-tuple-element.81), channel_id=1, source_target_pairs={{0,2},{1,3},{4,6},{5,7},{8,10},{9,11},{12,14},{13,15},{16,18},{17,... | collective-permute-start | bytes 737288 | tf_op jit(solution)/shard_map/ppermute | solution.py:507
  60.5 7.0 %collective-permute-start.17 = (bf16[96,1024]{1,0:T(8,128)(2,1)S(1)}, bf16[96,1024]{1,0:T(8,128)(2,1)S(1)}, u32[]{:S(2)}, u32[]{:S(2)}) collective-permute-start(bf16[96,1024]{1,0:T(8,128)(2,1)S(1)} %get-tuple-element.90), channel_id=1, source_target_pairs={{0,96},{1,97},{4,100},{5,101},{8,104},{9,105},{12,108},{13,109},{1... | collective-permute-start | bytes 589832 | tf_op jit(solution)/shard_map/ppermute | solution.py:507
  62.7 5.9 %collective-permute-start.18 = (bf16[96,1024]{1,0:T(8,128)(2,1)S(1)}, bf16[96,1024]{1,0:T(8,128)(2,1)S(1)}, u32[]{:S(2)}, u32[]{:S(2)}) collective-permute-start(bf16[96,1024]{1,0:T(8,128)(2,1)S(1)} %get-tuple-element.92), channel_id=1, source_target_pairs={{0,32},{1,33},{4,36},{5,37},{8,40},{9,41},{12,44},{13,45},{16,48},... | collective-permute-start | bytes 589832 | tf_op jit(solution)/shard_map/ppermute | solution.py:507
  68.7 8.4 %collective-permute-start.19 = (bf16[48,1024]{1,0:T(8,128)(2,1)S(1)}, bf16[48,1024]{1,0:T(8,128)(2,1)S(1)}, u32[]{:S(2)}, u32[]{:S(2)}) collective-permute-start(bf16[48,1024]{1,0:T(8,128)(2,1)S(1)} %get-tuple-element.94), channel_id=1, source_target_pairs={{0,2},{1,3},{4,6},{5,7},{8,10},{9,11},{12,14},{13,15},{16,18},{17,... | collective-permute-start | bytes 294920 | tf_op jit(solution)/shard_map/ppermute | solution.py:507
  71.5 11.2 %collective-permute-start.14 = (bf16[48,1280]{1,0:T(8,128)(2,1)S(1)}, bf16[48,1280]{1,0:T(8,128)(2,1)S(1)}, u32[]{:S(2)}, u32[]{:S(2)}) collective-permute-start(bf16[48,1280]{1,0:T(8,128)(2,1)S(1)} %get-tuple-element.87), channel_id=1, source_target_pairs={{0,32},{1,33},{4,36},{5,37},{8,40},{9,41},{12,44},{13,45},{16,48},... | collective-permute-start | bytes 368648 | tf_op jit(solution)/shard_map/ppermute | solution.py:507
  71.6 11.2 %collective-permute-start.15 = (bf16[48,1280]{1,0:T(8,128)(2,1)S(1)}, bf16[48,1280]{1,0:T(8,128)(2,1)S(1)}, u32[]{:S(2)}, u32[]{:S(2)}) collective-permute-start(bf16[48,1280]{1,0:T(8,128)(2,1)S(1)} %get-tuple-element.88), channel_id=1, source_target_pairs={{0,64},{1,65},{4,68},{5,69},{8,72},{9,73},{12,76},{13,77},{16,80},... | collective-permute-start | bytes 368648 | tf_op jit(solution)/shard_map/ppermute | solution.py:507
  73.5 9.3 %collective-permute-start.16 = (bf16[48,1280]{1,0:T(8,128)(2,1)S(1)}, bf16[48,1280]{1,0:T(8,128)(2,1)S(1)}, u32[]{:S(2)}, u32[]{:S(2)}) collective-permute-start(bf16[48,1280]{1,0:T(8,128)(2,1)S(1)} %get-tuple-element.89), channel_id=1, source_target_pairs={{0,96},{1,97},{4,100},{5,101},{8,104},{9,105},{12,108},{13,109},{1... | collective-permute-start | bytes 368648 | tf_op jit(solution)/shard_map/ppermute | solution.py:507
  76.2 6.2 %collective-permute-start.20 = (bf16[48,1024]{1,0:T(8,128)(2,1)S(1)}, bf16[48,1024]{1,0:T(8,128)(2,1)S(1)}, u32[]{:S(2)}, u32[]{:S(2)}) collective-permute-start(bf16[48,1024]{1,0:T(8,128)(2,1)S(1)} %get-tuple-element.95), channel_id=1, source_target_pairs={{0,128},{1,129},{4,132},{5,133},{8,136},{9,137},{12,140},{13,141},... | collective-permute-start | bytes 294920 | tf_op jit(solution)/shard_map/ppermute | solution.py:507
  77.1 5.7 %collective-permute-start.21 = (bf16[48,1024]{1,0:T(8,128)(2,1)S(1)}, bf16[48,1024]{1,0:T(8,128)(2,1)S(1)}, u32[]{:S(2)}, u32[]{:S(2)}) collective-permute-start(bf16[48,1024]{1,0:T(8,128)(2,1)S(1)} %get-tuple-element.96), channel_id=1, source_target_pairs={{0,130},{1,131},{4,134},{5,135},{8,138},{9,139},{12,142},{13,143},... | collective-permute-start | bytes 294920 | tf_op jit(solution)/shard_map/ppermute | solution.py:507
  82.9 5.3 %collective-permute-start.22 = (bf16[12,2304]{1,0:T(8,128)(2,1)S(1)}, bf16[12,2304]{1,0:T(8,128)(2,1)S(1)}, u32[]{:S(2)}, u32[]{:S(2)}) collective-permute-start(bf16[12,2304]{1,0:T(8,128)(2,1)S(1)} %get-tuple-element.98), channel_id=1, source_target_pairs={{0,8},{1,9},{4,12},{5,13},{8,0},{9,1},{12,4},{13,5},{16,24},{17,25... | collective-permute-start | bytes 165896 | tf_op jit(solution)/shard_map/ppermute | solution.py:538
  83.1 7.7 %collective-permute-start.24 = (bf16[12,2304]{1,0:T(8,128)(2,1)S(1)}, bf16[12,2304]{1,0:T(8,128)(2,1)S(1)}, u32[]{:S(2)}, u32[]{:S(2)}) collective-permute-start(bf16[12,2304]{1,0:T(8,128)(2,1)S(1)} %get-tuple-element.100), channel_id=1, source_target_pairs={{0,12},{1,13},{4,8},{5,9},{8,4},{9,5},{12,0},{13,1},{16,28},{17,29... | collective-permute-start | bytes 165896 | tf_op jit(solution)/shard_map/ppermute | solution.py:538
  90.8 8.0 %collective-permute-start.25 = (bf16[6,2304]{1,0:T(8,128)(2,1)S(1)}, bf16[6,2304]{1,0:T(8,128)(2,1)S(1)}, u32[]{:S(2)}, u32[]{:S(2)}) collective-permute-start(bf16[6,2304]{1,0:T(8,128)(2,1)S(1)} %get-tuple-element.102), channel_id=1, source_target_pairs={{0,16},{1,17},{4,20},{5,21},{8,24},{9,25},{12,28},{13,29},{16,0},{... | collective-permute-start | bytes 82952 | tf_op jit(solution)/shard_map/ppermute | solution.py:544
  (10 other events, 30.9 us)

commit v2 on v1

--- a/solution.py
+++ b/solution.py
@@ -56,6 +56,12 @@
 ACROSS_Z = {m: route(lambda x, y, z, c, m=m: (x, y, z ^ m, c)) for m in (1, 2, 3, 4)}
 
 
+def own_place():
+    dp, loop = lax.axis_index("dp"), lax.axis_index("loop")
+    half = lax.shift_right_logical
+    return dp & 3, (half(dp, 2) << 1) + (half(loop, 1) & 1), half(loop, 2), loop & 1
+
+
 def along_loop(distance):
     return [((i - distance) % 32, i) for i in range(32)]
 
@@ -93,9 +99,9 @@
     return pl.CostEstimate(flops=microseconds * 1_000_000_000, bytes_accessed=1000, transcendentals=0)
 
 
-def mask_kernel(incidence_ref, reach_ref, place_ref, types_ref, _, out_ref):
+def mask_kernel(incidence_ref, reach_ref, types_ref, out_ref):
     seq_len = types_ref.shape[1]
-    start = place_ref[4] * ROWS
+    start = lax.axis_index("loop") * ROWS
     ahead = pl.multiple_of(lax.rem(start + seq_len - 2 * HALO, seq_len), 2 * HALO)
     behind = pl.multiple_of(lax.rem(start + ROWS, seq_len), 2 * HALO)
     before = types_ref[:, pl.ds(ahead, 2 * HALO)]
@@ -115,59 +121,49 @@
         out_ref[t * WIN : (t + 1) * WIN, :] = jnp.where(allowed, 1.0, 0.0)
 
 
-def make_mask(types, place, incidence, reach, after):
+def make_mask(types, incidence, reach):
     return call(
         mask_kernel,
         shape(TILES * WIN, 2 * TILE, F32),
         incidence.T,
         reach,
-        place,
         types,
-        after,
         estimate=cost(2),
-        in_specs=[scalars(), scalars(), scalars(), whole(), anywhere()],
+        in_specs=[scalars(), scalars(), whole()],
         out_specs=whole(),
     )
 
 
 def projection_kernel(own_ref, left_ref, right_ref, w_ref, _, out_ref, rows):
-    @pl.when(pl.program_id(0) == 0)
-    def _():
-        rows[:ROWS] = own_ref[...]
-        rows[ROWS : ROWS + HALO] = left_ref[...]
-        rows[ROWS + HALO :] = right_ref[...]
-
-    out_ref[...] = dot(rows[...], w_ref[...], NN).astype(BF16)
+    rows[:ROWS] = own_ref[...]
+    rows[ROWS : ROWS + HALO] = left_ref[...]
+    rows[ROWS + HALO :] = right_ref[...]
+    for n in range(3):
+        cols = slice(n * HW, (n + 1) * HW)
+        out_ref[:, cols] = dot(rows[...], w_ref[:, cols], NN).astype(BF16)
 
 
 def projection(own, left, right, weights, after):
-    cols = weights.shape[1]
     return call(
         projection_kernel,
-        shape(EXT, cols, BF16),
+        shape(EXT, weights.shape[1], BF16),
         own,
         left,
         right,
         weights,
         after,
         vmem=32,
-        grid=(3,),
-        in_specs=[
-            pl.BlockSpec((ROWS, D), lambda i: (0, 0)),
-            pl.BlockSpec((HALO, D), lambda i: (0, 0)),
-            pl.BlockSpec((HALO, D), lambda i: (0, 0)),
-            pl.BlockSpec((D, HW), lambda i: (0, i)),
-            anywhere(),
-        ],
-        out_specs=pl.BlockSpec((EXT, HW), lambda i: (0, i)),
+        in_specs=[whole()] * 4 + [anywhere()],
+        out_specs=whole(),
         scratch_shapes=[pltpu.VMEM((EXT, D), BF16)],
     )
 
 
-def reorder_kernel(n_carried, place_ref, rows, *refs):
+def reorder_kernel(at, n_carried, rows, *refs):
     same_ref, other_ref, mark_ref = refs[n_carried:]
+    tokens = slice(at, at + rows.shape[0])
     mark_ref[...] = jnp.zeros_like(mark_ref)
-    x, y, z, core = place_ref[0], place_ref[1], place_ref[2], place_ref[3]
+    x, y, z, core = own_place()
     block = D // 4
     half = block // 2
     place = lax.broadcasted_iota(jnp.int32, (block, block), 0)
@@ -186,37 +182,34 @@
     piece = half // 4
     for a in range(2):
         for b in range(2):
-            at = (lax.shift_right_logical(y, 1) ^ a) * 2 + (lax.shift_right_logical(x, 1) ^ b)
-            cols = rows[:, pl.ds(pl.multiple_of(at * block, 128), block)]
+            n = (lax.shift_right_logical(y, 1) ^ a) * 2 + (lax.shift_right_logical(x, 1) ^ b)
+            cols = rows[:, pl.ds(pl.multiple_of(n * block, 128), block)]
             got = dot(pick, cols, NT).astype(BF16)
             for c, ref in enumerate((same_ref, other_ref)):
                 for low in range(4):
                     jy, jx = 2 * a + low // 2, 2 * b + low % 2
-                    ref[jy * half + jx * piece : jy * half + (jx + 1) * piece] = got[
+                    ref[jy * half + jx * piece : jy * half + (jx + 1) * piece, tokens] = got[
                         c * half + low * piece : c * half + (low + 1) * piece
                     ]
 
 
-def reorder(place, rows, at, carried, after):
-    n_rows = rows.shape[0]
-    out_spec = pl.BlockSpec((HALF, n_rows), lambda i: (0, at // n_rows))
+def reorder(rows, at, carried, after):
     extra = list(carried) + list(after)
     return call(
-        functools.partial(reorder_kernel, len(extra)),
+        functools.partial(reorder_kernel, at, len(extra)),
         (shape(HALF, EXT, BF16),) * 2 + (shape(8, 128, F32),),
-        place,
         rows,
         *extra,
-        estimate=cost(4),
-        grid=(1,),
-        in_specs=[scalars(), pl.BlockSpec((n_rows, D), lambda i: (0, 0))] + [anywhere()] * len(extra),
-        out_specs=(out_spec,) * 2 + (whole(),),
-        input_output_aliases={2 + i: i for i in range(len(carried))},
+        estimate=cost(1),
+        in_specs=[whole()] * (1 + len(carried)) + [anywhere()] * len(after),
+        out_specs=(whole(),) * 3,
+        input_output_aliases={1 + i: i for i in range(len(carried))},
     )
 
 
 def attention_kernel(n_carried, q_ref, k_ref, v_ref, go_ref, mask_ref, *refs):
-    att_ref, left_ref, right_ref, grad_ref, ke, ve, dk, dv = refs[n_carried:]
+    att_ref, rim_ref, grad_ref, ke, ve, dk, dv = refs[n_carried:]
+    edge = pl.ds(pl.multiple_of(own_place()[3] * (HALO + ROWS), HALO), HALO)
     for src, dst in ((k_ref, ke), (v_ref, ve)):
         dst[:HALO] = src[ROWS : ROWS + HALO]
         dst[HALO : HALO + ROWS] = src[:ROWS]
@@ -263,29 +256,27 @@
     for part, acc, factor in ((1, dk, HD**-0.5), (2, dv, 1.0)):
         cols = slice(part * GW, (part + 1) * GW)
         rim_cols = slice((part - 1) * GW, part * GW)
-        left = (acc[:HALO] * factor).astype(BF16)
-        right = (acc[HALO + ROWS :] * factor).astype(BF16)
         grad_ref[:ROWS, cols] = (acc[HALO : HALO + ROWS] * factor).astype(BF16)
-        grad_ref[ROWS : ROWS + HALO, cols] = left
-        grad_ref[ROWS + HALO :, cols] = right
-        left_ref[:, rim_cols] = left
-        right_ref[:, rim_cols] = right
-
-
-def attention(group, proj, grad_out, mask, carried, after):
+        grad_ref[ROWS : ROWS + HALO, cols] = (acc[:HALO] * factor).astype(BF16)
+        grad_ref[ROWS + HALO :, cols] = (acc[HALO + ROWS :] * factor).astype(BF16)
+        rim_ref[:, rim_cols] = (acc[edge] * factor).astype(BF16)
+
+
+def attention(group, proj, grad_out, mask, carried):
     def cols(rows, block, width=GW):
         return pl.BlockSpec((rows, width), lambda i: (0, block))
 
-    extra = list(carried) + list(after)
-    return call(
-        functools.partial(attention_kernel, len(extra)),
-        (shape(ROWS, HW, BF16), shape(HALO, 2 * HW, BF16), shape(HALO, 2 * HW, BF16), shape(EXT, 3 * GW, BF16)),
+    last = group == GROUPS - 1
+    n_cols = 3 * GW if last else 3 * GW * (GROUPS - 1)
+    return call(
+        functools.partial(attention_kernel, len(carried)),
+        (shape(ROWS, HW, BF16), shape(HALO, 2 * HW, BF16), shape(EXT, n_cols, BF16)),
         proj,
         proj,
         proj,
         grad_out,
         mask,
-        *extra,
+        *carried,
         vmem=20,
         grid=(1,),
         in_specs=[
@@ -295,13 +286,8 @@
             cols(ROWS, group),
             pl.BlockSpec((TILES * WIN, 2 * TILE), lambda i: (0, 0)),
         ]
-        + [anywhere()] * len(extra),
-        out_specs=(
-            cols(ROWS, group),
-            cols(HALO, group, 2 * GW),
-            cols(HALO, group, 2 * GW),
-            pl.BlockSpec((EXT, 3 * GW), lambda i: (0, 0)),
-        ),
+        + [anywhere()] * len(carried),
+        out_specs=(cols(ROWS, group), cols(HALO, group, 2 * GW), cols(EXT, 0 if last else group, 3 * GW)),
         scratch_shapes=[
             pltpu.VMEM((EXT, GW), BF16),
             pltpu.VMEM((EXT, GW), BF16),
@@ -442,41 +428,54 @@
     )
 
 
-def token_kernel(a_ref, b_ref, c_ref, left_ref, right_ref, w_ref, _, out_ref, mark_ref, grad):
+def token_kernel(a_ref, b_ref, c_ref, ao_ref, bo_ref, co_ref, rim_ref, w_ref, _, out_ref, mark_ref, grad):
     @pl.when(pl.program_id(0) == 0)
     def _():
-        for g, ref in enumerate((a_ref, b_ref, c_ref)):
+        core = own_place()[3]
+        first = core == 0
+        near = pl.ds(pl.multiple_of(ROWS + core * HALO, HALO), HALO)
+        for g, (ref, other) in enumerate(((a_ref, ao_ref), (b_ref, bo_ref), (c_ref, co_ref))):
             for k in range(3):
                 cols = slice(k * HW + g * GW, k * HW + (g + 1) * GW)
                 own = slice(k * GW, (k + 1) * GW)
                 if k == 0:
                     grad[:, cols] = ref[:ROWS, own]
                     continue
-                rim = slice((2 * g + k - 1) * GW, (2 * g + k) * GW)
-                for edge, got in ((slice(0, HALO), left_ref), (slice(ROWS - HALO, ROWS), right_ref)):
-                    grad[edge, cols] = (ref[edge, own].astype(F32) + got[:, rim].astype(F32)).astype(BF16)
+                far = rim_ref[:, (2 * g + k - 1) * GW : (2 * g + k) * GW].astype(F32)
+                close = other[near, own].astype(F32)
+                for edge, got in (
+                    (slice(0, HALO), jnp.where(first, far, close)),
+                    (slice(ROWS - HALO, ROWS), jnp.where(first, close, far)),
+                ):
+                    grad[edge, cols] = (ref[edge, own].astype(F32) + got).astype(BF16)
                 grad[HALO : ROWS - HALO, cols] = ref[HALO : ROWS - HALO, own]
 
     out_ref[...] = dot(grad[...], w_ref[...], NT).astype(BF16)
     mark_ref[...] = jnp.zeros_like(mark_ref)
 
 
-def token_gradient(grads, from_left, from_right, weights, after):
+def token_gradient(grads, others, rim, weights, after):
     block = 512
     cols = weights.shape[1]
-    grad_spec = pl.BlockSpec((EXT, 3 * GW), lambda i: (0, 0))
+    grad_specs = [pl.BlockSpec((EXT, 3 * GW), lambda i, n=n: (0, n)) for n in (0, 1, 0)]
     rim_spec = pl.BlockSpec((HALO, 2 * HW), lambda i: (0, 0))
+    pair, last = grads
+    pair_other, last_other = others
     return call(
         token_kernel,
         (shape(ROWS, D, BF16), shape(8, 128, F32)),
-        *grads,
-        from_left,
-        from_right,
+        pair,
+        pair,
+        last,
+        pair_other,
+        pair_other,
+        last_other,
+        rim,
         weights,
         after,
-        vmem=24,
+        vmem=40,
         grid=(D // block,),
-        in_specs=[grad_spec] * 3 + [rim_spec] * 2 + [pl.BlockSpec((block, cols), lambda i: (i, 0)), anywhere()],
+        in_specs=grad_specs * 2 + [rim_spec, pl.BlockSpec((block, cols), lambda i: (i, 0)), anywhere()],
         out_specs=(pl.BlockSpec((ROWS, block), lambda i: (0, i)), pl.BlockSpec((8, 128), lambda i: (0, 0))),
         scratch_shapes=[pltpu.VMEM((ROWS, cols), BF16)],
     )
@@ -484,24 +483,23 @@
 
 def body(tokens, weights, cotangent, token_types, incidence, window_reach):
     own = tokens[0]
-    dp, loop = lax.axis_index("dp"), lax.axis_index("loop")
-    place = jnp.stack([dp % 4, dp // 4 * 2 + loop // 2 % 2, loop // 4, loop % 2, loop]).astype(jnp.int32)
     left = lax.ppermute(own[ROWS - HALO :], "loop", along_loop(1))
     right = lax.ppermute(own[:HALO], "loop", along_loop(-1))
-    *arranged, mark = reorder(place, own, 0, (), ())
-    mask = make_mask(token_types, place, incidence[0], window_reach[0], mark)
-    x_own, x_send, mark = reorder(place, jnp.concatenate([left, right], axis=0), ROWS, arranged, (mask,))
+    mask = make_mask(token_types, incidence[0], window_reach[0])
+    *arranged, mark = reorder(own, 0, (), (mask,))
+    x_own, x_send, mark = reorder(jnp.concatenate([left, right], axis=0), ROWS, arranged, (mark,))
     x_other = lax.ppermute(x_send, AXES, TO_CORE)
     proj = projection(own, left, right, weights, mark)
 
-    blocks = [(g, k) for g in range(GROUPS) for k in range(3)]
-    carried, grads, others = (), [], []
-
-    def attend(group, after):
-        nonlocal carried
-        *carried, grad = attention(group, proj, cotangent[0], mask, carried, after)
-        grads.append(grad)
-        others.append(lax.ppermute(grad, AXES, TO_CORE))
+    blocks = [(0, n) for n in range(3 * GROUPS - 3)] + [(1, n) for n in range(3)]
+    attended, rim, pair = attention(0, proj, cotangent[0], mask, ())
+    attended, rim, pair = attention(1, proj, cotangent[0], mask, (attended, rim, pair))
+    pair_other = lax.ppermute(pair, AXES, TO_CORE)
+    attended, rim, last = attention(2, proj, cotangent[0], mask, (attended, rim))
+    attended_mark = rim
+    last_other = lax.ppermute(last, AXES, TO_CORE)
+    rim = lax.ppermute(rim, "loop", [(i, (i - 1 + i % 2 * 2) % 32) for i in range(32)])
+    grads, others = (pair, last), (pair_other, last_other)
 
     def swap(n, way, part):
         return lax.ppermute(part, AXES, (ACROSS_Y if way == "y" else ACROSS_X)[n - 1])
@@ -521,15 +519,9 @@
         keep, *sent = split_sum(*state, after)
         return [keep, *(swap(n + 1, way, part) for n, part in enumerate(sent))]
 
-    attend(0, ())
-    attend(1, ())
-    attend(2, ())
-    attended, rim_left, rim_right = carried
-    from_right = lax.ppermute(rim_left, "loop", along_loop(-1))
-    from_left = lax.ppermute(rim_right, "loop", along_loop(1))
-    by_y = round_one("y", blocks[:5], (rim_left,))
-    by_x = round_one("x", blocks[5:], (by_y[0], from_left, from_right))
-    token_grad, mark = token_gradient(grads, from_left, from_right, weights, by_x[0])
+    by_y = round_one("y", blocks[:5], (attended_mark,))
+    by_x = round_one("x", blocks[5:], (by_y[0], rim))
+    token_grad, mark = token_gradient(grads, others, rim, weights, by_x[0])
     by_y = round_two("y", by_y, (mark,))
     by_x = round_two("x", by_x, (by_y[0],))
     by_y = round_three("x", by_y, (by_x[0],))

time: 100 us -> 95.3 us (0.953)
  Pallas kernels: 33.9 us -> 31.8 us
  waiting for transfers between devices: 21.3 us -> 19.4 us
  local copies, waits for them, and re-layouts: 4.74 us -> 3.71 us
    pallas_call x17, Pallas kernels: 33.9 us -> 31.8 us  [call(): pl.pallas_call(kernel, out_shape=out_shape, cost_estimate=estimate or TIN...]
    unnamed x17 -> x13, local copies, waits for them, and re-layouts: 3.6 us -> 2.66 us
    ppermute x5 -> x3, starting transfers between devices: 6.84 us -> 6.35 us  [the longest x1 6.3 us: body(): lax.ppermute(rim, 'loop', [(i, (i - 1 + i % 2 * 2) % 32) for i in range(3...]
  transfers between devices with their start and end apart: 26 -> 24, of which waited for: 10 -> 10; matrix products, arithmetic and copies ran while one was open for 0% -> 1% of each run, Pallas kernels for 32% -> 19%
where the time goes in v2:
time: 95.3 us; the launch traced here: 94.6 us
  starting transfers between devices  39 us (41%)
  Pallas kernels  31.8 us (33%)
  waiting for transfers between devices  19.4 us (20%)
  local copies, waits for them, and re-layouts  3.71 us (4%)
    pallas_call x17, Pallas kernels, call(): pl.pallas_call(kernel, out_shape=out_shape, cost_estimate=estimate or TIN...  31.8 us
    ppermute x14, starting transfers between devices, swap(): lax.ppermute(part, AXES, (ACROSS_Y if way == 'y' else ACROSS_X)[n - 1])  22.8 us
    ppermute x14, waiting for transfers between devices, swap(): lax.ppermute(part, AXES, (ACROSS_Y if way == 'y' else ACROSS_X)[n - 1])  9.99 us
    ppermute x1, starting transfers between devices, body(): lax.ppermute(rim, 'loop', [(i, (i - 1 + i % 2 * 2) % 32) for i in range(3...  6.3 us
    ppermute x3, starting transfers between devices, body(): lax.ppermute(part, AXES, ACROSS_Z[m])  4.47 us
    ppermute x1, starting transfers between devices, body(): lax.ppermute(send, AXES, ACROSS_Z[4])  4.28 us
    ppermute x1, waiting for transfers between devices, body(): lax.ppermute(send, AXES, ACROSS_Z[4])  3.67 us
    ppermute x3, waiting for transfers between devices, body(): lax.ppermute(part, AXES, ACROSS_Z[m])  3.12 us
  transfers between devices with their start and end apart: 24, of which 10 were waited for; matrix products, arithmetic and copies ran while one was open for 1% of the time, Pallas kernels for 19%

profile of v2, /device:TPU:8, one launch (start us, length us, event | category | flops | bytes accessed | tf_op | source)
XLA Modules:
  0.0 94.6 jit_solution(15661415360572480847)
XLA Ops:
  7.0 2.6 %collective-permute-done.left_ref = bf16[64,1536]{1,0:T(8,128)(2,1)S(1)} collective-permute-done((bf16[64,1536]{1,0:T(8,128)(2,1)S(1)}, bf16[64,1536]{1,0:T(8,128)(2,1)S(1)}, u32[]{:S(2)}, u32[]{:S(2)}) %collective-permute-start) | collective-permute-done | bytes 196640 | tf_op jit(solution)/shard_map/ppermute | solution.py:486
  10.2 4.7 %shard_map.88.q_ref.k_ref.v_ref = bf16[640,2304]{1,0:T(8,128)(2,1)S(1)} custom-call(bf16[512,1536]{1,0:T(8,128)(2,1)S(1)} %bitcast.20, bf16[64,1536]{1,0:T(8,128)(2,1)S(1)} %collective-permute-done.left_ref, bf16[64,1536]{1,0:T(8,128)(2,1)S(1)} %collective-permute-done.1.right_ref, bf16[1536,2304]{1,0:T(8,128)(2,1)S(1)} %bitcast.15, ...), custom_call_target="tpu_custom_call" | custom-call | flops 1000 | bytes 1000 | tf_op jit(solution)/shard_map/pallas_call | solution.py:70
  14.9 4.0 %shard_map.89 = (bf16[512,768]{1,0:T(8,128)(2,1)}, bf16[64,1536]{1,0:T(8,128)(2,1)S(1)}, bf16[640,1536]{1,0:T(8,128)(2,1)S(1)}) custom-call(bf16[640,2304]{1,0:T(8,128)(2,1)S(1)} %shard_map.88.q_ref.k_ref.v_ref, bf16[640,2304]{1,0:T(8,128)(2,1)S(1)} %shard_map.88.q_ref.k_ref.v_ref, bf16[640,2304]{1,0:T(8,128)(2,1)S(1)} %shard_map.88.q_ref.k_ref.v_ref, ...), custom_call_target="tpu_custom_call" | custom-call | flops 1000 | bytes 1000 | tf_op jit(solution)/shard_map/pallas_call | solution.py:70
  18.9 4.0 %shard_map.90 = (bf16[512,768]{1,0:T(8,128)(2,1)}, bf16[64,1536]{1,0:T(8,128)(2,1)S(1)}, bf16[640,1536]{1,0:T(8,128)(2,1)S(1)}) custom-call(bf16[640,2304]{1,0:T(8,128)(2,1)S(1)} %shard_map.88.q_ref.k_ref.v_ref, bf16[640,2304]{1,0:T(8,128)(2,1)S(1)} %shard_map.88.q_ref.k_ref.v_ref, ...), custom_call_target="tpu_custom_call", output_to_operand_aliasing={{0}: (5, {}), {1}: (6, {}), {2}: (7, {})} | custom-call | flops 1000 | bytes 1000 | tf_op jit(solution)/shard_map/pallas_call | solution.py:70
  23.3 4.0 %shard_map.91 = (bf16[512,768]{1,0:T(8,128)(2,1)}, bf16[64,1536]{1,0:T(8,128)(2,1)S(1)}, bf16[640,768]{1,0:T(8,128)(2,1)S(1)}) custom-call(bf16[640,2304]{1,0:T(8,128)(2,1)S(1)} %shard_map.88.q_ref.k_ref.v_ref, bf16[640,2304]{1,0:T(8,128)(2,1)S(1)} %shard_map.88.q_ref.k_ref.v_ref, ...), custom_call_target="tpu_custom_call", output_to_operand_aliasing={{0}: (5, {}), {1}: (6, {})} | custom-call | flops 1000 | bytes 1000 | tf_op jit(solution)/shard_map/pallas_call | solution.py:70
  27.3 6.3 %collective-permute-start.4 = (bf16[64,1536]{1,0:T(8,128)(2,1)S(1)}, bf16[64,1536]{1,0:T(8,128)(2,1)S(1)}, u32[]{:S(2)}, u32[]{:S(2)}) collective-permute-start(bf16[64,1536]{1,0:T(8,128)(2,1)S(1)} %get-tuple-element.62.refs_2_), channel_id=1, source_target_pairs={{0,31},{1,2},{2,1},{3,4},{4,3},{5,6},{6,5},{7,8},{8,7},{9,10},{10,... | collective-permute-start | bytes 589832 | tf_op jit(solution)/shard_map/ppermute | solution.py:501
  33.6 3.2 %shard_map.92 = (f32[192,1280]{1,0:T(8,128)S(1)}, bf16[192,1280]{1,0:T(8,128)(2,1)S(1)}, f32[192,1280]{1,0:T(8,128)S(1)}, bf16[192,1280]{1,0:T(8,128)(2,1)S(1)}) custom-call(bf16[768,640]{1,0:T(8,128)(2,1)S(1)} %get-tuple-element.63.x_ref, bf16[768,640]{1,0:T(8,128)(2,1)S(1)} %collective-permute-done.5.xp_ref, ...), custom_call_target="tpu_custom_call" | custom-call | flops 1000 | bytes 1000 | tf_op jit(solution)/shard_map/pallas_call | solution.py:70
  36.8 1.9 %collective-permute-start.6 = (bf16[192,1280]{1,0:T(8,128)(2,1)S(1)}, bf16[192,1280]{1,0:T(8,128)(2,1)S(1)}, u32[]{:S(2)}, u32[]{:S(2)}) collective-permute-start(bf16[192,1280]{1,0:T(8,128)(2,1)S(1)} %get-tuple-element.68), channel_id=1, source_target_pairs={{0,2},{1,3},{4,6},{5,7},{8,10},{9,11},{12,14},{13,15},{16,18},{17,... | collective-permute-start | bytes 1474568 | tf_op jit(solution)/shard_map/ppermute | solution.py:505
  39.8 2.6 %shard_map.93 = (f32[192,1024]{1,0:T(8,128)S(1)}, bf16[192,1024]{1,0:T(8,128)(2,1)S(1)}, f32[192,1024]{1,0:T(8,128)S(1)}, bf16[192,1024]{1,0:T(8,128)(2,1)S(1)}) custom-call(bf16[768,640]{1,0:T(8,128)(2,1)S(1)} %get-tuple-element.63.x_ref, bf16[768,640]{1,0:T(8,128)(2,1)S(1)} %collective-permute-done.5.xp_ref, ...), custom_call_target="tpu_custom_call" | custom-call | flops 1000 | bytes 1000 | tf_op jit(solution)/shard_map/pallas_call | solution.py:70
  42.4 1.6 %collective-permute-start.10 = (bf16[192,1024]{1,0:T(8,128)(2,1)S(1)}, bf16[192,1024]{1,0:T(8,128)(2,1)S(1)}, u32[]{:S(2)}, u32[]{:S(2)}) collective-permute-start(bf16[192,1024]{1,0:T(8,128)(2,1)S(1)} %get-tuple-element.76), channel_id=1, source_target_pairs={{0,32},{1,33},{4,36},{5,37},{8,40},{9,41},{12,44},{13,45},{16,48},... | collective-permute-start | bytes 1179656 | tf_op jit(solution)/shard_map/ppermute | solution.py:505
  44.0 2.1 %collective-permute-start.11 = (bf16[192,1024]{1,0:T(8,128)(2,1)S(1)}, bf16[192,1024]{1,0:T(8,128)(2,1)S(1)}, u32[]{:S(2)}, u32[]{:S(2)}) collective-permute-start(bf16[192,1024]{1,0:T(8,128)(2,1)S(1)} %get-tuple-element.78), channel_id=1, source_target_pairs={{0,96},{1,97},{4,100},{5,101},{8,104},{9,105},{12,108},{13,109},{1... | collective-permute-start | bytes 1179656 | tf_op jit(solution)/shard_map/ppermute | solution.py:505
  46.1 5.5 %shard_map.94 = (bf16[512,1536]{1,0:T(8,128)(2,1)}, f32[8,128]{1,0:T(8,128)S(1)}) custom-call(bf16[640,1536]{1,0:T(8,128)(2,1)S(1)} %get-tuple-element.60.refs_0_.a_ref.b_ref, bf16[640,1536]{1,0:T(8,128)(2,1)S(1)} %get-tuple-element.60.refs_0_.a_ref.b_ref, bf16[640,768]{1,0:T(8,128)(2,1)S(1)} %get-tuple-element.61.refs_1_.c_ref, ...), custom_call_target="tpu_custom_call" | custom-call | flops 1000 | bytes 1000 | tf_op jit(solution)/shard_map/pallas_call | solution.py:70
  51.8 2.2 %collective-permute-start.8 = (bf16[96,1280]{1,0:T(8,128)(2,1)S(1)}, bf16[96,1280]{1,0:T(8,128)(2,1)S(1)}, u32[]{:S(2)}, u32[]{:S(2)}) collective-permute-start(bf16[96,1280]{1,0:T(8,128)(2,1)S(1)} %get-tuple-element.73), channel_id=1, source_target_pairs={{0,130},{1,131},{4,134},{5,135},{8,138},{9,139},{12,142},{13,143},... | collective-permute-start | bytes 737288 | tf_op jit(solution)/shard_map/ppermute | solution.py:505
  53.9 1.9 %collective-permute-start.9 = (bf16[96,1280]{1,0:T(8,128)(2,1)S(1)}, bf16[96,1280]{1,0:T(8,128)(2,1)S(1)}, u32[]{:S(2)}, u32[]{:S(2)}) collective-permute-start(bf16[96,1280]{1,0:T(8,128)(2,1)S(1)} %get-tuple-element.75), channel_id=1, source_target_pairs={{0,2},{1,3},{4,6},{5,7},{8,10},{9,11},{12,14},{13,15},{16,18},{17,... | collective-permute-start | bytes 737288 | tf_op jit(solution)/shard_map/ppermute | solution.py:505
  56.0 2.8 %collective-permute-start.15 = (bf16[96,1024]{1,0:T(8,128)(2,1)S(1)}, bf16[96,1024]{1,0:T(8,128)(2,1)S(1)}, u32[]{:S(2)}, u32[]{:S(2)}) collective-permute-start(bf16[96,1024]{1,0:T(8,128)(2,1)S(1)} %get-tuple-element.84), channel_id=1, source_target_pairs={{0,96},{1,97},{4,100},{5,101},{8,104},{9,105},{12,108},{13,109},{1... | collective-permute-start | bytes 589832 | tf_op jit(solution)/shard_map/ppermute | solution.py:505
  63.0 1.5 %collective-permute-done.16.got_b_ref = bf16[96,1024]{1,0:T(8,128)(2,1)S(1)} collective-permute-done((bf16[96,1024]{1,0:T(8,128)(2,1)S(1)}, bf16[96,1024]{1,0:T(8,128)(2,1)S(1)}, u32[]{:S(2)}, u32[]{:S(2)}) %collective-permute-start.16) | collective-permute-done | bytes 196640 | tf_op jit(solution)/shard_map/ppermute | solution.py:505
  66.0 2.7 %collective-permute-start.13 = (bf16[48,1280]{1,0:T(8,128)(2,1)S(1)}, bf16[48,1280]{1,0:T(8,128)(2,1)S(1)}, u32[]{:S(2)}, u32[]{:S(2)}) collective-permute-start(bf16[48,1280]{1,0:T(8,128)(2,1)S(1)} %get-tuple-element.82), channel_id=1, source_target_pairs={{0,64},{1,65},{4,68},{5,69},{8,72},{9,73},{12,76},{13,77},{16,80},... | collective-permute-start | bytes 368648 | tf_op jit(solution)/shard_map/ppermute | solution.py:505
  68.7 2.0 %collective-permute-start.14 = (bf16[48,1280]{1,0:T(8,128)(2,1)S(1)}, bf16[48,1280]{1,0:T(8,128)(2,1)S(1)}, u32[]{:S(2)}, u32[]{:S(2)}) collective-permute-start(bf16[48,1280]{1,0:T(8,128)(2,1)S(1)} %get-tuple-element.83), channel_id=1, source_target_pairs={{0,96},{1,97},{4,100},{5,101},{8,104},{9,105},{12,108},{13,109},{1... | collective-permute-start | bytes 368648 | tf_op jit(solution)/shard_map/ppermute | solution.py:505
  70.7 2.9 %collective-permute-start.18 = (bf16[48,1024]{1,0:T(8,128)(2,1)S(1)}, bf16[48,1024]{1,0:T(8,128)(2,1)S(1)}, u32[]{:S(2)}, u32[]{:S(2)}) collective-permute-start(bf16[48,1024]{1,0:T(8,128)(2,1)S(1)} %get-tuple-element.89), channel_id=1, source_target_pairs={{0,128},{1,129},{4,132},{5,133},{8,136},{9,137},{12,140},{13,141},... | collective-permute-start | bytes 294920 | tf_op jit(solution)/shard_map/ppermute | solution.py:505
  73.6 3.2 %collective-permute-done.18.refs_6_ = bf16[48,1024]{1,0:T(8,128)(2,1)S(1)} collective-permute-done((bf16[48,1024]{1,0:T(8,128)(2,1)S(1)}, bf16[48,1024]{1,0:T(8,128)(2,1)S(1)}, u32[]{:S(2)}, u32[]{:S(2)}) %collective-permute-start.18) | collective-permute-done | bytes 98336 | tf_op jit(solution)/shard_map/ppermute | solution.py:505
  79.3 3.6 %collective-permute-start.22 = (bf16[12,2304]{1,0:T(8,128)(2,1)S(1)}, bf16[12,2304]{1,0:T(8,128)(2,1)S(1)}, u32[]{:S(2)}, u32[]{:S(2)}) collective-permute-start(bf16[12,2304]{1,0:T(8,128)(2,1)S(1)} %get-tuple-element.94), channel_id=1, source_target_pairs={{0,12},{1,13},{4,8},{5,9},{8,4},{9,5},{12,0},{13,1},{16,28},{17,29... | collective-permute-start | bytes 165896 | tf_op jit(solution)/shard_map/ppermute | solution.py:530
  83.7 2.2 %collective-permute-done.22.c_ref = bf16[12,2304]{1,0:T(8,128)(2,1)S(1)} collective-permute-done((bf16[12,2304]{1,0:T(8,128)(2,1)S(1)}, bf16[12,2304]{1,0:T(8,128)(2,1)S(1)}, u32[]{:S(2)}, u32[]{:S(2)}) %collective-permute-start.22) | collective-permute-done | bytes 55328 | tf_op jit(solution)/shard_map/ppermute | solution.py:530
  86.0 4.3 %collective-permute-start.23 = (bf16[6,2304]{1,0:T(8,128)(2,1)S(1)}, bf16[6,2304]{1,0:T(8,128)(2,1)S(1)}, u32[]{:S(2)}, u32[]{:S(2)}) collective-permute-start(bf16[6,2304]{1,0:T(8,128)(2,1)S(1)} %get-tuple-element.96), channel_id=1, source_target_pairs={{0,16},{1,17},{4,20},{5,21},{8,24},{9,25},{12,28},{13,29},{16,0},{... | collective-permute-start | bytes 82952 | tf_op jit(solution)/shard_map/ppermute | solution.py:536
  90.3 3.7 %collective-permute-done.23.got_ref = bf16[6,2304]{1,0:T(8,128)(2,1)S(1)} collective-permute-done((bf16[6,2304]{1,0:T(8,128)(2,1)S(1)}, bf16[6,2304]{1,0:T(8,128)(2,1)S(1)}, u32[]{:S(2)}, u32[]{:S(2)}) %collective-permute-start.23) | collective-permute-done | bytes 27680 | tf_op jit(solution)/shard_map/ppermute | solution.py:536
  (57 shorter events, 18.4 us)
Async XLA Ops:
  1.7 5.3 %collective-permute-start.1 = (bf16[64,1536]{1,0:T(8,128)(2,1)S(1)}, bf16[64,1536]{1,0:T(8,128)(2,1)S(1)}, u32[]{:S(2)}, u32[]{:S(2)}) collective-permute-start(bf16[64,1536]{1,0:T(8,128)(2,1)S(1)} %get-tuple-element.97), channel_id=1, source_target_pairs={{1,0},{2,1},{3,2},{4,3},{5,4},{6,5},{7,6},{8,7},{9,8},{10,9},{11,1... | collective-permute-start | bytes 589832 | tf_op jit(solution)/shard_map/ppermute | solution.py:487
  1.8 7.7 %collective-permute-start = (bf16[64,1536]{1,0:T(8,128)(2,1)S(1)}, bf16[64,1536]{1,0:T(8,128)(2,1)S(1)}, u32[]{:S(2)}, u32[]{:S(2)}) collective-permute-start(bf16[64,1536]{1,0:T(8,128)(2,1)S(1)} %get-tuple-element.98), channel_id=1, source_target_pairs={{31,0},{0,1},{1,2},{2,3},{3,4},{4,5},{5,6},{6,7},{7,8},{8,9},{9,10... | collective-permute-start | bytes 589832 | tf_op jit(solution)/shard_map/ppermute | solution.py:486
  22.8 10.8 %collective-permute-start.2 = (bf16[640,1536]{1,0:T(8,128)(2,1)S(1)}, bf16[640,1536]{1,0:T(8,128)(2,1)S(1)}, u32[]{:S(2)}, u32[]{:S(2)}) collective-permute-start(bf16[640,1536]{1,0:T(8,128)(2,1)S(1)} %get-tuple-element.60.refs_0_.a_ref.b_ref), channel_id=1, source_target_pairs={{0,1},{1,0},{4,5},{5,4},{8,9},{9,8},{12,13},{13,12},{16,17},{17,16... | collective-permute-start | bytes 5898248 | tf_op jit(solution)/shard_map/ppermute | solution.py:497
  22.8 10.8 %collective-permute-start.5 = (bf16[768,640]{1,0:T(8,128)(2,1)S(1)}, bf16[768,640]{1,0:T(8,128)(2,1)S(1)}, u32[]{:S(2)}, u32[]{:S(2)}) collective-permute-start(bf16[768,640]{1,0:T(8,128)(2,1)S(1)} %get-tuple-element.64), channel_id=1, source_target_pairs={{0,1},{1,0},{4,5},{5,4},{8,9},{9,8},{12,13},{13,12},{16,17},{17,16... | collective-permute-start | bytes 2949128 | tf_op jit(solution)/shard_map/ppermute | solution.py:491
  27.3 12.5 %collective-permute-start.3 = (bf16[640,768]{1,0:T(8,128)(2,1)S(1)}, bf16[640,768]{1,0:T(8,128)(2,1)S(1)}, u32[]{:S(2)}, u32[]{:S(2)}) collective-permute-start(bf16[640,768]{1,0:T(8,128)(2,1)S(1)} %get-tuple-element.61.refs_1_.c_ref), channel_id=1, source_target_pairs={{0,1},{1,0},{4,5},{5,4},{8,9},{9,8},{12,13},{13,12},{16,17},{17,16... | collective-permute-start | bytes 2949128 | tf_op jit(solution)/shard_map/ppermute | solution.py:500
  27.3 12.5 %collective-permute-start.4 = (bf16[64,1536]{1,0:T(8,128)(2,1)S(1)}, bf16[64,1536]{1,0:T(8,128)(2,1)S(1)}, u32[]{:S(2)}, u32[]{:S(2)}) collective-permute-start(bf16[64,1536]{1,0:T(8,128)(2,1)S(1)} %get-tuple-element.62.refs_2_), channel_id=1, source_target_pairs={{0,31},{1,2},{2,1},{3,4},{4,3},{5,6},{6,5},{7,8},{8,7},{9,10},{10,... | collective-permute-start | bytes 589832 | tf_op jit(solution)/shard_map/ppermute | solution.py:501
  36.8 14.7 %collective-permute-start.6 = (bf16[192,1280]{1,0:T(8,128)(2,1)S(1)}, bf16[192,1280]{1,0:T(8,128)(2,1)S(1)}, u32[]{:S(2)}, u32[]{:S(2)}) collective-permute-start(bf16[192,1280]{1,0:T(8,128)(2,1)S(1)} %get-tuple-element.68), channel_id=1, source_target_pairs={{0,2},{1,3},{4,6},{5,7},{8,10},{9,11},{12,14},{13,15},{16,18},{17,... | collective-permute-start | bytes 1474568 | tf_op jit(solution)/shard_map/ppermute | solution.py:505
  38.8 12.8 %collective-permute-start.7 = (bf16[192,1280]{1,0:T(8,128)(2,1)S(1)}, bf16[192,1280]{1,0:T(8,128)(2,1)S(1)}, u32[]{:S(2)}, u32[]{:S(2)}) collective-permute-start(bf16[192,1280]{1,0:T(8,128)(2,1)S(1)} %get-tuple-element.70), channel_id=1, source_target_pairs={{0,130},{1,131},{4,134},{5,135},{8,138},{9,139},{12,142},{13,143},... | collective-permute-start | bytes 1474568 | tf_op jit(solution)/shard_map/ppermute | solution.py:505
  42.4 13.5 %collective-permute-start.10 = (bf16[192,1024]{1,0:T(8,128)(2,1)S(1)}, bf16[192,1024]{1,0:T(8,128)(2,1)S(1)}, u32[]{:S(2)}, u32[]{:S(2)}) collective-permute-start(bf16[192,1024]{1,0:T(8,128)(2,1)S(1)} %get-tuple-element.76), channel_id=1, source_target_pairs={{0,32},{1,33},{4,36},{5,37},{8,40},{9,41},{12,44},{13,45},{16,48},... | collective-permute-start | bytes 1179656 | tf_op jit(solution)/shard_map/ppermute | solution.py:505
  44.0 11.9 %collective-permute-start.11 = (bf16[192,1024]{1,0:T(8,128)(2,1)S(1)}, bf16[192,1024]{1,0:T(8,128)(2,1)S(1)}, u32[]{:S(2)}, u32[]{:S(2)}) collective-permute-start(bf16[192,1024]{1,0:T(8,128)(2,1)S(1)} %get-tuple-element.78), channel_id=1, source_target_pairs={{0,96},{1,97},{4,100},{5,101},{8,104},{9,105},{12,108},{13,109},{1... | collective-permute-start | bytes 1179656 | tf_op jit(solution)/shard_map/ppermute | solution.py:505
  51.8 8.6 %collective-permute-start.8 = (bf16[96,1280]{1,0:T(8,128)(2,1)S(1)}, bf16[96,1280]{1,0:T(8,128)(2,1)S(1)}, u32[]{:S(2)}, u32[]{:S(2)}) collective-permute-start(bf16[96,1280]{1,0:T(8,128)(2,1)S(1)} %get-tuple-element.73), channel_id=1, source_target_pairs={{0,130},{1,131},{4,134},{5,135},{8,138},{9,139},{12,142},{13,143},... | collective-permute-start | bytes 737288 | tf_op jit(solution)/shard_map/ppermute | solution.py:505
  53.9 7.9 %collective-permute-start.9 = (bf16[96,1280]{1,0:T(8,128)(2,1)S(1)}, bf16[96,1280]{1,0:T(8,128)(2,1)S(1)}, u32[]{:S(2)}, u32[]{:S(2)}) collective-permute-start(bf16[96,1280]{1,0:T(8,128)(2,1)S(1)} %get-tuple-element.75), channel_id=1, source_target_pairs={{0,2},{1,3},{4,6},{5,7},{8,10},{9,11},{12,14},{13,15},{16,18},{17,... | collective-permute-start | bytes 737288 | tf_op jit(solution)/shard_map/ppermute | solution.py:505
  56.0 7.0 %collective-permute-start.15 = (bf16[96,1024]{1,0:T(8,128)(2,1)S(1)}, bf16[96,1024]{1,0:T(8,128)(2,1)S(1)}, u32[]{:S(2)}, u32[]{:S(2)}) collective-permute-start(bf16[96,1024]{1,0:T(8,128)(2,1)S(1)} %get-tuple-element.84), channel_id=1, source_target_pairs={{0,96},{1,97},{4,100},{5,101},{8,104},{9,105},{12,108},{13,109},{1... | collective-permute-start | bytes 589832 | tf_op jit(solution)/shard_map/ppermute | solution.py:505
  58.8 5.7 %collective-permute-start.16 = (bf16[96,1024]{1,0:T(8,128)(2,1)S(1)}, bf16[96,1024]{1,0:T(8,128)(2,1)S(1)}, u32[]{:S(2)}, u32[]{:S(2)}) collective-permute-start(bf16[96,1024]{1,0:T(8,128)(2,1)S(1)} %get-tuple-element.86), channel_id=1, source_target_pairs={{0,32},{1,33},{4,36},{5,37},{8,40},{9,41},{12,44},{13,45},{16,48},... | collective-permute-start | bytes 589832 | tf_op jit(solution)/shard_map/ppermute | solution.py:505
  64.6 9.1 %collective-permute-start.17 = (bf16[48,1024]{1,0:T(8,128)(2,1)S(1)}, bf16[48,1024]{1,0:T(8,128)(2,1)S(1)}, u32[]{:S(2)}, u32[]{:S(2)}) collective-permute-start(bf16[48,1024]{1,0:T(8,128)(2,1)S(1)} %get-tuple-element.88), channel_id=1, source_target_pairs={{0,2},{1,3},{4,6},{5,7},{8,10},{9,11},{12,14},{13,15},{16,18},{17,... | collective-permute-start | bytes 294920 | tf_op jit(solution)/shard_map/ppermute | solution.py:505
  66.0 12.3 %collective-permute-start.12 = (bf16[48,1280]{1,0:T(8,128)(2,1)S(1)}, bf16[48,1280]{1,0:T(8,128)(2,1)S(1)}, u32[]{:S(2)}, u32[]{:S(2)}) collective-permute-start(bf16[48,1280]{1,0:T(8,128)(2,1)S(1)} %get-tuple-element.81), channel_id=1, source_target_pairs={{0,32},{1,33},{4,36},{5,37},{8,40},{9,41},{12,44},{13,45},{16,48},... | collective-permute-start | bytes 368648 | tf_op jit(solution)/shard_map/ppermute | solution.py:505
  66.0 12.3 %collective-permute-start.13 = (bf16[48,1280]{1,0:T(8,128)(2,1)S(1)}, bf16[48,1280]{1,0:T(8,128)(2,1)S(1)}, u32[]{:S(2)}, u32[]{:S(2)}) collective-permute-start(bf16[48,1280]{1,0:T(8,128)(2,1)S(1)} %get-tuple-element.82), channel_id=1, source_target_pairs={{0,64},{1,65},{4,68},{5,69},{8,72},{9,73},{12,76},{13,77},{16,80},... | collective-permute-start | bytes 368648 | tf_op jit(solution)/shard_map/ppermute | solution.py:505
  68.7 9.6 %collective-permute-start.14 = (bf16[48,1280]{1,0:T(8,128)(2,1)S(1)}, bf16[48,1280]{1,0:T(8,128)(2,1)S(1)}, u32[]{:S(2)}, u32[]{:S(2)}) collective-permute-start(bf16[48,1280]{1,0:T(8,128)(2,1)S(1)} %get-tuple-element.83), channel_id=1, source_target_pairs={{0,96},{1,97},{4,100},{5,101},{8,104},{9,105},{12,108},{13,109},{1... | collective-permute-start | bytes 368648 | tf_op jit(solution)/shard_map/ppermute | solution.py:505
  70.7 6.1 %collective-permute-start.18 = (bf16[48,1024]{1,0:T(8,128)(2,1)S(1)}, bf16[48,1024]{1,0:T(8,128)(2,1)S(1)}, u32[]{:S(2)}, u32[]{:S(2)}) collective-permute-start(bf16[48,1024]{1,0:T(8,128)(2,1)S(1)} %get-tuple-element.89), channel_id=1, source_target_pairs={{0,128},{1,129},{4,132},{5,133},{8,136},{9,137},{12,140},{13,141},... | collective-permute-start | bytes 294920 | tf_op jit(solution)/shard_map/ppermute | solution.py:505
  73.6 4.6 %collective-permute-start.19 = (bf16[48,1024]{1,0:T(8,128)(2,1)S(1)}, bf16[48,1024]{1,0:T(8,128)(2,1)S(1)}, u32[]{:S(2)}, u32[]{:S(2)}) collective-permute-start(bf16[48,1024]{1,0:T(8,128)(2,1)S(1)} %get-tuple-element.90), channel_id=1, source_target_pairs={{0,130},{1,131},{4,134},{5,135},{8,138},{9,139},{12,142},{13,143},... | collective-permute-start | bytes 294920 | tf_op jit(solution)/shard_map/ppermute | solution.py:505
  78.4 5.3 %collective-permute-start.20 = (bf16[12,2304]{1,0:T(8,128)(2,1)S(1)}, bf16[12,2304]{1,0:T(8,128)(2,1)S(1)}, u32[]{:S(2)}, u32[]{:S(2)}) collective-permute-start(bf16[12,2304]{1,0:T(8,128)(2,1)S(1)} %get-tuple-element.92), channel_id=1, source_target_pairs={{0,8},{1,9},{4,12},{5,13},{8,0},{9,1},{12,4},{13,5},{16,24},{17,25... | collective-permute-start | bytes 165896 | tf_op jit(solution)/shard_map/ppermute | solution.py:530
  78.5 5.2 %collective-permute-start.21 = (bf16[12,2304]{1,0:T(8,128)(2,1)S(1)}, bf16[12,2304]{1,0:T(8,128)(2,1)S(1)}, u32[]{:S(2)}, u32[]{:S(2)}) collective-permute-start(bf16[12,2304]{1,0:T(8,128)(2,1)S(1)} %get-tuple-element.93), channel_id=1, source_target_pairs={{0,4},{1,5},{4,0},{5,1},{8,12},{9,13},{12,8},{13,9},{16,20},{17,21... | collective-permute-start | bytes 165896 | tf_op jit(solution)/shard_map/ppermute | solution.py:530
  79.3 6.7 %collective-permute-start.22 = (bf16[12,2304]{1,0:T(8,128)(2,1)S(1)}, bf16[12,2304]{1,0:T(8,128)(2,1)S(1)}, u32[]{:S(2)}, u32[]{:S(2)}) collective-permute-start(bf16[12,2304]{1,0:T(8,128)(2,1)S(1)} %get-tuple-element.94), channel_id=1, source_target_pairs={{0,12},{1,13},{4,8},{5,9},{8,4},{9,5},{12,0},{13,1},{16,28},{17,29... | collective-permute-start | bytes 165896 | tf_op jit(solution)/shard_map/ppermute | solution.py:530
  86.0 8.0 %collective-permute-start.23 = (bf16[6,2304]{1,0:T(8,128)(2,1)S(1)}, bf16[6,2304]{1,0:T(8,128)(2,1)S(1)}, u32[]{:S(2)}, u32[]{:S(2)}) collective-permute-start(bf16[6,2304]{1,0:T(8,128)(2,1)S(1)} %get-tuple-element.96), channel_id=1, source_target_pairs={{0,16},{1,17},{4,20},{5,21},{8,24},{9,25},{12,28},{13,29},{16,0},{... | collective-permute-start | bytes 82952 | tf_op jit(solution)/shard_map/ppermute | solution.py:536
  (6 other events, 17.6 us)

commit v3 on v2

--- a/solution.py
+++ b/solution.py
@@ -99,7 +99,7 @@
     return pl.CostEstimate(flops=microseconds * 1_000_000_000, bytes_accessed=1000, transcendentals=0)
 
 
-def mask_kernel(incidence_ref, reach_ref, types_ref, out_ref):
+def mask_kernel(incidence_ref, reach_ref, types_ref, _, out_ref):
     seq_len = types_ref.shape[1]
     start = lax.axis_index("loop") * ROWS
     ahead = pl.multiple_of(lax.rem(start + seq_len - 2 * HALO, seq_len), 2 * HALO)
@@ -121,15 +121,16 @@
         out_ref[t * WIN : (t + 1) * WIN, :] = jnp.where(allowed, 1.0, 0.0)
 
 
-def make_mask(types, incidence, reach):
+def make_mask(types, incidence, reach, after):
     return call(
         mask_kernel,
         shape(TILES * WIN, 2 * TILE, F32),
         incidence.T,
         reach,
         types,
+        after,
         estimate=cost(2),
-        in_specs=[scalars(), scalars(), whole()],
+        in_specs=[scalars(), scalars(), whole(), anywhere()],
         out_specs=whole(),
     )
 
@@ -485,9 +486,9 @@
     own = tokens[0]
     left = lax.ppermute(own[ROWS - HALO :], "loop", along_loop(1))
     right = lax.ppermute(own[:HALO], "loop", along_loop(-1))
-    mask = make_mask(token_types, incidence[0], window_reach[0])
-    *arranged, mark = reorder(own, 0, (), (mask,))
-    x_own, x_send, mark = reorder(jnp.concatenate([left, right], axis=0), ROWS, arranged, (mark,))
+    *arranged, mark = reorder(own, 0, (), ())
+    mask = make_mask(token_types, incidence[0], window_reach[0], mark)
+    x_own, x_send, mark = reorder(jnp.concatenate([left, right], axis=0), ROWS, arranged, (mask,))
     x_other = lax.ppermute(x_send, AXES, TO_CORE)
     proj = projection(own, left, right, weights, mark)
 
@@ -517,7 +518,7 @@
 
     def round_three(way, state, after):
         keep, *sent = split_sum(*state, after)
-        return [keep, *(swap(n + 1, way, part) for n, part in enumerate(sent))]
+        return [keep, *(swap(n, way, sent[n - 1]) for n in (2, 1, 3))]
 
     by_y = round_one("y", blocks[:5], (attended_mark,))
     by_x = round_one("x", blocks[5:], (by_y[0], rim))
@@ -527,7 +528,8 @@
     by_y = round_three("x", by_y, (by_x[0],))
     by_x = round_three("y", by_x, (by_y[0],))
     keep, *sent = cut_rows(join_kernel, 12, 3, *by_y, *by_x)
-    got = [lax.ppermute(part, AXES, ACROSS_Z[m]) for part, m in zip(sent, (2, 1, 3))]
+    by_z = dict(zip((2, 1, 3), sent))
+    got = [lax.ppermute(by_z[m], AXES, ACROSS_Z[m]) for m in (3, 2, 1)]
     keep, send = cut_rows(halve_kernel, 6, 1, keep, *got)
     weight_grad = call(
         functools.partial(last_kernel, (256 * ROWS) ** -0.5),

time: 95.3 us -> 95.9 us (level)
  waiting for transfers between devices: 19.4 us -> 22.6 us
  starting transfers between devices: 39 us -> 36.8 us
    ppermute x1, waiting for transfers between devices: 3.67 us -> 6.03 us  [body(): lax.ppermute(send, AXES, ACROSS_Z[4])]
    ppermute x1, starting transfers between devices: 4.28 us -> 1.93 us  [body(): lax.ppermute(send, AXES, ACROSS_Z[4])]
    ppermute x1, waiting for transfers between devices: 2.57 us -> 3.76 us  [body(): left = lax.ppermute(own[ROWS - HALO:], 'loop', along_loop(1))]
    unnamed x13 -> x17, local copies, waits for them, and re-layouts: 2.66 us -> 2.26 us
  transfers between devices with their start and end apart: 24 -> 24, of which waited for: 10 -> 10; matrix products, arithmetic and copies ran while one was open for 1% -> 0% of each run, Pallas kernels for 19% -> 19%
where the time goes in v3:
time: 95.9 us; the launch traced here: 95.3 us
  starting transfers between devices  36.8 us (38%)
  Pallas kernels  31.8 us (33%)
  waiting for transfers between devices  22.6 us (24%)
  local copies, waits for them, and re-layouts  3.34 us (3%)
    pallas_call x17, Pallas kernels, call(): pl.pallas_call(kernel, out_shape=out_shape, cost_estimate=estimate or TIN...  31.8 us
    ppermute x14, starting transfers between devices, swap(): lax.ppermute(part, AXES, (ACROSS_Y if way == 'y' else ACROSS_X)[n - 1])  23 us
    ppermute x14, waiting for transfers between devices, swap(): lax.ppermute(part, AXES, (ACROSS_Y if way == 'y' else ACROSS_X)[n - 1])  9.83 us
    ppermute x1, starting transfers between devices, body(): lax.ppermute(rim, 'loop', [(i, (i - 1 + i % 2 * 2) % 32) for i in range(3...  6.31 us
    ppermute x1, waiting for transfers between devices, body(): lax.ppermute(send, AXES, ACROSS_Z[4])  6.03 us
    ppermute x3, starting transfers between devices, body(): got = [lax.ppermute(by_z[m], AXES, ACROSS_Z[m]) for m in (3, 2, 1)]  4.46 us
    ppermute x1, waiting for transfers between devices, body(): left = lax.ppermute(own[ROWS - HALO:], 'loop', along_loop(1))  3.76 us
    ppermute x3, waiting for transfers between devices, body(): got = [lax.ppermute(by_z[m], AXES, ACROSS_Z[m]) for m in (3, 2, 1)]  2.95 us
  transfers between devices with their start and end apart: 24, of which 10 were waited for; matrix products, arithmetic and copies ran while one was open for 0% of the time, Pallas kernels for 19%

profile of v3, /device:TPU:8, one launch (start us, length us, event | category | flops | bytes accessed | tf_op | source)
XLA Modules:
  0.0 95.3 jit_solution(819628320307325394)
XLA Ops:
  5.8 3.8 %collective-permute-done.left_ref = bf16[64,1536]{1,0:T(8,128)(2,1)S(1)} collective-permute-done((bf16[64,1536]{1,0:T(8,128)(2,1)S(1)}, bf16[64,1536]{1,0:T(8,128)(2,1)S(1)}, u32[]{:S(2)}, u32[]{:S(2)}) %collective-permute-start) | collective-permute-done | bytes 196640 | tf_op jit(solution)/shard_map/ppermute | solution.py:487
  11.0 4.7 %shard_map.88.q_ref.k_ref.v_ref = bf16[640,2304]{1,0:T(8,128)(2,1)S(1)} custom-call(bf16[512,1536]{1,0:T(8,128)(2,1)S(1)} %bitcast.20, bf16[64,1536]{1,0:T(8,128)(2,1)S(1)} %collective-permute-done.left_ref, bf16[64,1536]{1,0:T(8,128)(2,1)S(1)} %collective-permute-done.1.right_ref, bf16[1536,2304]{1,0:T(8,128)(2,1)S(1)} %bitcast.15, ...), custom_call_target="tpu_custom_call" | custom-call | flops 1000 | bytes 1000 | tf_op jit(solution)/shard_map/pallas_call | solution.py:70
  15.8 4.0 %shard_map.89 = (bf16[512,768]{1,0:T(8,128)(2,1)}, bf16[64,1536]{1,0:T(8,128)(2,1)S(1)}, bf16[640,1536]{1,0:T(8,128)(2,1)S(1)}) custom-call(bf16[640,2304]{1,0:T(8,128)(2,1)S(1)} %shard_map.88.q_ref.k_ref.v_ref, bf16[640,2304]{1,0:T(8,128)(2,1)S(1)} %shard_map.88.q_ref.k_ref.v_ref, bf16[640,2304]{1,0:T(8,128)(2,1)S(1)} %shard_map.88.q_ref.k_ref.v_ref, ...), custom_call_target="tpu_custom_call" | custom-call | flops 1000 | bytes 1000 | tf_op jit(solution)/shard_map/pallas_call | solution.py:70
  19.7 4.0 %shard_map.90 = (bf16[512,768]{1,0:T(8,128)(2,1)}, bf16[64,1536]{1,0:T(8,128)(2,1)S(1)}, bf16[640,1536]{1,0:T(8,128)(2,1)S(1)}) custom-call(bf16[640,2304]{1,0:T(8,128)(2,1)S(1)} %shard_map.88.q_ref.k_ref.v_ref, bf16[640,2304]{1,0:T(8,128)(2,1)S(1)} %shard_map.88.q_ref.k_ref.v_ref, ...), custom_call_target="tpu_custom_call", output_to_operand_aliasing={{0}: (5, {}), {1}: (6, {}), {2}: (7, {})} | custom-call | flops 1000 | bytes 1000 | tf_op jit(solution)/shard_map/pallas_call | solution.py:70
  24.2 4.0 %shard_map.91 = (bf16[512,768]{1,0:T(8,128)(2,1)}, bf16[64,1536]{1,0:T(8,128)(2,1)S(1)}, bf16[640,768]{1,0:T(8,128)(2,1)S(1)}) custom-call(bf16[640,2304]{1,0:T(8,128)(2,1)S(1)} %shard_map.88.q_ref.k_ref.v_ref, bf16[640,2304]{1,0:T(8,128)(2,1)S(1)} %shard_map.88.q_ref.k_ref.v_ref, ...), custom_call_target="tpu_custom_call", output_to_operand_aliasing={{0}: (5, {}), {1}: (6, {})} | custom-call | flops 1000 | bytes 1000 | tf_op jit(solution)/shard_map/pallas_call | solution.py:70
  28.2 6.3 %collective-permute-start.4 = (bf16[64,1536]{1,0:T(8,128)(2,1)S(1)}, bf16[64,1536]{1,0:T(8,128)(2,1)S(1)}, u32[]{:S(2)}, u32[]{:S(2)}) collective-permute-start(bf16[64,1536]{1,0:T(8,128)(2,1)S(1)} %get-tuple-element.62.refs_2_), channel_id=1, source_target_pairs={{0,31},{1,2},{2,1},{3,4},{4,3},{5,6},{6,5},{7,8},{8,7},{9,10},{10,... | collective-permute-start | bytes 589832 | tf_op jit(solution)/shard_map/ppermute | solution.py:502
  34.5 3.2 %shard_map.92 = (f32[192,1280]{1,0:T(8,128)S(1)}, bf16[192,1280]{1,0:T(8,128)(2,1)S(1)}, f32[192,1280]{1,0:T(8,128)S(1)}, bf16[192,1280]{1,0:T(8,128)(2,1)S(1)}) custom-call(bf16[768,640]{1,0:T(8,128)(2,1)S(1)} %get-tuple-element.63.x_ref, bf16[768,640]{1,0:T(8,128)(2,1)S(1)} %collective-permute-done.5.xp_ref, ...), custom_call_target="tpu_custom_call" | custom-call | flops 1000 | bytes 1000 | tf_op jit(solution)/shard_map/pallas_call | solution.py:70
  38.6 2.1 %collective-permute-start.7 = (bf16[192,1280]{1,0:T(8,128)(2,1)S(1)}, bf16[192,1280]{1,0:T(8,128)(2,1)S(1)}, u32[]{:S(2)}, u32[]{:S(2)}) collective-permute-start(bf16[192,1280]{1,0:T(8,128)(2,1)S(1)} %get-tuple-element.70), channel_id=1, source_target_pairs={{0,130},{1,131},{4,134},{5,135},{8,138},{9,139},{12,142},{13,143},... | collective-permute-start | bytes 1474568 | tf_op jit(solution)/shard_map/ppermute | solution.py:506
  40.7 2.6 %shard_map.93 = (f32[192,1024]{1,0:T(8,128)S(1)}, bf16[192,1024]{1,0:T(8,128)(2,1)S(1)}, f32[192,1024]{1,0:T(8,128)S(1)}, bf16[192,1024]{1,0:T(8,128)(2,1)S(1)}) custom-call(bf16[768,640]{1,0:T(8,128)(2,1)S(1)} %get-tuple-element.63.x_ref, bf16[768,640]{1,0:T(8,128)(2,1)S(1)} %collective-permute-done.5.xp_ref, ...), custom_call_target="tpu_custom_call" | custom-call | flops 1000 | bytes 1000 | tf_op jit(solution)/shard_map/pallas_call | solution.py:70
  43.3 1.6 %collective-permute-start.10 = (bf16[192,1024]{1,0:T(8,128)(2,1)S(1)}, bf16[192,1024]{1,0:T(8,128)(2,1)S(1)}, u32[]{:S(2)}, u32[]{:S(2)}) collective-permute-start(bf16[192,1024]{1,0:T(8,128)(2,1)S(1)} %get-tuple-element.76), channel_id=1, source_target_pairs={{0,32},{1,33},{4,36},{5,37},{8,40},{9,41},{12,44},{13,45},{16,48},... | collective-permute-start | bytes 1179656 | tf_op jit(solution)/shard_map/ppermute | solution.py:506
  44.9 2.1 %collective-permute-start.11 = (bf16[192,1024]{1,0:T(8,128)(2,1)S(1)}, bf16[192,1024]{1,0:T(8,128)(2,1)S(1)}, u32[]{:S(2)}, u32[]{:S(2)}) collective-permute-start(bf16[192,1024]{1,0:T(8,128)(2,1)S(1)} %get-tuple-element.78), channel_id=1, source_target_pairs={{0,96},{1,97},{4,100},{5,101},{8,104},{9,105},{12,108},{13,109},{1... | collective-permute-start | bytes 1179656 | tf_op jit(solution)/shard_map/ppermute | solution.py:506
  46.9 5.5 %shard_map.94 = (bf16[512,1536]{1,0:T(8,128)(2,1)}, f32[8,128]{1,0:T(8,128)S(1)}) custom-call(bf16[640,1536]{1,0:T(8,128)(2,1)S(1)} %get-tuple-element.60.refs_0_.a_ref.b_ref, bf16[640,1536]{1,0:T(8,128)(2,1)S(1)} %get-tuple-element.60.refs_0_.a_ref.b_ref, bf16[640,768]{1,0:T(8,128)(2,1)S(1)} %get-tuple-element.61.refs_1_.c_ref, ...), custom_call_target="tpu_custom_call" | custom-call | flops 1000 | bytes 1000 | tf_op jit(solution)/shard_map/pallas_call | solution.py:70
  52.7 2.2 %collective-permute-start.8 = (bf16[96,1280]{1,0:T(8,128)(2,1)S(1)}, bf16[96,1280]{1,0:T(8,128)(2,1)S(1)}, u32[]{:S(2)}, u32[]{:S(2)}) collective-permute-start(bf16[96,1280]{1,0:T(8,128)(2,1)S(1)} %get-tuple-element.73), channel_id=1, source_target_pairs={{0,130},{1,131},{4,134},{5,135},{8,138},{9,139},{12,142},{13,143},... | collective-permute-start | bytes 737288 | tf_op jit(solution)/shard_map/ppermute | solution.py:506
  54.8 1.9 %collective-permute-start.9 = (bf16[96,1280]{1,0:T(8,128)(2,1)S(1)}, bf16[96,1280]{1,0:T(8,128)(2,1)S(1)}, u32[]{:S(2)}, u32[]{:S(2)}) collective-permute-start(bf16[96,1280]{1,0:T(8,128)(2,1)S(1)} %get-tuple-element.75), channel_id=1, source_target_pairs={{0,2},{1,3},{4,6},{5,7},{8,10},{9,11},{12,14},{13,15},{16,18},{17,... | collective-permute-start | bytes 737288 | tf_op jit(solution)/shard_map/ppermute | solution.py:506
  56.9 2.8 %collective-permute-start.15 = (bf16[96,1024]{1,0:T(8,128)(2,1)S(1)}, bf16[96,1024]{1,0:T(8,128)(2,1)S(1)}, u32[]{:S(2)}, u32[]{:S(2)}) collective-permute-start(bf16[96,1024]{1,0:T(8,128)(2,1)S(1)} %get-tuple-element.84), channel_id=1, source_target_pairs={{0,96},{1,97},{4,100},{5,101},{8,104},{9,105},{12,108},{13,109},{1... | collective-permute-start | bytes 589832 | tf_op jit(solution)/shard_map/ppermute | solution.py:506
  63.8 1.5 %collective-permute-done.16.got_b_ref = bf16[96,1024]{1,0:T(8,128)(2,1)S(1)} collective-permute-done((bf16[96,1024]{1,0:T(8,128)(2,1)S(1)}, bf16[96,1024]{1,0:T(8,128)(2,1)S(1)}, u32[]{:S(2)}, u32[]{:S(2)}) %collective-permute-start.16) | collective-permute-done | bytes 196640 | tf_op jit(solution)/shard_map/ppermute | solution.py:506
  67.7 2.0 %collective-permute-start.14 = (bf16[48,1280]{1,0:T(8,128)(2,1)S(1)}, bf16[48,1280]{1,0:T(8,128)(2,1)S(1)}, u32[]{:S(2)}, u32[]{:S(2)}) collective-permute-start(bf16[48,1280]{1,0:T(8,128)(2,1)S(1)} %get-tuple-element.83), channel_id=1, source_target_pairs={{0,96},{1,97},{4,100},{5,101},{8,104},{9,105},{12,108},{13,109},{1... | collective-permute-start | bytes 368648 | tf_op jit(solution)/shard_map/ppermute | solution.py:506
  69.7 4.8 %collective-permute-start.18 = (bf16[48,1024]{1,0:T(8,128)(2,1)S(1)}, bf16[48,1024]{1,0:T(8,128)(2,1)S(1)}, u32[]{:S(2)}, u32[]{:S(2)}) collective-permute-start(bf16[48,1024]{1,0:T(8,128)(2,1)S(1)} %get-tuple-element.89), channel_id=1, source_target_pairs={{0,2},{1,3},{4,6},{5,7},{8,10},{9,11},{12,14},{13,15},{16,18},{17,... | collective-permute-start | bytes 294920 | tf_op jit(solution)/shard_map/ppermute | solution.py:506
  74.7 2.4 %collective-permute-done.18.refs_6_ = bf16[48,1024]{1,0:T(8,128)(2,1)S(1)} collective-permute-done((bf16[48,1024]{1,0:T(8,128)(2,1)S(1)}, bf16[48,1024]{1,0:T(8,128)(2,1)S(1)}, u32[]{:S(2)}, u32[]{:S(2)}) %collective-permute-start.18) | collective-permute-done | bytes 98336 | tf_op jit(solution)/shard_map/ppermute | solution.py:506
  77.1 2.0 %collective-permute-done.19.refs_7_ = bf16[48,1024]{1,0:T(8,128)(2,1)S(1)} collective-permute-done((bf16[48,1024]{1,0:T(8,128)(2,1)S(1)}, bf16[48,1024]{1,0:T(8,128)(2,1)S(1)}, u32[]{:S(2)}, u32[]{:S(2)}) %collective-permute-start.19) | collective-permute-done | bytes 98336 | tf_op jit(solution)/shard_map/ppermute | solution.py:506
  79.5 4.3 %collective-permute-start.22 = (bf16[12,2304]{1,0:T(8,128)(2,1)S(1)}, bf16[12,2304]{1,0:T(8,128)(2,1)S(1)}, u32[]{:S(2)}, u32[]{:S(2)}) collective-permute-start(bf16[12,2304]{1,0:T(8,128)(2,1)S(1)} %get-tuple-element.94), channel_id=1, source_target_pairs={{0,4},{1,5},{4,0},{5,1},{8,12},{9,13},{12,8},{13,9},{16,20},{17,21... | collective-permute-start | bytes 165896 | tf_op jit(solution)/shard_map/ppermute | solution.py:532
  83.7 1.8 %collective-permute-done.20.a_ref = bf16[12,2304]{1,0:T(8,128)(2,1)S(1)} collective-permute-done((bf16[12,2304]{1,0:T(8,128)(2,1)S(1)}, bf16[12,2304]{1,0:T(8,128)(2,1)S(1)}, u32[]{:S(2)}, u32[]{:S(2)}) %collective-permute-start.20) | collective-permute-done | bytes 55328 | tf_op jit(solution)/shard_map/ppermute | solution.py:532
  86.7 1.9 %collective-permute-start.23 = (bf16[6,2304]{1,0:T(8,128)(2,1)S(1)}, bf16[6,2304]{1,0:T(8,128)(2,1)S(1)}, u32[]{:S(2)}, u32[]{:S(2)}) collective-permute-start(bf16[6,2304]{1,0:T(8,128)(2,1)S(1)} %get-tuple-element.96), channel_id=1, source_target_pairs={{0,16},{1,17},{4,20},{5,21},{8,24},{9,25},{12,28},{13,29},{16,0},{... | collective-permute-start | bytes 82952 | tf_op jit(solution)/shard_map/ppermute | solution.py:538
  88.7 6.0 %collective-permute-done.23.got_ref = bf16[6,2304]{1,0:T(8,128)(2,1)S(1)} collective-permute-done((bf16[6,2304]{1,0:T(8,128)(2,1)S(1)}, bf16[6,2304]{1,0:T(8,128)(2,1)S(1)}, u32[]{:S(2)}, u32[]{:S(2)}) %collective-permute-start.23) | collective-permute-done | bytes 27680 | tf_op jit(solution)/shard_map/ppermute | solution.py:538
  (61 shorter events, 17.0 us)
Async XLA Ops:
  1.7 4.1 %collective-permute-start.1 = (bf16[64,1536]{1,0:T(8,128)(2,1)S(1)}, bf16[64,1536]{1,0:T(8,128)(2,1)S(1)}, u32[]{:S(2)}, u32[]{:S(2)}) collective-permute-start(bf16[64,1536]{1,0:T(8,128)(2,1)S(1)} %get-tuple-element.97), channel_id=1, source_target_pairs={{1,0},{2,1},{3,2},{4,3},{5,4},{6,5},{7,6},{8,7},{9,8},{10,9},{11,1... | collective-permute-start | bytes 589832 | tf_op jit(solution)/shard_map/ppermute | solution.py:488
  1.8 7.7 %collective-permute-start = (bf16[64,1536]{1,0:T(8,128)(2,1)S(1)}, bf16[64,1536]{1,0:T(8,128)(2,1)S(1)}, u32[]{:S(2)}, u32[]{:S(2)}) collective-permute-start(bf16[64,1536]{1,0:T(8,128)(2,1)S(1)} %get-tuple-element.98), channel_id=1, source_target_pairs={{31,0},{0,1},{1,2},{2,3},{3,4},{4,5},{5,6},{6,7},{7,8},{8,9},{9,10... | collective-permute-start | bytes 589832 | tf_op jit(solution)/shard_map/ppermute | solution.py:487
  23.7 10.8 %collective-permute-start.2 = (bf16[640,1536]{1,0:T(8,128)(2,1)S(1)}, bf16[640,1536]{1,0:T(8,128)(2,1)S(1)}, u32[]{:S(2)}, u32[]{:S(2)}) collective-permute-start(bf16[640,1536]{1,0:T(8,128)(2,1)S(1)} %get-tuple-element.60.refs_0_.a_ref.b_ref), channel_id=1, source_target_pairs={{0,1},{1,0},{4,5},{5,4},{8,9},{9,8},{12,13},{13,12},{16,17},{17,16... | collective-permute-start | bytes 5898248 | tf_op jit(solution)/shard_map/ppermute | solution.py:498
  23.7 10.8 %collective-permute-start.5 = (bf16[768,640]{1,0:T(8,128)(2,1)S(1)}, bf16[768,640]{1,0:T(8,128)(2,1)S(1)}, u32[]{:S(2)}, u32[]{:S(2)}) collective-permute-start(bf16[768,640]{1,0:T(8,128)(2,1)S(1)} %get-tuple-element.64), channel_id=1, source_target_pairs={{0,1},{1,0},{4,5},{5,4},{8,9},{9,8},{12,13},{13,12},{16,17},{17,16... | collective-permute-start | bytes 2949128 | tf_op jit(solution)/shard_map/ppermute | solution.py:492
  28.2 12.5 %collective-permute-start.3 = (bf16[640,768]{1,0:T(8,128)(2,1)S(1)}, bf16[640,768]{1,0:T(8,128)(2,1)S(1)}, u32[]{:S(2)}, u32[]{:S(2)}) collective-permute-start(bf16[640,768]{1,0:T(8,128)(2,1)S(1)} %get-tuple-element.61.refs_1_.c_ref), channel_id=1, source_target_pairs={{0,1},{1,0},{4,5},{5,4},{8,9},{9,8},{12,13},{13,12},{16,17},{17,16... | collective-permute-start | bytes 2949128 | tf_op jit(solution)/shard_map/ppermute | solution.py:501
  28.2 12.5 %collective-permute-start.4 = (bf16[64,1536]{1,0:T(8,128)(2,1)S(1)}, bf16[64,1536]{1,0:T(8,128)(2,1)S(1)}, u32[]{:S(2)}, u32[]{:S(2)}) collective-permute-start(bf16[64,1536]{1,0:T(8,128)(2,1)S(1)} %get-tuple-element.62.refs_2_), channel_id=1, source_target_pairs={{0,31},{1,2},{2,1},{3,4},{4,3},{5,6},{6,5},{7,8},{8,7},{9,10},{10,... | collective-permute-start | bytes 589832 | tf_op jit(solution)/shard_map/ppermute | solution.py:502
  37.7 14.8 %collective-permute-start.6 = (bf16[192,1280]{1,0:T(8,128)(2,1)S(1)}, bf16[192,1280]{1,0:T(8,128)(2,1)S(1)}, u32[]{:S(2)}, u32[]{:S(2)}) collective-permute-start(bf16[192,1280]{1,0:T(8,128)(2,1)S(1)} %get-tuple-element.68), channel_id=1, source_target_pairs={{0,2},{1,3},{4,6},{5,7},{8,10},{9,11},{12,14},{13,15},{16,18},{17,... | collective-permute-start | bytes 1474568 | tf_op jit(solution)/shard_map/ppermute | solution.py:506
  38.6 13.9 %collective-permute-start.7 = (bf16[192,1280]{1,0:T(8,128)(2,1)S(1)}, bf16[192,1280]{1,0:T(8,128)(2,1)S(1)}, u32[]{:S(2)}, u32[]{:S(2)}) collective-permute-start(bf16[192,1280]{1,0:T(8,128)(2,1)S(1)} %get-tuple-element.70), channel_id=1, source_target_pairs={{0,130},{1,131},{4,134},{5,135},{8,138},{9,139},{12,142},{13,143},... | collective-permute-start | bytes 1474568 | tf_op jit(solution)/shard_map/ppermute | solution.py:506
  43.3 13.5 %collective-permute-start.10 = (bf16[192,1024]{1,0:T(8,128)(2,1)S(1)}, bf16[192,1024]{1,0:T(8,128)(2,1)S(1)}, u32[]{:S(2)}, u32[]{:S(2)}) collective-permute-start(bf16[192,1024]{1,0:T(8,128)(2,1)S(1)} %get-tuple-element.76), channel_id=1, source_target_pairs={{0,32},{1,33},{4,36},{5,37},{8,40},{9,41},{12,44},{13,45},{16,48},... | collective-permute-start | bytes 1179656 | tf_op jit(solution)/shard_map/ppermute | solution.py:506
  44.9 11.9 %collective-permute-start.11 = (bf16[192,1024]{1,0:T(8,128)(2,1)S(1)}, bf16[192,1024]{1,0:T(8,128)(2,1)S(1)}, u32[]{:S(2)}, u32[]{:S(2)}) collective-permute-start(bf16[192,1024]{1,0:T(8,128)(2,1)S(1)} %get-tuple-element.78), channel_id=1, source_target_pairs={{0,96},{1,97},{4,100},{5,101},{8,104},{9,105},{12,108},{13,109},{1... | collective-permute-start | bytes 1179656 | tf_op jit(solution)/shard_map/ppermute | solution.py:506
  52.7 8.6 %collective-permute-start.8 = (bf16[96,1280]{1,0:T(8,128)(2,1)S(1)}, bf16[96,1280]{1,0:T(8,128)(2,1)S(1)}, u32[]{:S(2)}, u32[]{:S(2)}) collective-permute-start(bf16[96,1280]{1,0:T(8,128)(2,1)S(1)} %get-tuple-element.73), channel_id=1, source_target_pairs={{0,130},{1,131},{4,134},{5,135},{8,138},{9,139},{12,142},{13,143},... | collective-permute-start | bytes 737288 | tf_op jit(solution)/shard_map/ppermute | solution.py:506
  54.8 7.9 %collective-permute-start.9 = (bf16[96,1280]{1,0:T(8,128)(2,1)S(1)}, bf16[96,1280]{1,0:T(8,128)(2,1)S(1)}, u32[]{:S(2)}, u32[]{:S(2)}) collective-permute-start(bf16[96,1280]{1,0:T(8,128)(2,1)S(1)} %get-tuple-element.75), channel_id=1, source_target_pairs={{0,2},{1,3},{4,6},{5,7},{8,10},{9,11},{12,14},{13,15},{16,18},{17,... | collective-permute-start | bytes 737288 | tf_op jit(solution)/shard_map/ppermute | solution.py:506
  56.9 7.0 %collective-permute-start.15 = (bf16[96,1024]{1,0:T(8,128)(2,1)S(1)}, bf16[96,1024]{1,0:T(8,128)(2,1)S(1)}, u32[]{:S(2)}, u32[]{:S(2)}) collective-permute-start(bf16[96,1024]{1,0:T(8,128)(2,1)S(1)} %get-tuple-element.84), channel_id=1, source_target_pairs={{0,96},{1,97},{4,100},{5,101},{8,104},{9,105},{12,108},{13,109},{1... | collective-permute-start | bytes 589832 | tf_op jit(solution)/shard_map/ppermute | solution.py:506
  59.7 5.7 %collective-permute-start.16 = (bf16[96,1024]{1,0:T(8,128)(2,1)S(1)}, bf16[96,1024]{1,0:T(8,128)(2,1)S(1)}, u32[]{:S(2)}, u32[]{:S(2)}) collective-permute-start(bf16[96,1024]{1,0:T(8,128)(2,1)S(1)} %get-tuple-element.86), channel_id=1, source_target_pairs={{0,32},{1,33},{4,36},{5,37},{8,40},{9,41},{12,44},{13,45},{16,48},... | collective-permute-start | bytes 589832 | tf_op jit(solution)/shard_map/ppermute | solution.py:506
  65.5 9.1 %collective-permute-start.17 = (bf16[48,1024]{1,0:T(8,128)(2,1)S(1)}, bf16[48,1024]{1,0:T(8,128)(2,1)S(1)}, u32[]{:S(2)}, u32[]{:S(2)}) collective-permute-start(bf16[48,1024]{1,0:T(8,128)(2,1)S(1)} %get-tuple-element.88), channel_id=1, source_target_pairs={{0,128},{1,129},{4,132},{5,133},{8,136},{9,137},{12,140},{13,141},... | collective-permute-start | bytes 294920 | tf_op jit(solution)/shard_map/ppermute | solution.py:506
  65.6 13.6 %collective-permute-start.12 = (bf16[48,1280]{1,0:T(8,128)(2,1)S(1)}, bf16[48,1280]{1,0:T(8,128)(2,1)S(1)}, u32[]{:S(2)}, u32[]{:S(2)}) collective-permute-start(bf16[48,1280]{1,0:T(8,128)(2,1)S(1)} %get-tuple-element.81), channel_id=1, source_target_pairs={{0,64},{1,65},{4,68},{5,69},{8,72},{9,73},{12,76},{13,77},{16,80},... | collective-permute-start | bytes 368648 | tf_op jit(solution)/shard_map/ppermute | solution.py:506
  66.9 12.2 %collective-permute-start.13 = (bf16[48,1280]{1,0:T(8,128)(2,1)S(1)}, bf16[48,1280]{1,0:T(8,128)(2,1)S(1)}, u32[]{:S(2)}, u32[]{:S(2)}) collective-permute-start(bf16[48,1280]{1,0:T(8,128)(2,1)S(1)} %get-tuple-element.82), channel_id=1, source_target_pairs={{0,32},{1,33},{4,36},{5,37},{8,40},{9,41},{12,44},{13,45},{16,48},... | collective-permute-start | bytes 368648 | tf_op jit(solution)/shard_map/ppermute | solution.py:506
  67.7 11.4 %collective-permute-start.14 = (bf16[48,1280]{1,0:T(8,128)(2,1)S(1)}, bf16[48,1280]{1,0:T(8,128)(2,1)S(1)}, u32[]{:S(2)}, u32[]{:S(2)}) collective-permute-start(bf16[48,1280]{1,0:T(8,128)(2,1)S(1)} %get-tuple-element.83), channel_id=1, source_target_pairs={{0,96},{1,97},{4,100},{5,101},{8,104},{9,105},{12,108},{13,109},{1... | collective-permute-start | bytes 368648 | tf_op jit(solution)/shard_map/ppermute | solution.py:506
  69.7 7.4 %collective-permute-start.18 = (bf16[48,1024]{1,0:T(8,128)(2,1)S(1)}, bf16[48,1024]{1,0:T(8,128)(2,1)S(1)}, u32[]{:S(2)}, u32[]{:S(2)}) collective-permute-start(bf16[48,1024]{1,0:T(8,128)(2,1)S(1)} %get-tuple-element.89), channel_id=1, source_target_pairs={{0,2},{1,3},{4,6},{5,7},{8,10},{9,11},{12,14},{13,15},{16,18},{17,... | collective-permute-start | bytes 294920 | tf_op jit(solution)/shard_map/ppermute | solution.py:506
  74.5 4.6 %collective-permute-start.19 = (bf16[48,1024]{1,0:T(8,128)(2,1)S(1)}, bf16[48,1024]{1,0:T(8,128)(2,1)S(1)}, u32[]{:S(2)}, u32[]{:S(2)}) collective-permute-start(bf16[48,1024]{1,0:T(8,128)(2,1)S(1)} %get-tuple-element.90), channel_id=1, source_target_pairs={{0,130},{1,131},{4,134},{5,135},{8,138},{9,139},{12,142},{13,143},... | collective-permute-start | bytes 294920 | tf_op jit(solution)/shard_map/ppermute | solution.py:506
  79.3 6.3 %collective-permute-start.20 = (bf16[12,2304]{1,0:T(8,128)(2,1)S(1)}, bf16[12,2304]{1,0:T(8,128)(2,1)S(1)}, u32[]{:S(2)}, u32[]{:S(2)}) collective-permute-start(bf16[12,2304]{1,0:T(8,128)(2,1)S(1)} %get-tuple-element.92), channel_id=1, source_target_pairs={{0,12},{1,13},{4,8},{5,9},{8,4},{9,5},{12,0},{13,1},{16,28},{17,29... | collective-permute-start | bytes 165896 | tf_op jit(solution)/shard_map/ppermute | solution.py:532
  79.4 6.2 %collective-permute-start.21 = (bf16[12,2304]{1,0:T(8,128)(2,1)S(1)}, bf16[12,2304]{1,0:T(8,128)(2,1)S(1)}, u32[]{:S(2)}, u32[]{:S(2)}) collective-permute-start(bf16[12,2304]{1,0:T(8,128)(2,1)S(1)} %get-tuple-element.93), channel_id=1, source_target_pairs={{0,8},{1,9},{4,12},{5,13},{8,0},{9,1},{12,4},{13,5},{16,24},{17,25... | collective-permute-start | bytes 165896 | tf_op jit(solution)/shard_map/ppermute | solution.py:532
  79.5 7.2 %collective-permute-start.22 = (bf16[12,2304]{1,0:T(8,128)(2,1)S(1)}, bf16[12,2304]{1,0:T(8,128)(2,1)S(1)}, u32[]{:S(2)}, u32[]{:S(2)}) collective-permute-start(bf16[12,2304]{1,0:T(8,128)(2,1)S(1)} %get-tuple-element.94), channel_id=1, source_target_pairs={{0,4},{1,5},{4,0},{5,1},{8,12},{9,13},{12,8},{13,9},{16,20},{17,21... | collective-permute-start | bytes 165896 | tf_op jit(solution)/shard_map/ppermute | solution.py:532
  86.7 8.0 %collective-permute-start.23 = (bf16[6,2304]{1,0:T(8,128)(2,1)S(1)}, bf16[6,2304]{1,0:T(8,128)(2,1)S(1)}, u32[]{:S(2)}, u32[]{:S(2)}) collective-permute-start(bf16[6,2304]{1,0:T(8,128)(2,1)S(1)} %get-tuple-element.96), channel_id=1, source_target_pairs={{0,16},{1,17},{4,20},{5,21},{8,24},{9,25},{12,28},{13,29},{16,0},{... | collective-permute-start | bytes 82952 | tf_op jit(solution)/shard_map/ppermute | solution.py:538
  (8 other events, 29.8 us)

commit v4 on v2

--- a/solution.py
+++ b/solution.py
@@ -11,6 +11,7 @@
 HD = 64
 TILE = 64
 CAP = 20
+LOG2_E = 1.4426950408889634
 HW = 768
 HALO = 64
 GROUPS = 3
@@ -115,7 +116,7 @@
     for t in range(TILES):
         own = row[:, HALO + t * TILE : HALO + (t + 1) * TILE]
         other_kind = column[t * TILE : t * TILE + WIN] != jnp.concatenate([own, own], axis=1)
-        linked = [jnp.full((TILE, 2 * TILE), incidence_ref[r, t], jnp.int32) for r in range(3)]
+        linked = [jnp.full((TILE, 2 * TILE), incidence_ref[r, 0, t], jnp.int32) for r in range(3)]
         linked = jnp.concatenate(linked, axis=0) == 1
         allowed = (distance == 0) | ((distance <= reach_ref[t]) & other_kind & linked)
         out_ref[t * WIN : (t + 1) * WIN, :] = jnp.where(allowed, 1.0, 0.0)
@@ -125,7 +126,7 @@
     return call(
         mask_kernel,
         shape(TILES * WIN, 2 * TILE, F32),
-        incidence.T,
+        incidence,
         reach,
         types,
         estimate=cost(2),
@@ -239,7 +240,7 @@
         mask = mask_ref[pl.ds(pl.multiple_of(t * WIN, WIN), WIN), :]
         mask = jnp.concatenate([mask] * (GH // 2), axis=1)
         bent = jnp.tanh(dot(k_win, q_bd, NT) * (HD**-0.5 / CAP))
-        numer = jnp.exp(bent * CAP) * mask
+        numer = jnp.exp2(bent * (CAP * LOG2_E)) * mask
         probs = numer * (1.0 / jnp.sum(numer, axis=0, keepdims=True))
         low = probs.astype(BF16)
         weighted = probs * dot(v_win, g_bd, NT)
@@ -485,7 +486,7 @@
     own = tokens[0]
     left = lax.ppermute(own[ROWS - HALO :], "loop", along_loop(1))
     right = lax.ppermute(own[:HALO], "loop", along_loop(-1))
-    mask = make_mask(token_types, incidence[0], window_reach[0])
+    mask = make_mask(token_types, incidence.transpose(2, 0, 1), window_reach[0])
     *arranged, mark = reorder(own, 0, (), (mask,))
     x_own, x_send, mark = reorder(jnp.concatenate([left, right], axis=0), ROWS, arranged, (mark,))
     x_other = lax.ppermute(x_send, AXES, TO_CORE)

time: 95.3 us -> 95.3 us (level)
    unnamed x13 -> x14, local copies, waits for them, and re-layouts: 2.66 us -> 2.67 us
  transfers between devices with their start and end apart: 24 -> 24, of which waited for: 10 -> 10; matrix products, arithmetic and copies ran while one was open for 1% -> 0% of each run, Pallas kernels for 19% -> 19%
where the time goes in v4:
time: 95.3 us; the launch traced here: 94.6 us
  starting transfers between devices  39 us (41%)
  Pallas kernels  31.7 us (33%)
  waiting for transfers between devices  19.4 us (20%)
  local copies, waits for them, and re-layouts  3.72 us (4%)
    pallas_call x17, Pallas kernels, call(): pl.pallas_call(kernel, out_shape=out_shape, cost_estimate=estimate or TIN...  31.7 us
    ppermute x14, starting transfers between devices, swap(): lax.ppermute(part, AXES, (ACROSS_Y if way == 'y' else ACROSS_X)[n - 1])  22.8 us
    ppermute x14, waiting for transfers between devices, swap(): lax.ppermute(part, AXES, (ACROSS_Y if way == 'y' else ACROSS_X)[n - 1])  9.99 us
    ppermute x1, starting transfers between devices, body(): lax.ppermute(rim, 'loop', [(i, (i - 1 + i % 2 * 2) % 32) for i in range(3...  6.29 us
    ppermute x3, starting transfers between devices, body(): lax.ppermute(part, AXES, ACROSS_Z[m])  4.47 us
    ppermute x1, starting transfers between devices, body(): lax.ppermute(send, AXES, ACROSS_Z[4])  4.28 us
    ppermute x1, waiting for transfers between devices, body(): lax.ppermute(send, AXES, ACROSS_Z[4])  3.67 us
    ppermute x3, waiting for transfers between devices, body(): lax.ppermute(part, AXES, ACROSS_Z[m])  3.12 us
  transfers between devices with their start and end apart: 24, of which 10 were waited for; matrix products, arithmetic and copies ran while one was open for 0% of the time, Pallas kernels for 19%

profile of v4, /device:TPU:8, one launch (start us, length us, event | category | flops | bytes accessed | tf_op | source)
XLA Modules:
  0.0 94.6 jit_solution(7586526285897327561)
XLA Ops:
  6.9 2.6 %collective-permute-done.left_ref = bf16[64,1536]{1,0:T(8,128)(2,1)S(1)} collective-permute-done((bf16[64,1536]{1,0:T(8,128)(2,1)S(1)}, bf16[64,1536]{1,0:T(8,128)(2,1)S(1)}, u32[]{:S(2)}, u32[]{:S(2)}) %collective-permute-start) | collective-permute-done | bytes 196640 | tf_op jit(solution)/shard_map/ppermute | solution.py:487
  10.2 4.7 %shard_map.88.q_ref.k_ref.v_ref = bf16[640,2304]{1,0:T(8,128)(2,1)S(1)} custom-call(bf16[512,1536]{1,0:T(8,128)(2,1)S(1)} %bitcast.16, bf16[64,1536]{1,0:T(8,128)(2,1)S(1)} %collective-permute-done.left_ref, bf16[64,1536]{1,0:T(8,128)(2,1)S(1)} %collective-permute-done.1.right_ref, bf16[1536,2304]{1,0:T(8,128)(2,1)S(1)} %bitcast.11, ...), custom_call_target="tpu_custom_call" | custom-call | flops 1000 | bytes 1000 | tf_op jit(solution)/shard_map/pallas_call | solution.py:71
  14.9 4.0 %shard_map.89 = (bf16[512,768]{1,0:T(8,128)(2,1)}, bf16[64,1536]{1,0:T(8,128)(2,1)S(1)}, bf16[640,1536]{1,0:T(8,128)(2,1)S(1)}) custom-call(bf16[640,2304]{1,0:T(8,128)(2,1)S(1)} %shard_map.88.q_ref.k_ref.v_ref, bf16[640,2304]{1,0:T(8,128)(2,1)S(1)} %shard_map.88.q_ref.k_ref.v_ref, bf16[640,2304]{1,0:T(8,128)(2,1)S(1)} %shard_map.88.q_ref.k_ref.v_ref, ...), custom_call_target="tpu_custom_call" | custom-call | flops 1000 | bytes 1000 | tf_op jit(solution)/shard_map/pallas_call | solution.py:71
  18.9 4.0 %shard_map.90 = (bf16[512,768]{1,0:T(8,128)(2,1)}, bf16[64,1536]{1,0:T(8,128)(2,1)S(1)}, bf16[640,1536]{1,0:T(8,128)(2,1)S(1)}) custom-call(bf16[640,2304]{1,0:T(8,128)(2,1)S(1)} %shard_map.88.q_ref.k_ref.v_ref, bf16[640,2304]{1,0:T(8,128)(2,1)S(1)} %shard_map.88.q_ref.k_ref.v_ref, ...), custom_call_target="tpu_custom_call", output_to_operand_aliasing={{0}: (5, {}), {1}: (6, {}), {2}: (7, {})} | custom-call | flops 1000 | bytes 1000 | tf_op jit(solution)/shard_map/pallas_call | solution.py:71
  23.3 4.0 %shard_map.91 = (bf16[512,768]{1,0:T(8,128)(2,1)}, bf16[64,1536]{1,0:T(8,128)(2,1)S(1)}, bf16[640,768]{1,0:T(8,128)(2,1)S(1)}) custom-call(bf16[640,2304]{1,0:T(8,128)(2,1)S(1)} %shard_map.88.q_ref.k_ref.v_ref, bf16[640,2304]{1,0:T(8,128)(2,1)S(1)} %shard_map.88.q_ref.k_ref.v_ref, ...), custom_call_target="tpu_custom_call", output_to_operand_aliasing={{0}: (5, {}), {1}: (6, {})} | custom-call | flops 1000 | bytes 1000 | tf_op jit(solution)/shard_map/pallas_call | solution.py:71
  27.3 6.3 %collective-permute-start.4 = (bf16[64,1536]{1,0:T(8,128)(2,1)S(1)}, bf16[64,1536]{1,0:T(8,128)(2,1)S(1)}, u32[]{:S(2)}, u32[]{:S(2)}) collective-permute-start(bf16[64,1536]{1,0:T(8,128)(2,1)S(1)} %get-tuple-element.62.refs_2_), channel_id=1, source_target_pairs={{0,31},{1,2},{2,1},{3,4},{4,3},{5,6},{6,5},{7,8},{8,7},{9,10},{10,... | collective-permute-start | bytes 589832 | tf_op jit(solution)/shard_map/ppermute | solution.py:502
  33.6 3.2 %shard_map.92 = (f32[192,1280]{1,0:T(8,128)S(1)}, bf16[192,1280]{1,0:T(8,128)(2,1)S(1)}, f32[192,1280]{1,0:T(8,128)S(1)}, bf16[192,1280]{1,0:T(8,128)(2,1)S(1)}) custom-call(bf16[768,640]{1,0:T(8,128)(2,1)S(1)} %get-tuple-element.63.x_ref, bf16[768,640]{1,0:T(8,128)(2,1)S(1)} %collective-permute-done.5.xp_ref, ...), custom_call_target="tpu_custom_call" | custom-call | flops 1000 | bytes 1000 | tf_op jit(solution)/shard_map/pallas_call | solution.py:71
  36.8 1.9 %collective-permute-start.6 = (bf16[192,1280]{1,0:T(8,128)(2,1)S(1)}, bf16[192,1280]{1,0:T(8,128)(2,1)S(1)}, u32[]{:S(2)}, u32[]{:S(2)}) collective-permute-start(bf16[192,1280]{1,0:T(8,128)(2,1)S(1)} %get-tuple-element.68), channel_id=1, source_target_pairs={{0,2},{1,3},{4,6},{5,7},{8,10},{9,11},{12,14},{13,15},{16,18},{17,... | collective-permute-start | bytes 1474568 | tf_op jit(solution)/shard_map/ppermute | solution.py:506
  39.8 2.6 %shard_map.93 = (f32[192,1024]{1,0:T(8,128)S(1)}, bf16[192,1024]{1,0:T(8,128)(2,1)S(1)}, f32[192,1024]{1,0:T(8,128)S(1)}, bf16[192,1024]{1,0:T(8,128)(2,1)S(1)}) custom-call(bf16[768,640]{1,0:T(8,128)(2,1)S(1)} %get-tuple-element.63.x_ref, bf16[768,640]{1,0:T(8,128)(2,1)S(1)} %collective-permute-done.5.xp_ref, ...), custom_call_target="tpu_custom_call" | custom-call | flops 1000 | bytes 1000 | tf_op jit(solution)/shard_map/pallas_call | solution.py:71
  42.4 1.6 %collective-permute-start.10 = (bf16[192,1024]{1,0:T(8,128)(2,1)S(1)}, bf16[192,1024]{1,0:T(8,128)(2,1)S(1)}, u32[]{:S(2)}, u32[]{:S(2)}) collective-permute-start(bf16[192,1024]{1,0:T(8,128)(2,1)S(1)} %get-tuple-element.76), channel_id=1, source_target_pairs={{0,32},{1,33},{4,36},{5,37},{8,40},{9,41},{12,44},{13,45},{16,48},... | collective-permute-start | bytes 1179656 | tf_op jit(solution)/shard_map/ppermute | solution.py:506
  44.0 2.1 %collective-permute-start.11 = (bf16[192,1024]{1,0:T(8,128)(2,1)S(1)}, bf16[192,1024]{1,0:T(8,128)(2,1)S(1)}, u32[]{:S(2)}, u32[]{:S(2)}) collective-permute-start(bf16[192,1024]{1,0:T(8,128)(2,1)S(1)} %get-tuple-element.78), channel_id=1, source_target_pairs={{0,96},{1,97},{4,100},{5,101},{8,104},{9,105},{12,108},{13,109},{1... | collective-permute-start | bytes 1179656 | tf_op jit(solution)/shard_map/ppermute | solution.py:506
  46.1 5.5 %shard_map.94 = (bf16[512,1536]{1,0:T(8,128)(2,1)}, f32[8,128]{1,0:T(8,128)S(1)}) custom-call(bf16[640,1536]{1,0:T(8,128)(2,1)S(1)} %get-tuple-element.60.refs_0_.a_ref.b_ref, bf16[640,1536]{1,0:T(8,128)(2,1)S(1)} %get-tuple-element.60.refs_0_.a_ref.b_ref, bf16[640,768]{1,0:T(8,128)(2,1)S(1)} %get-tuple-element.61.refs_1_.c_ref, ...), custom_call_target="tpu_custom_call" | custom-call | flops 1000 | bytes 1000 | tf_op jit(solution)/shard_map/pallas_call | solution.py:71
  51.8 2.2 %collective-permute-start.8 = (bf16[96,1280]{1,0:T(8,128)(2,1)S(1)}, bf16[96,1280]{1,0:T(8,128)(2,1)S(1)}, u32[]{:S(2)}, u32[]{:S(2)}) collective-permute-start(bf16[96,1280]{1,0:T(8,128)(2,1)S(1)} %get-tuple-element.73), channel_id=1, source_target_pairs={{0,130},{1,131},{4,134},{5,135},{8,138},{9,139},{12,142},{13,143},... | collective-permute-start | bytes 737288 | tf_op jit(solution)/shard_map/ppermute | solution.py:506
  53.9 1.9 %collective-permute-start.9 = (bf16[96,1280]{1,0:T(8,128)(2,1)S(1)}, bf16[96,1280]{1,0:T(8,128)(2,1)S(1)}, u32[]{:S(2)}, u32[]{:S(2)}) collective-permute-start(bf16[96,1280]{1,0:T(8,128)(2,1)S(1)} %get-tuple-element.75), channel_id=1, source_target_pairs={{0,2},{1,3},{4,6},{5,7},{8,10},{9,11},{12,14},{13,15},{16,18},{17,... | collective-permute-start | bytes 737288 | tf_op jit(solution)/shard_map/ppermute | solution.py:506
  56.0 2.8 %collective-permute-start.15 = (bf16[96,1024]{1,0:T(8,128)(2,1)S(1)}, bf16[96,1024]{1,0:T(8,128)(2,1)S(1)}, u32[]{:S(2)}, u32[]{:S(2)}) collective-permute-start(bf16[96,1024]{1,0:T(8,128)(2,1)S(1)} %get-tuple-element.84), channel_id=1, source_target_pairs={{0,96},{1,97},{4,100},{5,101},{8,104},{9,105},{12,108},{13,109},{1... | collective-permute-start | bytes 589832 | tf_op jit(solution)/shard_map/ppermute | solution.py:506
  63.0 1.5 %collective-permute-done.16.got_b_ref = bf16[96,1024]{1,0:T(8,128)(2,1)S(1)} collective-permute-done((bf16[96,1024]{1,0:T(8,128)(2,1)S(1)}, bf16[96,1024]{1,0:T(8,128)(2,1)S(1)}, u32[]{:S(2)}, u32[]{:S(2)}) %collective-permute-start.16) | collective-permute-done | bytes 196640 | tf_op jit(solution)/shard_map/ppermute | solution.py:506
  66.0 2.7 %collective-permute-start.13 = (bf16[48,1280]{1,0:T(8,128)(2,1)S(1)}, bf16[48,1280]{1,0:T(8,128)(2,1)S(1)}, u32[]{:S(2)}, u32[]{:S(2)}) collective-permute-start(bf16[48,1280]{1,0:T(8,128)(2,1)S(1)} %get-tuple-element.82), channel_id=1, source_target_pairs={{0,64},{1,65},{4,68},{5,69},{8,72},{9,73},{12,76},{13,77},{16,80},... | collective-permute-start | bytes 368648 | tf_op jit(solution)/shard_map/ppermute | solution.py:506
  68.7 2.0 %collective-permute-start.14 = (bf16[48,1280]{1,0:T(8,128)(2,1)S(1)}, bf16[48,1280]{1,0:T(8,128)(2,1)S(1)}, u32[]{:S(2)}, u32[]{:S(2)}) collective-permute-start(bf16[48,1280]{1,0:T(8,128)(2,1)S(1)} %get-tuple-element.83), channel_id=1, source_target_pairs={{0,96},{1,97},{4,100},{5,101},{8,104},{9,105},{12,108},{13,109},{1... | collective-permute-start | bytes 368648 | tf_op jit(solution)/shard_map/ppermute | solution.py:506
  70.7 2.9 %collective-permute-start.18 = (bf16[48,1024]{1,0:T(8,128)(2,1)S(1)}, bf16[48,1024]{1,0:T(8,128)(2,1)S(1)}, u32[]{:S(2)}, u32[]{:S(2)}) collective-permute-start(bf16[48,1024]{1,0:T(8,128)(2,1)S(1)} %get-tuple-element.89), channel_id=1, source_target_pairs={{0,128},{1,129},{4,132},{5,133},{8,136},{9,137},{12,140},{13,141},... | collective-permute-start | bytes 294920 | tf_op jit(solution)/shard_map/ppermute | solution.py:506
  73.6 3.2 %collective-permute-done.18.refs_6_ = bf16[48,1024]{1,0:T(8,128)(2,1)S(1)} collective-permute-done((bf16[48,1024]{1,0:T(8,128)(2,1)S(1)}, bf16[48,1024]{1,0:T(8,128)(2,1)S(1)}, u32[]{:S(2)}, u32[]{:S(2)}) %collective-permute-start.18) | collective-permute-done | bytes 98336 | tf_op jit(solution)/shard_map/ppermute | solution.py:506
  79.3 3.6 %collective-permute-start.22 = (bf16[12,2304]{1,0:T(8,128)(2,1)S(1)}, bf16[12,2304]{1,0:T(8,128)(2,1)S(1)}, u32[]{:S(2)}, u32[]{:S(2)}) collective-permute-start(bf16[12,2304]{1,0:T(8,128)(2,1)S(1)} %get-tuple-element.94), channel_id=1, source_target_pairs={{0,12},{1,13},{4,8},{5,9},{8,4},{9,5},{12,0},{13,1},{16,28},{17,29... | collective-permute-start | bytes 165896 | tf_op jit(solution)/shard_map/ppermute | solution.py:531
  83.7 2.2 %collective-permute-done.22.c_ref = bf16[12,2304]{1,0:T(8,128)(2,1)S(1)} collective-permute-done((bf16[12,2304]{1,0:T(8,128)(2,1)S(1)}, bf16[12,2304]{1,0:T(8,128)(2,1)S(1)}, u32[]{:S(2)}, u32[]{:S(2)}) %collective-permute-start.22) | collective-permute-done | bytes 55328 | tf_op jit(solution)/shard_map/ppermute | solution.py:531
  86.0 4.3 %collective-permute-start.23 = (bf16[6,2304]{1,0:T(8,128)(2,1)S(1)}, bf16[6,2304]{1,0:T(8,128)(2,1)S(1)}, u32[]{:S(2)}, u32[]{:S(2)}) collective-permute-start(bf16[6,2304]{1,0:T(8,128)(2,1)S(1)} %get-tuple-element.96), channel_id=1, source_target_pairs={{0,16},{1,17},{4,20},{5,21},{8,24},{9,25},{12,28},{13,29},{16,0},{... | collective-permute-start | bytes 82952 | tf_op jit(solution)/shard_map/ppermute | solution.py:537
  90.3 3.7 %collective-permute-done.23.got_ref = bf16[6,2304]{1,0:T(8,128)(2,1)S(1)} collective-permute-done((bf16[6,2304]{1,0:T(8,128)(2,1)S(1)}, bf16[6,2304]{1,0:T(8,128)(2,1)S(1)}, u32[]{:S(2)}, u32[]{:S(2)}) %collective-permute-start.23) | collective-permute-done | bytes 27680 | tf_op jit(solution)/shard_map/ppermute | solution.py:537
  (58 shorter events, 18.4 us)
Async XLA Ops:
  1.7 5.3 %collective-permute-start.1 = (bf16[64,1536]{1,0:T(8,128)(2,1)S(1)}, bf16[64,1536]{1,0:T(8,128)(2,1)S(1)}, u32[]{:S(2)}, u32[]{:S(2)}) collective-permute-start(bf16[64,1536]{1,0:T(8,128)(2,1)S(1)} %get-tuple-element.97), channel_id=1, source_target_pairs={{1,0},{2,1},{3,2},{4,3},{5,4},{6,5},{7,6},{8,7},{9,8},{10,9},{11,1... | collective-permute-start | bytes 589832 | tf_op jit(solution)/shard_map/ppermute | solution.py:488
  1.8 7.7 %collective-permute-start = (bf16[64,1536]{1,0:T(8,128)(2,1)S(1)}, bf16[64,1536]{1,0:T(8,128)(2,1)S(1)}, u32[]{:S(2)}, u32[]{:S(2)}) collective-permute-start(bf16[64,1536]{1,0:T(8,128)(2,1)S(1)} %get-tuple-element.98), channel_id=1, source_target_pairs={{31,0},{0,1},{1,2},{2,3},{3,4},{4,5},{5,6},{6,7},{7,8},{8,9},{9,10... | collective-permute-start | bytes 589832 | tf_op jit(solution)/shard_map/ppermute | solution.py:487
  22.8 10.8 %collective-permute-start.2 = (bf16[640,1536]{1,0:T(8,128)(2,1)S(1)}, bf16[640,1536]{1,0:T(8,128)(2,1)S(1)}, u32[]{:S(2)}, u32[]{:S(2)}) collective-permute-start(bf16[640,1536]{1,0:T(8,128)(2,1)S(1)} %get-tuple-element.60.refs_0_.a_ref.b_ref), channel_id=1, source_target_pairs={{0,1},{1,0},{4,5},{5,4},{8,9},{9,8},{12,13},{13,12},{16,17},{17,16... | collective-permute-start | bytes 5898248 | tf_op jit(solution)/shard_map/ppermute | solution.py:498
  22.8 10.8 %collective-permute-start.5 = (bf16[768,640]{1,0:T(8,128)(2,1)S(1)}, bf16[768,640]{1,0:T(8,128)(2,1)S(1)}, u32[]{:S(2)}, u32[]{:S(2)}) collective-permute-start(bf16[768,640]{1,0:T(8,128)(2,1)S(1)} %get-tuple-element.64), channel_id=1, source_target_pairs={{0,1},{1,0},{4,5},{5,4},{8,9},{9,8},{12,13},{13,12},{16,17},{17,16... | collective-permute-start | bytes 2949128 | tf_op jit(solution)/shard_map/ppermute | solution.py:492
  27.3 12.5 %collective-permute-start.3 = (bf16[640,768]{1,0:T(8,128)(2,1)S(1)}, bf16[640,768]{1,0:T(8,128)(2,1)S(1)}, u32[]{:S(2)}, u32[]{:S(2)}) collective-permute-start(bf16[640,768]{1,0:T(8,128)(2,1)S(1)} %get-tuple-element.61.refs_1_.c_ref), channel_id=1, source_target_pairs={{0,1},{1,0},{4,5},{5,4},{8,9},{9,8},{12,13},{13,12},{16,17},{17,16... | collective-permute-start | bytes 2949128 | tf_op jit(solution)/shard_map/ppermute | solution.py:501
  27.3 12.5 %collective-permute-start.4 = (bf16[64,1536]{1,0:T(8,128)(2,1)S(1)}, bf16[64,1536]{1,0:T(8,128)(2,1)S(1)}, u32[]{:S(2)}, u32[]{:S(2)}) collective-permute-start(bf16[64,1536]{1,0:T(8,128)(2,1)S(1)} %get-tuple-element.62.refs_2_), channel_id=1, source_target_pairs={{0,31},{1,2},{2,1},{3,4},{4,3},{5,6},{6,5},{7,8},{8,7},{9,10},{10,... | collective-permute-start | bytes 589832 | tf_op jit(solution)/shard_map/ppermute | solution.py:502
  36.8 14.8 %collective-permute-start.6 = (bf16[192,1280]{1,0:T(8,128)(2,1)S(1)}, bf16[192,1280]{1,0:T(8,128)(2,1)S(1)}, u32[]{:S(2)}, u32[]{:S(2)}) collective-permute-start(bf16[192,1280]{1,0:T(8,128)(2,1)S(1)} %get-tuple-element.68), channel_id=1, source_target_pairs={{0,2},{1,3},{4,6},{5,7},{8,10},{9,11},{12,14},{13,15},{16,18},{17,... | collective-permute-start | bytes 1474568 | tf_op jit(solution)/shard_map/ppermute | solution.py:506
  38.8 12.8 %collective-permute-start.7 = (bf16[192,1280]{1,0:T(8,128)(2,1)S(1)}, bf16[192,1280]{1,0:T(8,128)(2,1)S(1)}, u32[]{:S(2)}, u32[]{:S(2)}) collective-permute-start(bf16[192,1280]{1,0:T(8,128)(2,1)S(1)} %get-tuple-element.70), channel_id=1, source_target_pairs={{0,130},{1,131},{4,134},{5,135},{8,138},{9,139},{12,142},{13,143},... | collective-permute-start | bytes 1474568 | tf_op jit(solution)/shard_map/ppermute | solution.py:506
  42.4 13.5 %collective-permute-start.10 = (bf16[192,1024]{1,0:T(8,128)(2,1)S(1)}, bf16[192,1024]{1,0:T(8,128)(2,1)S(1)}, u32[]{:S(2)}, u32[]{:S(2)}) collective-permute-start(bf16[192,1024]{1,0:T(8,128)(2,1)S(1)} %get-tuple-element.76), channel_id=1, source_target_pairs={{0,32},{1,33},{4,36},{5,37},{8,40},{9,41},{12,44},{13,45},{16,48},... | collective-permute-start | bytes 1179656 | tf_op jit(solution)/shard_map/ppermute | solution.py:506
  44.0 11.9 %collective-permute-start.11 = (bf16[192,1024]{1,0:T(8,128)(2,1)S(1)}, bf16[192,1024]{1,0:T(8,128)(2,1)S(1)}, u32[]{:S(2)}, u32[]{:S(2)}) collective-permute-start(bf16[192,1024]{1,0:T(8,128)(2,1)S(1)} %get-tuple-element.78), channel_id=1, source_target_pairs={{0,96},{1,97},{4,100},{5,101},{8,104},{9,105},{12,108},{13,109},{1... | collective-permute-start | bytes 1179656 | tf_op jit(solution)/shard_map/ppermute | solution.py:506
  51.8 8.6 %collective-permute-start.8 = (bf16[96,1280]{1,0:T(8,128)(2,1)S(1)}, bf16[96,1280]{1,0:T(8,128)(2,1)S(1)}, u32[]{:S(2)}, u32[]{:S(2)}) collective-permute-start(bf16[96,1280]{1,0:T(8,128)(2,1)S(1)} %get-tuple-element.73), channel_id=1, source_target_pairs={{0,130},{1,131},{4,134},{5,135},{8,138},{9,139},{12,142},{13,143},... | collective-permute-start | bytes 737288 | tf_op jit(solution)/shard_map/ppermute | solution.py:506
  53.9 7.9 %collective-permute-start.9 = (bf16[96,1280]{1,0:T(8,128)(2,1)S(1)}, bf16[96,1280]{1,0:T(8,128)(2,1)S(1)}, u32[]{:S(2)}, u32[]{:S(2)}) collective-permute-start(bf16[96,1280]{1,0:T(8,128)(2,1)S(1)} %get-tuple-element.75), channel_id=1, source_target_pairs={{0,2},{1,3},{4,6},{5,7},{8,10},{9,11},{12,14},{13,15},{16,18},{17,... | collective-permute-start | bytes 737288 | tf_op jit(solution)/shard_map/ppermute | solution.py:506
  56.0 7.0 %collective-permute-start.15 = (bf16[96,1024]{1,0:T(8,128)(2,1)S(1)}, bf16[96,1024]{1,0:T(8,128)(2,1)S(1)}, u32[]{:S(2)}, u32[]{:S(2)}) collective-permute-start(bf16[96,1024]{1,0:T(8,128)(2,1)S(1)} %get-tuple-element.84), channel_id=1, source_target_pairs={{0,96},{1,97},{4,100},{5,101},{8,104},{9,105},{12,108},{13,109},{1... | collective-permute-start | bytes 589832 | tf_op jit(solution)/shard_map/ppermute | solution.py:506
  58.8 5.7 %collective-permute-start.16 = (bf16[96,1024]{1,0:T(8,128)(2,1)S(1)}, bf16[96,1024]{1,0:T(8,128)(2,1)S(1)}, u32[]{:S(2)}, u32[]{:S(2)}) collective-permute-start(bf16[96,1024]{1,0:T(8,128)(2,1)S(1)} %get-tuple-element.86), channel_id=1, source_target_pairs={{0,32},{1,33},{4,36},{5,37},{8,40},{9,41},{12,44},{13,45},{16,48},... | collective-permute-start | bytes 589832 | tf_op jit(solution)/shard_map/ppermute | solution.py:506
  64.6 9.1 %collective-permute-start.17 = (bf16[48,1024]{1,0:T(8,128)(2,1)S(1)}, bf16[48,1024]{1,0:T(8,128)(2,1)S(1)}, u32[]{:S(2)}, u32[]{:S(2)}) collective-permute-start(bf16[48,1024]{1,0:T(8,128)(2,1)S(1)} %get-tuple-element.88), channel_id=1, source_target_pairs={{0,2},{1,3},{4,6},{5,7},{8,10},{9,11},{12,14},{13,15},{16,18},{17,... | collective-permute-start | bytes 294920 | tf_op jit(solution)/shard_map/ppermute | solution.py:506
  66.0 12.3 %collective-permute-start.12 = (bf16[48,1280]{1,0:T(8,128)(2,1)S(1)}, bf16[48,1280]{1,0:T(8,128)(2,1)S(1)}, u32[]{:S(2)}, u32[]{:S(2)}) collective-permute-start(bf16[48,1280]{1,0:T(8,128)(2,1)S(1)} %get-tuple-element.81), channel_id=1, source_target_pairs={{0,32},{1,33},{4,36},{5,37},{8,40},{9,41},{12,44},{13,45},{16,48},... | collective-permute-start | bytes 368648 | tf_op jit(solution)/shard_map/ppermute | solution.py:506
  66.0 12.3 %collective-permute-start.13 = (bf16[48,1280]{1,0:T(8,128)(2,1)S(1)}, bf16[48,1280]{1,0:T(8,128)(2,1)S(1)}, u32[]{:S(2)}, u32[]{:S(2)}) collective-permute-start(bf16[48,1280]{1,0:T(8,128)(2,1)S(1)} %get-tuple-element.82), channel_id=1, source_target_pairs={{0,64},{1,65},{4,68},{5,69},{8,72},{9,73},{12,76},{13,77},{16,80},... | collective-permute-start | bytes 368648 | tf_op jit(solution)/shard_map/ppermute | solution.py:506
  68.7 9.6 %collective-permute-start.14 = (bf16[48,1280]{1,0:T(8,128)(2,1)S(1)}, bf16[48,1280]{1,0:T(8,128)(2,1)S(1)}, u32[]{:S(2)}, u32[]{:S(2)}) collective-permute-start(bf16[48,1280]{1,0:T(8,128)(2,1)S(1)} %get-tuple-element.83), channel_id=1, source_target_pairs={{0,96},{1,97},{4,100},{5,101},{8,104},{9,105},{12,108},{13,109},{1... | collective-permute-start | bytes 368648 | tf_op jit(solution)/shard_map/ppermute | solution.py:506
  70.7 6.1 %collective-permute-start.18 = (bf16[48,1024]{1,0:T(8,128)(2,1)S(1)}, bf16[48,1024]{1,0:T(8,128)(2,1)S(1)}, u32[]{:S(2)}, u32[]{:S(2)}) collective-permute-start(bf16[48,1024]{1,0:T(8,128)(2,1)S(1)} %get-tuple-element.89), channel_id=1, source_target_pairs={{0,128},{1,129},{4,132},{5,133},{8,136},{9,137},{12,140},{13,141},... | collective-permute-start | bytes 294920 | tf_op jit(solution)/shard_map/ppermute | solution.py:506
  73.6 4.6 %collective-permute-start.19 = (bf16[48,1024]{1,0:T(8,128)(2,1)S(1)}, bf16[48,1024]{1,0:T(8,128)(2,1)S(1)}, u32[]{:S(2)}, u32[]{:S(2)}) collective-permute-start(bf16[48,1024]{1,0:T(8,128)(2,1)S(1)} %get-tuple-element.90), channel_id=1, source_target_pairs={{0,130},{1,131},{4,134},{5,135},{8,138},{9,139},{12,142},{13,143},... | collective-permute-start | bytes 294920 | tf_op jit(solution)/shard_map/ppermute | solution.py:506
  78.4 5.3 %collective-permute-start.20 = (bf16[12,2304]{1,0:T(8,128)(2,1)S(1)}, bf16[12,2304]{1,0:T(8,128)(2,1)S(1)}, u32[]{:S(2)}, u32[]{:S(2)}) collective-permute-start(bf16[12,2304]{1,0:T(8,128)(2,1)S(1)} %get-tuple-element.92), channel_id=1, source_target_pairs={{0,8},{1,9},{4,12},{5,13},{8,0},{9,1},{12,4},{13,5},{16,24},{17,25... | collective-permute-start | bytes 165896 | tf_op jit(solution)/shard_map/ppermute | solution.py:531
  78.5 5.2 %collective-permute-start.21 = (bf16[12,2304]{1,0:T(8,128)(2,1)S(1)}, bf16[12,2304]{1,0:T(8,128)(2,1)S(1)}, u32[]{:S(2)}, u32[]{:S(2)}) collective-permute-start(bf16[12,2304]{1,0:T(8,128)(2,1)S(1)} %get-tuple-element.93), channel_id=1, source_target_pairs={{0,4},{1,5},{4,0},{5,1},{8,12},{9,13},{12,8},{13,9},{16,20},{17,21... | collective-permute-start | bytes 165896 | tf_op jit(solution)/shard_map/ppermute | solution.py:531
  79.3 6.7 %collective-permute-start.22 = (bf16[12,2304]{1,0:T(8,128)(2,1)S(1)}, bf16[12,2304]{1,0:T(8,128)(2,1)S(1)}, u32[]{:S(2)}, u32[]{:S(2)}) collective-permute-start(bf16[12,2304]{1,0:T(8,128)(2,1)S(1)} %get-tuple-element.94), channel_id=1, source_target_pairs={{0,12},{1,13},{4,8},{5,9},{8,4},{9,5},{12,0},{13,1},{16,28},{17,29... | collective-permute-start | bytes 165896 | tf_op jit(solution)/shard_map/ppermute | solution.py:531
  86.0 8.0 %collective-permute-start.23 = (bf16[6,2304]{1,0:T(8,128)(2,1)S(1)}, bf16[6,2304]{1,0:T(8,128)(2,1)S(1)}, u32[]{:S(2)}, u32[]{:S(2)}) collective-permute-start(bf16[6,2304]{1,0:T(8,128)(2,1)S(1)} %get-tuple-element.96), channel_id=1, source_target_pairs={{0,16},{1,17},{4,20},{5,21},{8,24},{9,25},{12,28},{13,29},{16,0},{... | collective-permute-start | bytes 82952 | tf_op jit(solution)/shard_map/ppermute | solution.py:537
  (7 other events, 18.3 us)
